TPU v7x, 32 devices: a whole 2x2x4 slice. The times are simulated.
32 devices in a mesh: band: 4 (over z), fft: 8 (over y, x, core).
Axes of the slice: x: 2, y: 2, z: 4, core: 2. Of those that a mesh axis runs over, the one named last changes fastest.
Arguments:
- band_coeffs: float32 [8, 512, 192], P('band', 'fft'), may hold values from -6 to 6
- potential: float32 [192, 192, 192], P('fft'), may hold values from -12 to 12
- stick_column: int32 [512], replicated, may hold values from 0 to 9215, as said below
- stick_length: int32 [512], P('fft'), may hold values from 1 to 96
- orbitals: bfloat16 [512, 512, 192], P(None, ('band', 'fft')), may hold values from -0.0546875 to 0.0546875
Outputs:
- applied: bfloat16 [8, 512, 192], P('band', 'fft')
- margin: float32 [512, 16], P(('band', 'fft'))
Inputs may be any that keep to these rules, and one draw needn't show every extreme that they name: `stick_column`: distinct columns of a 96 x 96 frequency box; column q stands for gx = q // 96 - 96/2 and gy = q % 96 - 96/2.
All inputs are finite; a program needn't handle non-finite values.
Results may differ from a plain program's by a relative error of at most 0.0055.
Values may be sent and summed in bfloat16 or wider, within the bound.
No kernel may reach another device: no remote copies, remote signals or barrier semaphores. Data moves between devices by JAX's collectives and lax.ppermute only.
A program may use at most 64 MiB of HBM per device.

v0:
```python
import math

import jax
import jax.numpy as jnp
from jax import lax
from jax.sharding import PartitionSpec as P

HIGHEST_MODE = lax.Precision.HIGHEST


def phase_tables(half_box, grid_cells):
    frequency = jnp.arange(half_box, dtype=jnp.int32) - half_box // 2
    positions = jnp.arange(grid_cells, dtype=jnp.int32)
    turn_count = frequency[:, None] * positions[None, :] % grid_cells
    angles = turn_count.astype(jnp.float32) * (2.0 * math.pi / grid_cells)
    cosine = jnp.cos(angles)
    sine_part = jnp.sin(angles)
    forward = jnp.stack([jnp.stack([cosine, sine_part], 1), jnp.stack([-sine_part, cosine], 1)], 0)
    cos_back = cosine.T
    sin_back = sine_part.T
    backward = jnp.stack(
        [jnp.stack([cos_back, -sin_back], 1), jnp.stack([sin_back, cos_back], 1)], 0
    )
    return (forward, backward)


def per_device(band_coeffs, potential, stick_column, stick_length, orbitals):
    band_dev, sticks_dev, coef_width = band_coeffs.shape
    half_box = coef_width // 2
    grid_cells = potential.shape[1]
    forward, backward = phase_tables(half_box, grid_cells)
    first_stick = lax.axis_index("fft") * sticks_dev
    own_columns = lax.dynamic_slice_in_dim(stick_column, first_stick, sticks_dev)
    z_freq = jnp.arange(half_box, dtype=jnp.int32) - half_box // 2
    stick_len = stick_length[:, None]
    live_slots = (z_freq[None, :] >= -(stick_len // 2)) & (
        z_freq[None, :] < stick_len - stick_len // 2
    )
    x_freq = own_columns // half_box - half_box // 2
    y_freq = own_columns % half_box - half_box // 2
    kinetic = (x_freq[:, None] ** 2 + y_freq[:, None] ** 2 + z_freq[None, :] ** 2).astype(
        jnp.float32
    ) * (2.0 / (half_box * half_box))
    norm_factor = 1.0 / float(grid_cells) ** 3
    live_mask = live_slots[:, None, :]
    kinetic_mask = kinetic[:, None, :]
    box_index = jnp.arange(half_box, dtype=jnp.int32)
    onehot_x = (box_index[:, None] == (stick_column // half_box)[None, :]).astype(jnp.float32)
    onehot_y = ((stick_column % half_box)[:, None] == box_index[None, :]).astype(jnp.float32)

    def place_plane(plane_vals):
        spread = plane_vals[..., None] * onehot_y
        return jnp.einsum("xs,bcsy->bcxy", onehot_x, spread, precision=HIGHEST_MODE)

    def pick_plane(plane_box):
        rows_x = jnp.einsum("xs,bcxy->bcsy", onehot_x, plane_box, precision=HIGHEST_MODE)
        return jnp.sum(rows_x * onehot_y, axis=-1)

    band_count = band_coeffs.shape[0]
    masked = jnp.where(live_mask, band_coeffs.reshape(band_count, sticks_dev, 2, half_box), 0.0)
    columns = jnp.einsum("bsck,ckdz->bdzs", masked, forward, precision=HIGHEST_MODE)
    planes = lax.all_to_all(
        columns.astype(jnp.bfloat16), "fft", split_axis=2, concat_axis=3, tiled=True
    ).astype(columns.dtype)
    freq_box = lax.map(place_plane, jnp.moveaxis(planes, 2, 0))
    freq_box = jnp.moveaxis(freq_box, 0, 2)
    half_done = jnp.einsum("bcpxk,ckdy->bdpxy", freq_box, forward, precision=HIGHEST_MODE)
    real_field = jnp.einsum("bcpky,ckdx->bdpxy", half_done, forward, precision=HIGHEST_MODE)
    real_field = real_field * potential[None, None]
    half_done = jnp.einsum("bcpxy,cxdk->bdpky", real_field, backward, precision=HIGHEST_MODE)
    freq_box = jnp.einsum("bcpky,cydq->bdpkq", half_done, backward, precision=HIGHEST_MODE)
    picked = lax.map(pick_plane, jnp.moveaxis(freq_box, 2, 0))
    picked = jnp.moveaxis(picked, 0, 2)
    stick_data = lax.all_to_all(
        picked.astype(jnp.bfloat16), "fft", split_axis=3, concat_axis=2, tiled=True
    ).astype(picked.dtype)
    local_term = (
        jnp.einsum("bczs,czdk->bsdk", stick_data, backward, precision=HIGHEST_MODE) * norm_factor
    )
    h_coeffs = jnp.where(live_mask, kinetic_mask * masked + local_term, 0.0)
    applied = h_coeffs.astype(jnp.bfloat16).reshape(band_count, sticks_dev, coef_width)
    gathered = lax.all_to_all(applied, "band", split_axis=1, concat_axis=0, tiled=True)
    real_part = gathered[:, :, :half_box]
    imag_part = gathered[:, :, half_box:]
    stacked = jnp.concatenate([gathered, jnp.concatenate([imag_part, -real_part], 2)], 0)
    stacked = stacked.reshape(stacked.shape[0], -1)
    orbital_rows = orbitals.reshape(orbitals.shape[0], -1)
    margin = lax.psum_scatter(
        lax.dot_general(
            orbital_rows, stacked, (((1,), (1,)), ((), ())), preferred_element_type=jnp.float32
        ),
        ("band", "fft"),
        scatter_dimension=0,
        tiled=True,
    )
    return (applied, margin)


def solution(mesh):
    placed = (
        P("band", "fft", None),
        P("fft", None, None),
        P(),
        P("fft"),
        P(None, ("band", "fft"), None),
    )
    return jax.shard_map(
        per_device,
        mesh=mesh,
        in_specs=placed,
        out_specs=(P("band", "fft", None), P(("band", "fft"), None)),
        check_vma=False,
    )
```

profile of v0, /device:TPU:0, one launch (start us, length us, event | category | flops | bytes accessed | tf_op | source)
XLA Modules:
  0.0 415.3 jit_solution(1476835426234655566)
XLA Ops:
  15.5 5.2 %all-to-all-start = ((bf16[8,2,3072]{2,1,0:T(2,128)(2,1)}), bf16[8,2,3072]{2,1,0:T(2,128)(2,1)}, u32[]{:S(2)}, u32[]{:S(2)}) async-start(bf16[8,2,3072]{2,1,0:T(2,128)(2,1)} %reshape.321), calls=%async_computation | async-start | bytes 196608 | tf_op jit(solution)/shard_map/all_to_all | solution.py:62
  25.9 1.8 reshape.322
  29.5 1.8 reshape.297
  31.3 56.4 %while.22 = (s32[]{:T(128)}, f32[24,2,2,96,96]{3,4,2,1,0:T(8,128)}, f32[24,2,2,512]{3,0,2,1:T(8,128)}, s32[512]{0:T(512)S(1)}, s32[512]{0:T(512)S(1)}, /*index=5*/s32[]{:T(128)}) while((s32[]{:T(128)}, f32[24,2,2,96,96]{3,4,2,1,0:T(8,128)}, f32[24,2,2,512]{3,0,2,1:T(8,128)}, s32[512]{0:T(512)S(1)}, s32[512]{0:T(512)S(1)}, ...), condition=%wide.region_1.2_spmd.clone, body=%wide.region_0.1_spmd.clone.sunk | while | flops 226885632 | bytes 635465 | solution.py:65
  32.2 1.5 fusion.100
  34.6 1.5 fusion.100
  36.9 1.5 fusion.100
  39.2 1.5 fusion.100
  41.6 1.5 fusion.100
  43.9 1.5 fusion.100
  46.3 1.5 fusion.100
  51.0 1.5 fusion.100
  53.3 1.5 fusion.100
  55.7 1.5 fusion.100
  58.0 1.5 fusion.100
  60.4 1.5 fusion.100
  62.7 1.5 fusion.100
  65.1 1.5 fusion.100
  67.4 1.5 fusion.100
  69.8 1.5 fusion.100
  72.1 1.5 fusion.100
  74.5 1.5 fusion.100
  76.8 1.5 fusion.100
  79.2 1.5 fusion.100
  81.5 1.5 fusion.100
  83.8 1.5 fusion.100
  86.2 1.5 fusion.100
  87.7 10.8 %fusion.31 = f32[2,192,2,24,96,1]{4,1,5,3,2,0:T(8,128)S(1)} fusion(f32[1,96,2,192]{3,1,0,2:T(8,128)} %copy-done.3, f32[1,96,2,192]{3,1,0,2:T(8,128)} %copy-done.1, f32[24,2,2,96,96]{3,4,2,1,0:T(8,128)} %get-tuple-element.56), kind=kOutput, calls=%fused_computation.36 | convolution fusion | flops 4076937216 | bytes 10911744 | tf_op jit(solution)/shard_map/bcpxk,ckdy->bdpxy/dot_general | solution.py:67
  98.5 39.7 %fusion.22 = f32[2,2,24,192,192,1]{4,3,2,0,1,5:T(8,128)} fusion(f32[24,192,192]{2,1,0:T(8,128)S(1)} %bitcast.183, f32[2,192,2,24,96,1]{4,1,5,3,2,0:T(8,128)S(1)} %fusion.31, f32[1,96,2,192]{3,1,0,2:T(8,128)S(1)} %copy-done.4, f32[1,96,2,192]{3,1,0,2:T(8,128)S(1)} %copy-done.2), kind=kOutput, calls=%fused_computation.29 | convolution fusion | flops 8157339648 | bytes 25067520 | tf_op jit(solution)/shard_map/bcpky,ckdx->bdpxy/dot_general | solution.py:68
  138.3 19.7 %fusion.23 = f32[2,96,2,24,192,1]{4,1,5,0,3,2:T(8,128)S(1)} fusion(f32[2,2,24,192,192,1]{4,3,2,0,1,5:T(8,128)} %fusion.22, f32[1,192,2,96]{1,3,0,2:T(8,128)S(1)} %get-tuple-element.173, f32[1,192,2,96]{1,3,0,2:T(8,128)S(1)} %get-tuple-element.172), kind=kOutput, calls=%fused_computation.30 | convolution fusion | flops 8153800704 | bytes 21528576 | tf_op jit(solution)/shard_map/bcpxy,cxdk->bdpky/dot_general | solution.py:70
  157.9 12.0 %fusion.33 = f32[24,2,2,96,96]{3,4,0,1,2:T(8,128)} fusion(f32[2,96,2,24,192,1]{4,1,5,0,3,2:T(8,128)S(1)} %fusion.23, f32[1,192,2,96]{1,3,0,2:T(8,128)S(1)} %get-tuple-element.173, f32[1,192,2,96]{1,3,0,2:T(8,128)S(1)} %get-tuple-element.172), kind=kOutput, calls=%fused_computation.38 | convolution fusion | flops 4076937216 | bytes 10911744 | tf_op jit(solution)/shard_map/bcpky,cydq->bdpkq/dot_general | solution.py:71
  169.9 76.7 %while.23 = (s32[]{:T(128)}, bf16[24,2,2,512]{3,0,2,1:T(8,128)(2,1)}, f32[24,2,2,96,96]{3,4,0,1,2:T(8,128)}, s32[512]{0:T(512)S(1)}, s32[512]{0:T(512)S(1)}, /*index=5*/s32[]{:T(128)}, s32[]{:T(128)}) while((s32[]{:T(128)}, bf16[24,2,2,512]{3,0,2,1:T(8,128)(2,1)}, f32[24,2,2,96,96]{3,4,0,1,2:T(8,128)}, s32[512]{0:T(512)S(1)}, ...), condition=%wide.region_4.5_spmd.clone, body=%wide.region_2.4_spmd.clone.sunk | while | flops 227080192 | bytes 614993 | solution.py:72
  170.0 1.7 fusion.103
  173.2 1.7 fusion.103
  176.4 1.7 fusion.103
  179.5 1.7 fusion.103
  182.7 1.7 fusion.103
  185.9 1.7 fusion.103
  189.1 1.7 fusion.103
  192.3 1.7 fusion.103
  195.5 1.7 fusion.103
  198.7 1.7 fusion.103
  201.9 1.7 fusion.103
  205.1 1.7 fusion.103
  208.3 1.7 fusion.103
  211.5 1.7 fusion.103
  214.7 1.7 fusion.103
  217.9 1.7 fusion.103
  221.1 1.7 fusion.103
  224.3 1.7 fusion.103
  227.5 1.7 fusion.103
  230.7 1.7 fusion.103
  233.9 1.7 fusion.103
  237.1 1.7 fusion.103
  240.3 1.7 fusion.103
  243.5 1.7 fusion.103
  246.6 1.8 copy.102
  248.5 2.3 reshape.323
  250.8 4.0 all-to-all-start.1
  256.2 3.8 all-to-all-done.1
  260.0 2.4 reshape.324
  262.4 1.9 copy.103
  266.0 10.6 %all_to_all.45 = bf16[2,64,192]{2,0,1:T(2,128)(2,1)S(1)} all-to-all(bf16[2,64,192]{2,0,1:T(2,128)(2,1)S(1)} %copy.107), channel_id=1, replica_groups=mesh['band'=4,'fft'=8] {'band'}, dimensions={1} | all-to-all | bytes 98304 | tf_op jit(solution)/shard_map/all_to_all | solution.py:82
  278.3 130.2 %reduce-scatter.4.cloned.1.call-done = f32[16,16]{1,0:T(8,128)} async-done(((f32[512,16]{1,0:T(8,128)}), f32[16,16]{1,0:T(8,128)}) %reduce-scatter.4.cloned.1.call-update) | async-done | bytes 1040
  (199 shorter events, 76.7 us)
Async XLA Ops:
  7.2 269.6 %copy-start = (bf16[512,16,192]{0,2,1:T(8,128)(2,1)S(1)}, bf16[512,16,192]{0,2,1:T(8,128)(2,1)}, u32[]{:S(2)}) copy-start(bf16[512,16,192]{0,2,1:T(8,128)(2,1)} %param.13) | copy-start | bytes 9437188
  10.7 12.4 %copy-start.5 = (f32[2,64,2,96]{3,2,1,0:T(2,128)}, f32[2,64,2,96]{3,2,1,0:T(2,128)S(1)}, u32[]{:S(2)}) copy-start(f32[2,64,2,96]{3,2,1,0:T(2,128)S(1)} %reshape.295) | copy-start | bytes 294916
  10.8 1.0 copy-start.7
  11.7 0.7 copy-start.1
  11.7 0.8 copy-start.3
  15.5 10.5 %all-to-all-start = ((bf16[8,2,3072]{2,1,0:T(2,128)(2,1)}), bf16[8,2,3072]{2,1,0:T(2,128)(2,1)}, u32[]{:S(2)}, u32[]{:S(2)}) async-start(bf16[8,2,3072]{2,1,0:T(2,128)(2,1)} %reshape.321), calls=%async_computation | async-start | bytes 196608 | tf_op jit(solution)/shard_map/all_to_all | solution.py:62
  87.7 10.8 %slice-start = ((s8[4718592]{0:T(1024)(128)(4,1)}), s8[4194304]{0:T(1024)(128)(4,1)S(1)}, s32[]{:S(2)}) async-start(s8[4718592]{0:T(1024)(128)(4,1)} %bitcast.182), calls=%async_computation.5 | async-start | bytes 8388608
  87.7 10.8 %slice-start.1 = ((s8[4718592]{0:T(1024)(128)(4,1)}), s8[524288]{0:T(1024)(128)(4,1)S(1)}, s32[]{:S(2)}) async-start(s8[4718592]{0:T(1024)(128)(4,1)} %bitcast.182), calls=%async_computation.6 | async-start | bytes 1048576
  87.7 10.8 %copy-start.2 = (f32[1,96,2,192]{3,1,0,2:T(8,128)S(1)}, f32[1,96,2,192]{3,1,0,2:T(8,128)}, u32[]{:S(2)}) copy-start(f32[1,96,2,192]{3,1,0,2:T(8,128)} %copy-done.1) | copy-start | bytes 442372
  87.7 10.8 %copy-start.4 = (f32[1,96,2,192]{3,1,0,2:T(8,128)S(1)}, f32[1,96,2,192]{3,1,0,2:T(8,128)}, u32[]{:S(2)}) copy-start(f32[1,96,2,192]{3,1,0,2:T(8,128)} %copy-done.3) | copy-start | bytes 442372
  250.8 9.2 %all-to-all-start.1 = ((bf16[8,2,3072]{2,1,0:T(2,128)(2,1)}), bf16[8,2,3072]{2,1,0:T(2,128)(2,1)}, u32[]{:S(2)}, u32[]{:S(2)}) async-start(bf16[8,2,3072]{2,1,0:T(2,128)(2,1)} %reshape.323), calls=%async_computation.1 | async-start | bytes 196608 | tf_op jit(solution)/shard_map/all_to_all | solution.py:74
  254.8 153.7 %reduce-scatter.4.cloned.1.call-start = ((), (), s32[]{:S(2)}) async-start(), calls=%async_computation.4 | async-start | bytes 270336
  265.9 142.6 %copy-start.6 = (bf16[2,64,192]{2,1,0:T(8,128)(2,1)}, bf16[2,64,192]{2,1,0:T(8,128)(2,1)S(1)}, u32[]{:S(2)}) copy-start(bf16[2,64,192]{2,1,0:T(8,128)(2,1)S(1)} %reshape.296) | copy-start | bytes 147460
Sparse Core Ops, SparseCore 0:
  278.4 130.0 reduce-scatter.3
where the time goes:
time: 419 us; the launch traced here: 415 us
  matrix products  162 us (39%)
  waiting for transfers between devices  134 us (32%)
  local copies, waits for them, and re-layouts  73.1 us (17%)
  between operations  14.3 us (3%)
  other arithmetic  10.7 us (3%)
  blocking collectives  10.6 us (3%)
  starting transfers between devices  9.18 us (2%)
    unnamed x2, waiting for transfers between devices  130 us
    dot_general x24, matrix products, pick_plane(): jnp.einsum('xs,bcxy->bcsy', onehot_x, plane_box, precision=HIGHEST_MODE)  41.9 us
    dot_general x1, matrix products, per_device(): jnp.einsum('bcpky,ckdx->bdpxy', half_done, forward, precision=HIGHEST_MODE)  39.7 us
    dot_general x24, matrix products, place_plane(): return jnp.einsum('xs,bcsy->bcxy', onehot_x, spread, precision=HIGHEST_MODE)  35.2 us
    dynamic_update_slice x48, local copies, waits for them, and re-layouts, per_device(): picked = lax.map(pick_plane, jnp.moveaxis(freq_box, 2, 0))  33.9 us
    dynamic_slice x48, local copies, waits for them, and re-layouts, per_device(): freq_box = lax.map(place_plane, jnp.moveaxis(planes, 2, 0))  20.5 us
    dot_general x1, matrix products, per_device(): jnp.einsum('bcpxy,cxdk->bdpky', real_field, backward, precision=HIGHEST_M...  19.7 us
    dot_general x1, matrix products, per_device(): jnp.einsum('bcpky,cydq->bdpkq', half_done, backward, precision=HIGHEST_MODE)  12 us
  transfers between devices with their start and end apart: 3, of which 3 were waited for; matrix products, arithmetic and copies ran while one was open for 2% of the time, Pallas kernels for 0%

commit v1 on v0

v1 whole, which is shorter than its diff:
```python
import functools
import math

import jax
import jax.numpy as jnp
import numpy as np
from jax import lax
from jax.experimental import pallas as pl
from jax.experimental.pallas import tpu as pltpu
from jax.sharding import PartitionSpec as P

F32 = jnp.float32
BF16 = jnp.bfloat16
LANES = 128
GROUP = 4
VMEM_BYTES = 40 * 2**20


def dot(a, b, dims=((1,), (0,)), precision=None):
    return lax.dot_general(a, b, (dims, ((), ())), precision=precision, preferred_element_type=F32)


def split_bf16(table):
    high = table.astype(BF16)
    return high, (table - high.astype(np.float32)).astype(BF16)


def angles(grid, half):
    freq = np.arange(half) - half // 2
    return (np.outer(np.arange(grid), freq) % grid) * (2.0 * math.pi / grid)


def z_forward_table(grid, half):
    theta = angles(grid, half)
    rows_re = np.concatenate([np.cos(theta), -np.sin(theta)], 1)
    rows_im = np.concatenate([np.sin(theta), np.cos(theta)], 1)
    return split_bf16(np.concatenate([rows_re, rows_im], 0).astype(np.float32))


def z_backward_table(grid, half, bands):
    theta = angles(grid, half)
    width = 2 * LANES
    table = np.zeros((grid, bands, 2, bands, width), np.float32)
    for band in range(bands):
        table[:, band, 0, band, : 2 * half] = np.concatenate([np.cos(theta), -np.sin(theta)], 1)
        table[:, band, 1, band, : 2 * half] = np.concatenate([np.sin(theta), np.cos(theta)], 1)
    return split_bf16(table.reshape(grid * bands, 2 * bands * width))


def y_table(grid, half):
    theta = angles(grid, half)
    rows_re = np.concatenate([np.cos(theta), -np.sin(theta)], 1)
    rows_im = np.concatenate([np.sin(theta), np.cos(theta)], 1)
    both = np.stack([rows_re, rows_im], 0).reshape(2, grid // 64, 64, 2 * half)
    return both.transpose(1, 0, 2, 3).reshape(2 * grid, 2 * half).astype(BF16)


def x_table(grid, half):
    theta = angles(grid, half)
    return np.concatenate([np.cos(theta), np.sin(theta)], 1).astype(BF16)


def lane_iota(shape):
    return lax.broadcasted_iota(jnp.int32, shape, len(shape) - 1)


def row_iota(shape):
    return lax.broadcasted_iota(jnp.int32, shape, len(shape) - 2)


def to_column(row):
    n = row.shape[1]
    square = jnp.broadcast_to(row, (n, n))
    return jnp.sum(jnp.where(lane_iota((n, n)) == row_iota((n, n)), square, 0.0), axis=1, keepdims=True)


def slot_freq(shape, half):
    lane = lane_iota(shape)
    return (jnp.where(lane < half, lane, lane - half) - half // 2).astype(F32)


def live_slots(length_row, half):
    length = to_column(length_row.astype(F32))
    below = jnp.floor(length * 0.5)
    freq = slot_freq((length.shape[0], 2 * half), half)
    return (freq >= -below) & (freq < length - below)


def z_forward_kernel(coeffs_ref, length_ref, high_ref, low_ref, out_ref):
    bands, sticks, width = coeffs_ref.shape
    grid = high_ref.shape[0] // 2
    parts = out_ref.shape[0]
    depth = grid // parts
    live = live_slots(length_ref[...], width // 2)
    masked = jnp.concatenate([jnp.where(live, coeffs_ref[b], 0.0) for b in range(bands)], 0)
    c_high = masked.astype(BF16)
    c_low = (masked - c_high.astype(F32)).astype(BF16)
    nt = ((1,), (1,))
    sums = dot(high_ref[...], c_high, nt) + dot(high_ref[...], c_low, nt) + dot(low_ref[...], c_high, nt)
    real, imag = sums[:grid], sums[grid:]
    first = lane_iota(real.shape) < sticks
    values = [
        jnp.where(first, real, pltpu.roll(imag, sticks, 1)),
        jnp.where(first, pltpu.roll(real, sticks, 1), imag),
    ]
    for part in range(parts):
        rows = [v[part * depth : (part + 1) * depth] for v in values]
        out_ref[part] = jnp.concatenate(rows, 0).astype(BF16)


def stick_tables_kernel(column_ref, y_ref, back_ref, forward_ref, mask_ref):
    half = y_ref.shape[1] // 2
    for row in range(column_ref.shape[0]):
        column = column_ref[pl.ds(row, 1), :].astype(F32)
        x_pos = jnp.floor((column + 0.5) * (1.0 / half))
        y_pos = column - x_pos * half
        low = lane_iota(column.shape) < LANES // 2
        for odd in range(2):
            part = 2 * row + odd

            def twice(v):
                other = pltpu.roll(v, LANES // 2, 1)
                return jnp.where(low, other, v) if odd else jnp.where(low, v, other)

            at = pl.ds(part * LANES, LANES)
            x_row, y_row = twice(x_pos), twice(y_pos)
            imag_row = jnp.where(low, 0.0, float(half))
            shape = (2 * half, LANES)
            onehot = jnp.where(row_iota(shape).astype(F32) == y_row + imag_row, 1.0, 0.0).astype(BF16)
            back = dot(y_ref[...], onehot)
            back_ref[:, at] = back.astype(BF16)
            forward_ref[at, :] = back.T.astype(BF16)
            mask = jnp.where(row_iota((half, LANES)).astype(F32) == x_row, 1.0, 0.0)
            mask_ref[:, at] = mask.astype(BF16)


def planes_kernel(recv_ref, pot_ref, back_ref, forward_ref, mask_ref, x_ref, xt_ref, out_ref, value_ref, placed_ref, picked_ref, sums_ref):
    step = pl.program_id(0)
    parts, rows, _ = recv_ref.shape
    group, grid, _ = pot_ref.shape
    half = mask_ref.shape[0]
    planes = group * pl.num_programs(0)
    bands = rows // planes
    chunks = 2 * grid // LANES

    @pl.when(step == 0)
    def _():
        for part in range(parts):
            value_ref[:, part * LANES : (part + 1) * LANES] = recv_ref[part].astype(F32)

    mask = mask_ref[...]
    for p in range(group):
        for b in range(bands):
            row = value_ref[pl.ds(b * planes + step * group + p, 1), :].astype(BF16)
            at = (p * bands + b) * half
            placed_ref[at : at + half, :] = mask * row
    spread = dot(placed_ref[...], forward_ref[...])

    first = lane_iota((1, LANES)) < LANES // 2
    sign = jnp.where(first, -1.0, 1.0)
    for p in range(group):
        pot = []
        for k in range(chunks):
            piece = pot_ref[p, :, k * 64 : (k + 1) * 64]
            pot.append(jnp.concatenate([piece, piece], 1))
        pieces = []
        for b in range(bands):
            at = (p * bands + b) * half
            for k in range(chunks):
                top = spread[at : at + half, k * LANES : (k + 1) * LANES]
                turned = sign * pltpu.roll(top, LANES // 2, 1)
                pieces.append(jnp.concatenate([top, turned], 0).astype(BF16))
        for j in range(0, bands * chunks, 2):
            field = dot(x_ref[...], jnp.concatenate(pieces[j : j + 2], 1))
            weight = jnp.concatenate([pot[j % chunks], pot[(j + 1) % chunks]], 1)
            back = dot(xt_ref[...], (field * weight).astype(BF16))
            for i in range(2):
                b, k = (j + i) // chunks, (j + i) % chunks
                at = (p * bands + b) * half
                top = back[:half, i * LANES : (i + 1) * LANES]
                low = back[half:, i * LANES : (i + 1) * LANES]
                result = top - sign * pltpu.roll(low, LANES // 2, 1)
                picked_ref[at : at + half, k * LANES : (k + 1) * LANES] = result.astype(BF16)

    wide = 2 * LANES
    pairs = group * bands
    for n in range(parts * LANES // wide):
        at = slice(n * wide, (n + 1) * wide)
        full = dot(picked_ref[...], back_ref[:, at]).reshape(pairs, half, wide)
        kept = jnp.sum(full * mask_ref[:, at].astype(F32)[None], axis=1)
        sums_ref[pl.ds(pl.multiple_of(step * pairs, pairs), pairs), at] = kept

    @pl.when(step == pl.num_programs(0) - 1)
    def _():
        for part in range(parts):
            out_ref[part] = sums_ref[:, part * LANES : (part + 1) * LANES].astype(BF16)


def z_backward_kernel(norm, recv_ref, coeffs_ref, length_ref, column_ref, high_ref, low_ref, applied_ref, send_ref):
    bands, sticks, width = coeffs_ref.shape
    half = width // 2
    wide = 2 * LANES
    owners, _, own_sticks, _ = send_ref.shape
    me = lax.axis_index("fft")
    at_me = row_iota(column_ref.shape) == me // 2
    column = jnp.sum(jnp.where(at_me, column_ref[...].astype(F32), 0.0), axis=0, keepdims=True)
    column = jnp.where(me % 2 == 1, pltpu.roll(column, LANES // 2, 1), column)[:, :sticks]
    column = to_column(column)
    x_pos = jnp.floor((column + 0.5) * (1.0 / half))
    x_freq = x_pos - half // 2
    y_freq = column - x_pos * half - half // 2
    z_freq = slot_freq((sticks, width), half)
    kinetic = (x_freq * x_freq + y_freq * y_freq + z_freq * z_freq) * (2.0 / (half * half))
    live = live_slots(length_ref[...], half)
    values = recv_ref[...].astype(F32).reshape(-1, LANES).T.astype(BF16)
    sums = dot(values, high_ref[...]) + dot(values, low_ref[...])
    for b in range(bands):
        real_at = b * wide
        imag_at = (bands + b) * wide
        local = sums[:sticks, real_at : real_at + wide] + sums[sticks:, imag_at : imag_at + wide]
        h = jnp.where(live, kinetic * coeffs_ref[b] + local[:, :width] * norm, 0.0)
        applied_ref[b] = h.astype(BF16)
        for r in range(owners):
            send_ref[r, b] = h[r * own_sticks : (r + 1) * own_sticks].astype(BF16)


def margin_kernel(recv_ref, orbitals_ref, order_ref, swap_ref, repeat_ref, keep_ref, fold_ref, out_ref):
    own_sticks, width, n_orbitals = orbitals_ref.shape
    h = recv_ref[...].astype(F32).reshape(-1, width).astype(BF16)
    swapped = dot(h, swap_ref[...])
    both = jnp.concatenate([h.astype(F32), swapped], 0).astype(BF16)
    ordered = dot(order_ref[...], both).astype(BF16)
    columns = ordered.shape[0] // own_sticks
    total = jnp.zeros((columns, n_orbitals), F32)
    for j in range(own_sticks):
        total = total + dot(ordered[j * columns : (j + 1) * columns], orbitals_ref[j])
    exact = lax.Precision.HIGHEST
    spread = dot(total.T, repeat_ref[...], precision=exact) * keep_ref[...]
    packed = dot(fold_ref[...], spread, precision=exact)
    for k in range(out_ref.shape[1]):
        out_ref[:, k, :] = packed[:, k * LANES : (k + 1) * LANES]


def margin_sum_kernel(recv_ref, keep_ref, fold_ref, out_ref):
    total = jnp.sum(recv_ref[...], axis=0)
    flat = jnp.concatenate([total[k : k + 1] for k in range(total.shape[0])], 1)
    spread = flat * keep_ref[...]
    out_ref[...] = dot(spread, fold_ref[...], precision=lax.Precision.HIGHEST)


def call(kernel, out_shape, *operands, **options):
    return pl.pallas_call(
        kernel,
        out_shape=out_shape,
        compiler_params=pltpu.CompilerParams(vmem_limit_bytes=VMEM_BYTES),
        **options,
    )(*operands)


def per_device(n_band, n_fft, band_coeffs, potential, stick_column, stick_length, orbitals):
    bands, sticks, width = band_coeffs.shape
    half = width // 2
    grid = potential.shape[1]
    planes = potential.shape[0]
    all_sticks = stick_column.shape[0]
    n_orbitals, own_sticks, _ = orbitals.shape
    shape = jax.ShapeDtypeStruct
    columns = stick_column.reshape(all_sticks // LANES, LANES)
    lengths = stick_length.reshape(1, sticks)
    exchanged = shape((n_fft, bands * planes, LANES), BF16)

    sent = call(z_forward_kernel, exchanged, band_coeffs, lengths, *z_forward_table(grid, half))
    received = lax.all_to_all(sent, "fft", 0, 0, tiled=True)

    span = n_fft * LANES
    back, forward, mask = call(
        stick_tables_kernel,
        (shape((2 * grid, span), BF16), shape((span, 2 * grid), BF16), shape((half, span), BF16)),
        columns,
        y_table(grid, half),
    )

    table = x_table(grid, half)
    whole = lambda a: pl.BlockSpec(a, lambda i: (0,) * len(a))
    pairs = GROUP * bands
    sent = call(
        planes_kernel,
        exchanged,
        received,
        potential,
        back,
        forward,
        mask,
        table,
        np.ascontiguousarray(table.T),
        grid=(planes // GROUP,),
        in_specs=[
            whole(received.shape),
            pl.BlockSpec((GROUP, grid, grid), lambda i: (i, 0, 0)),
            whole(back.shape),
            whole(forward.shape),
            whole(mask.shape),
            whole(table.shape),
            whole(table.T.shape),
        ],
        out_specs=whole(exchanged.shape),
        scratch_shapes=[
            pltpu.VMEM((bands * planes, span), F32),
            pltpu.VMEM((pairs * half, span), BF16),
            pltpu.VMEM((pairs * half, 2 * grid), BF16),
            pltpu.VMEM((bands * planes, span), F32),
        ],
    )
    received = lax.all_to_all(sent, "fft", 0, 0, tiled=True)

    applied, sent = call(
        functools.partial(z_backward_kernel, 1.0 / float(grid) ** 3),
        (shape((bands, sticks, width), BF16), shape((n_band, bands, own_sticks, width), BF16)),
        received,
        band_coeffs,
        lengths,
        columns,
        *z_backward_table(grid, half, bands),
    )
    received = lax.all_to_all(sent, "band", 0, 0, tiled=True)

    n_columns = 2 * n_band * bands
    n_dev = n_band * n_fft
    own = n_orbitals // n_dev
    packed = own * n_columns
    source = np.arange(n_columns * own_sticks).reshape(n_columns, own_sticks)
    order = np.zeros((n_columns * own_sticks,) * 2, np.float32)
    order[np.arange(n_columns * own_sticks), source.T.reshape(-1)] = 1.0
    swap = np.zeros((width, width), np.float32)
    swap[np.arange(half) + half, np.arange(half)] = 1.0
    swap[np.arange(half), np.arange(half) + half] = -1.0
    slot = np.arange(packed)
    repeat = (np.arange(n_columns)[:, None] == slot[None] % n_columns).astype(np.float32)
    keep = (np.arange(own)[:, None] == slot[None] // n_columns).astype(np.float32)
    fold = (np.arange(n_dev)[:, None] == np.arange(n_orbitals)[None] // own).astype(np.float32)
    sent = call(
        margin_kernel,
        shape((n_dev, packed // LANES, LANES), F32),
        received,
        orbitals.transpose(1, 2, 0),
        order.astype(BF16),
        swap.astype(BF16),
        repeat,
        np.tile(keep, (n_dev, 1)),
        fold,
    )
    received = lax.all_to_all(sent, ("band", "fft"), 0, 0, tiled=True)
    margin = call(
        margin_sum_kernel, shape((own, n_columns), F32), received, keep, np.ascontiguousarray(repeat.T)
    )
    return applied, margin


def solution(mesh):
    placed = (
        P("band", "fft", None),
        P("fft", None, None),
        P(),
        P("fft"),
        P(None, ("band", "fft"), None),
    )
    return jax.shard_map(
        functools.partial(per_device, mesh.shape["band"], mesh.shape["fft"]),
        mesh=mesh,
        in_specs=placed,
        out_specs=(P("band", "fft", None), P(("band", "fft"), None)),
        check_vma=False,
    )
```

time: 419 us -> 67.8 us (0.16)
  matrix products: 162 us -> 0 us
  waiting for transfers between devices: 134 us -> 2.84 us
  local copies, waits for them, and re-layouts: 73.1 us -> 9.26 us
  Pallas kernels: 0 us -> 22.1 us
  blocking collectives: 10.6 us -> 27.1 us
  between operations: 14.3 us -> 0.77 us
  other arithmetic: 10.7 us -> 0 us
    dot_general x55 -> x0, matrix products: 162 us -> none  [the longest x24 41.9 us: pick_plane(): jnp.einsum('xs,bcxy->bcsy', onehot_x, plane_box, precision=HIGHEST_MODE)]
    unnamed x2 -> x0, waiting for transfers between devices: 130 us -> none
    dynamic_update_slice x48 -> x0, local copies, waits for them, and re-layouts: 33.9 us -> none  [per_device(): picked = lax.map(pick_plane, jnp.moveaxis(freq_box, 2, 0))]
    pallas_call x0 -> x6, Pallas kernels: none -> 22.1 us  [call(): pl.pallas_call(kernel, out_shape=out_shape, compiler_params=pltpu.Compile...]
    dynamic_slice x48 -> x0, local copies, waits for them, and re-layouts: 20.5 us -> none  [per_device(): freq_box = lax.map(place_plane, jnp.moveaxis(planes, 2, 0))]
    all_to_all x1 -> x3, blocking collectives: 10.6 us -> 27.1 us  [the longest x1 10.4 us: per_device(): received = lax.all_to_all(sent, 'band', 0, 0, tiled=True)]
    all_to_all x2 -> x1, starting transfers between devices: 9.14 us -> 5.17 us  [per_device(): received = lax.all_to_all(sent, 'fft', 0, 0, tiled=True)]
    unnamed x25 -> x44, local copies, waits for them, and re-layouts: 8.93 us -> 9.26 us
  transfers between devices with their start and end apart: 3 -> 1, of which waited for: 3 -> 1; matrix products, arithmetic and copies ran while one was open for 2% -> 0% of each run, Pallas kernels for 0% -> 1%
where the time goes in v1:
time: 67.8 us; the launch traced here: 67.3 us
  blocking collectives  27.1 us (40%)
  Pallas kernels  22.1 us (33%)
  local copies, waits for them, and re-layouts  9.26 us (14%)
  starting transfers between devices  5.17 us (8%)
  waiting for transfers between devices  2.84 us (4%)
  between operations  0.77 us (1%)
    pallas_call x6, Pallas kernels, call(): pl.pallas_call(kernel, out_shape=out_shape, compiler_params=pltpu.Compile...  22.1 us
    all_to_all x1, blocking collectives, per_device(): received = lax.all_to_all(sent, 'band', 0, 0, tiled=True)  10.4 us
    unnamed x44, local copies, waits for them, and re-layouts  9.26 us
    all_to_all x1, blocking collectives, per_device(): received = lax.all_to_all(sent, ('band', 'fft'), 0, 0, tiled=True)  8.95 us
    all_to_all x1, blocking collectives, per_device(): received = lax.all_to_all(sent, 'fft', 0, 0, tiled=True)  7.71 us
    all_to_all x1, starting transfers between devices, per_device(): received = lax.all_to_all(sent, 'fft', 0, 0, tiled=True)  5.17 us
    all_to_all x1, waiting for transfers between devices, per_device(): received = lax.all_to_all(sent, 'fft', 0, 0, tiled=True)  2.84 us
  transfers between devices with their start and end apart: 1, of which 1 were waited for; matrix products, arithmetic and copies ran while one was open for 0% of the time, Pallas kernels for 1%

profile of v1, /device:TPU:0, one launch (start us, length us, event | category | flops | bytes accessed | tf_op | source)
XLA Modules:
  0.0 67.3 jit_solution(2111963039954067343)
XLA Ops:
  0.6 0.0 copy-start.2
  0.6 0.0 copy-start.4
  0.7 1.0 %copy-done.4 = f32[2,64,192]{2,1,0:T(8,128)S(1)} copy-done((f32[2,64,192]{2,1,0:T(8,128)S(1)}, f32[2,64,192]{2,1,0:T(8,128)}, u32[]{:S(2)}) %copy-start.4) | copy-done | bytes 98328
  1.6 0.0 copy-start.8
  1.6 0.9 %copy-done.8 = bf16[384,192]{1,0:T(8,128)(2,1)S(1)} copy-done((bf16[384,192]{1,0:T(8,128)(2,1)S(1)}, bf16[384,192]{1,0:T(8,128)(2,1)}, u32[]{:S(2)}) %copy-start.8) | copy-done | bytes 147480
  2.5 0.0 copy-start.9
  2.5 0.9 %copy-done.9 = bf16[384,192]{1,0:T(8,128)(2,1)S(1)} copy-done((bf16[384,192]{1,0:T(8,128)(2,1)S(1)}, bf16[384,192]{1,0:T(8,128)(2,1)}, u32[]{:S(2)}) %copy-start.9) | copy-done | bytes 147480
  3.5 0.0 copy-start.20
  3.5 0.7 copy-done.20
  4.1 0.0 copy-start.5
  4.1 1.1 %shard_map.194 = bf16[8,48,128]{2,1,0:T(8,128)(2,1)} custom-call(f32[2,64,192]{2,1,0:T(8,128)S(1)} %copy-done.4, s32[1,64]{1,0:T(1,128)S(1)} %bitcast.6, bf16[384,192]{1,0:T(8,128)(2,1)S(1)} %copy-done.9, bf16[384,192]{1,0:T(8,128)(2,1)S(1)} %copy-done.8), custom_call_target="tpu_custom_call" | custom-call | tf_op jit(solution)/shard_map/pallas_call | solution.py:252
  5.2 5.2 %all-to-all-start = ((bf16[8,48,128]{2,1,0:T(8,128)(2,1)}), bf16[8,48,128]{2,1,0:T(8,128)(2,1)S(1)}, u32[]{:S(2)}, u32[]{:S(2)}) async-start(bf16[8,48,128]{2,1,0:T(8,128)(2,1)} %shard_map.194), calls=%async_computation | async-start | bytes 196608 | tf_op jit(solution)/shard_map/all_to_all | solution.py:273
  10.4 0.0 copy-start.7
  10.4 0.9 %copy-done.7 = bf16[384,192]{1,0:T(8,128)(2,1)S(1)} copy-done((bf16[384,192]{1,0:T(8,128)(2,1)S(1)}, bf16[384,192]{1,0:T(8,128)(2,1)}, u32[]{:S(2)}) %copy-start.7) | copy-done | bytes 147480
  11.3 0.0 copy-start.18
  11.4 0.7 %copy-done.18 = s32[512]{0:T(512)S(1)} copy-done((s32[512]{0:T(512)S(1)}, s32[512]{0:T(512)}, u32[]{:S(2)}) %copy-start.18) | copy-done | bytes 2072
  12.0 0.0 copy-start.19
  12.0 0.0 copy-start.21
  12.0 0.0 copy-start.12
  12.0 0.0 copy-start.16
  12.0 0.7 %shard_map.195 = (bf16[384,1024]{1,0:T(8,128)(2,1)S(1)}, bf16[1024,384]{1,0:T(8,128)(2,1)S(1)}, bf16[96,1024]{1,0:T(8,128)(2,1)S(1)}) custom-call(s32[4,128]{1,0:T(4,128)S(1)} %bitcast.4, bf16[384,192]{1,0:T(8,128)(2,1)S(1)} %copy-done.7), custom_call_target="tpu_custom_call" | custom-call | tf_op jit(solution)/shard_map/pallas_call | solution.py:252
  12.8 2.8 %all-to-all-done.recv_ref = bf16[8,48,128]{2,1,0:T(8,128)(2,1)S(1)} async-done(((bf16[8,48,128]{2,1,0:T(8,128)(2,1)}), bf16[8,48,128]{2,1,0:T(8,128)(2,1)S(1)}, u32[]{:S(2)}, u32[]{:S(2)}) %all-to-all-start) | async-done | bytes 98336 | tf_op jit(solution)/shard_map/all_to_all | solution.py:273
  15.6 0.0 copy-start
  15.6 2.3 %copy-done = f32[24,192,192]{2,1,0:T(8,128)S(1)} copy-done((f32[24,192,192]{2,1,0:T(8,128)S(1)}, f32[24,192,192]{2,1,0:T(8,128)}, u32[]{:S(2)}) %copy-start) | copy-done | bytes 3538968
  18.0 0.0 copy-start.13
  18.0 0.9 %copy-done.13 = bf16[192,192]{1,0:T(8,128)(2,1)S(1)} copy-done((bf16[192,192]{1,0:T(8,128)(2,1)S(1)}, bf16[192,192]{1,0:T(8,128)(2,1)}, u32[]{:S(2)}) %copy-start.13) | copy-done | bytes 73752
  18.8 0.0 copy-start.14
  18.9 0.9 %copy-done.14 = bf16[192,192]{1,0:T(8,128)(2,1)S(1)} copy-done((bf16[192,192]{1,0:T(8,128)(2,1)S(1)}, bf16[192,192]{1,0:T(8,128)(2,1)}, u32[]{:S(2)}) %copy-start.14) | copy-done | bytes 73752
  19.7 0.0 copy-start.3
  19.7 0.0 copy-start.1
  19.7 0.0 copy-start.6
  19.7 0.0 copy-start.10
  19.8 0.0 copy-start.15
  19.8 15.9 %shard_map.196 = bf16[8,48,128]{2,1,0:T(8,128)(2,1)S(1)} custom-call(bf16[8,48,128]{2,1,0:T(8,128)(2,1)S(1)} %all-to-all-done.recv_ref, f32[24,192,192]{2,1,0:T(8,128)S(1)} %copy-done, bf16[384,1024]{1,0:T(8,128)(2,1)S(1)} %get-tuple-element.7.back_ref, bf16[1024,384]{1,0:T(8,128)(2,1)S(1)} %get-tuple-element.8.forward_ref, ...), custom_call_target="tpu_custom_call" | custom-call | tf_op jit(solution)/shard_map/pallas_call | solution.py:252
  35.6 0.0 copy-start.11
  35.6 0.0 copy-start.17
  35.7 7.7 %all_to_all.20.recv_ref = bf16[8,48,128]{2,1,0:T(8,128)(2,1)S(1)} all-to-all(bf16[8,48,128]{2,1,0:T(8,128)(2,1)S(1)} %shard_map.196), channel_id=1, replica_groups=mesh['band'=4,'fft'=8] {'fft'}, dimensions={0} | all-to-all | bytes 196608 | tf_op jit(solution)/shard_map/all_to_all | solution.py:314
  43.4 0.0 copy-done.2
  43.4 0.0 copy-done.5
  43.4 0.0 copy-done.19
  43.4 0.0 copy-done.21
  43.4 0.0 copy-done.3
  43.4 1.1 %shard_map.197 = (bf16[2,64,192]{2,1,0:T(8,128)(2,1)}, bf16[4,2,16,192]{3,2,1,0:T(8,128)(2,1)S(1)}) custom-call(bf16[8,48,128]{2,1,0:T(8,128)(2,1)S(1)} %all_to_all.20.recv_ref, f32[2,64,192]{2,1,0:T(8,128)S(1)} %copy-done.5, s32[1,64]{1,0:T(1,128)S(1)} %bitcast.7, s32[4,128]{1,0:T(4,128)S(1)} %bitcast.5, bf16[384,1024]{1,0:T(8,128)(2,1)S(1)} %copy-done.3, ...), custom_call_target="tpu_custom_call" | custom-call | tf_op jit(solution)/shard_map/pallas_call | solution.py:252
  44.5 10.4 %all_to_all.21.recv_ref = bf16[4,2,16,192]{3,2,1,0:T(8,128)(2,1)S(1)} all-to-all(bf16[4,2,16,192]{3,2,1,0:T(8,128)(2,1)S(1)} %get-tuple-element.11), channel_id=1, replica_groups=mesh['band'=4,'fft'=8] {'band'}, dimensions={0} | all-to-all | bytes 98304 | tf_op jit(solution)/shard_map/all_to_all | solution.py:325
  55.0 0.0 copy-done.12
  55.0 0.0 copy-done.16
  55.0 0.0 copy-done.1
  55.0 0.0 copy-done.6
  55.0 0.0 copy-done.10
  55.0 0.0 copy-done.15
  55.0 2.5 %shard_map.198 = f32[32,2,128]{2,1,0:T(2,128)S(1)} custom-call(bf16[4,2,16,192]{3,2,1,0:T(8,128)(2,1)S(1)} %all_to_all.21.recv_ref, bf16[16,192,512]{2,1,0:T(8,128)(2,1)S(1)} %bitcast.3, bf16[256,256]{1,0:T(8,128)(2,1)S(1)} %copy-done.10, bf16[192,192]{1,0:T(8,128)(2,1)S(1)} %copy-done.12, f32[16,256]{1,0:T(8,128)S(1)} %copy-done.16, ...), custom_call_target="tpu_custom_call" | custom-call | tf_op jit(solution)/shard_map/pallas_call | solution.py:252
  57.5 8.9 %all_to_all.22.recv_ref = f32[32,2,128]{2,1,0:T(2,128)S(1)} all-to-all(f32[32,2,128]{2,1,0:T(2,128)S(1)} %shard_map.198), channel_id=1, replica_groups=mesh['band'=4,'fft'=8] {'band','fft'}, dimensions={0} | all-to-all | bytes 65536 | tf_op jit(solution)/shard_map/all_to_all | solution.py:352
  66.4 0.0 copy-done.11
  66.4 0.0 copy-done.17
  66.4 0.8 %shard_map.199 = f32[16,16]{1,0:T(8,128)} custom-call(f32[32,2,128]{2,1,0:T(2,128)S(1)} %all_to_all.22.recv_ref, f32[16,256]{1,0:T(8,128)S(1)} %copy-done.17, f32[256,16]{1,0:T(8,128)S(1)} %copy-done.11), custom_call_target="tpu_custom_call" | custom-call | tf_op jit(solution)/shard_map/pallas_call | solution.py:252
Async XLA Ops:
  0.6 42.7 %copy-start.2 = (bf16[384,1024]{1,0:T(8,128)(2,1)S(1)}, bf16[384,1024]{1,0:T(8,128)(2,1)}, u32[]{:S(2)}) copy-start(bf16[384,1024]{1,0:T(8,128)(2,1)} %constant.34.clone.low_ref) | copy-start | bytes 2359300
  0.6 1.0 %copy-start.4 = (f32[2,64,192]{2,1,0:T(8,128)S(1)}, f32[2,64,192]{2,1,0:T(8,128)}, u32[]{:S(2)}) copy-start(f32[2,64,192]{2,1,0:T(8,128)} %coeffs_ref.3) | copy-start | bytes 294916
  1.6 0.9 %copy-start.8 = (bf16[384,192]{1,0:T(8,128)(2,1)S(1)}, bf16[384,192]{1,0:T(8,128)(2,1)}, u32[]{:S(2)}) copy-start(bf16[384,192]{1,0:T(8,128)(2,1)} %constant.29.clone.low_ref) | copy-start | bytes 442372
  2.5 0.9 %copy-start.9 = (bf16[384,192]{1,0:T(8,128)(2,1)S(1)}, bf16[384,192]{1,0:T(8,128)(2,1)}, u32[]{:S(2)}) copy-start(bf16[384,192]{1,0:T(8,128)(2,1)} %constant.28.clone.high_ref) | copy-start | bytes 442372
  3.5 0.7 copy-start.20
  4.1 39.2 %copy-start.5 = (f32[2,64,192]{2,1,0:T(8,128)S(1)}, f32[2,64,192]{2,1,0:T(8,128)}, u32[]{:S(2)}) copy-start(f32[2,64,192]{2,1,0:T(8,128)} %coeffs_ref.3) | copy-start | bytes 294916
  5.2 10.4 %all-to-all-start = ((bf16[8,48,128]{2,1,0:T(8,128)(2,1)}), bf16[8,48,128]{2,1,0:T(8,128)(2,1)S(1)}, u32[]{:S(2)}, u32[]{:S(2)}) async-start(bf16[8,48,128]{2,1,0:T(8,128)(2,1)} %shard_map.194), calls=%async_computation | async-start | bytes 196608 | tf_op jit(solution)/shard_map/all_to_all | solution.py:273
  10.4 0.9 %copy-start.7 = (bf16[384,192]{1,0:T(8,128)(2,1)S(1)}, bf16[384,192]{1,0:T(8,128)(2,1)}, u32[]{:S(2)}) copy-start(bf16[384,192]{1,0:T(8,128)(2,1)} %constant.30.clone.y_ref) | copy-start | bytes 442372
  11.3 0.7 %copy-start.18 = (s32[512]{0:T(512)S(1)}, s32[512]{0:T(512)}, u32[]{:S(2)}) copy-start(s32[512]{0:T(512)} %param.21) | copy-start | bytes 6148
  12.0 31.3 %copy-start.19 = (s32[512]{0:T(512)S(1)}, s32[512]{0:T(512)}, u32[]{:S(2)}) copy-start(s32[512]{0:T(512)} %param.21) | copy-start | bytes 6148
  12.0 31.3 %copy-start.21 = (s32[64]{0:T(128)S(1)}, s32[64]{0:T(128)}, u32[]{:S(2)}) copy-start(s32[64]{0:T(128)} %param.22) | copy-start | bytes 772
  12.0 42.9 %copy-start.12 = (bf16[192,192]{1,0:T(8,128)(2,1)S(1)}, bf16[192,192]{1,0:T(8,128)(2,1)}, u32[]{:S(2)}) copy-start(bf16[192,192]{1,0:T(8,128)(2,1)} %constant.36.clone.swap_ref) | copy-start | bytes 221188
  12.0 42.9 %copy-start.16 = (f32[16,256]{1,0:T(8,128)S(1)}, f32[16,256]{1,0:T(8,128)}, u32[]{:S(2)}) copy-start(f32[16,256]{1,0:T(8,128)} %constant.37.clone.repeat_ref) | copy-start | bytes 49156
  15.6 2.3 %copy-start = (f32[24,192,192]{2,1,0:T(8,128)S(1)}, f32[24,192,192]{2,1,0:T(8,128)}, u32[]{:S(2)}) copy-start(f32[24,192,192]{2,1,0:T(8,128)} %pot_ref.1) | copy-start | bytes 10616836
  18.0 0.9 %copy-start.13 = (bf16[192,192]{1,0:T(8,128)(2,1)S(1)}, bf16[192,192]{1,0:T(8,128)(2,1)}, u32[]{:S(2)}) copy-start(bf16[192,192]{1,0:T(8,128)(2,1)} %constant.32.clone.xt_ref) | copy-start | bytes 221188
  18.8 0.9 %copy-start.14 = (bf16[192,192]{1,0:T(8,128)(2,1)S(1)}, bf16[192,192]{1,0:T(8,128)(2,1)}, u32[]{:S(2)}) copy-start(bf16[192,192]{1,0:T(8,128)(2,1)} %constant.31.clone.x_ref) | copy-start | bytes 221188
  19.7 23.7 %copy-start.3 = (bf16[384,1024]{1,0:T(8,128)(2,1)S(1)}, bf16[384,1024]{1,0:T(8,128)(2,1)}, u32[]{:S(2)}) copy-start(bf16[384,1024]{1,0:T(8,128)(2,1)} %constant.33.clone.high_ref) | copy-start | bytes 2359300
  19.7 35.2 %copy-start.1 = (bf16[512,16,192]{0,2,1:T(8,128)(2,1)S(1)}, bf16[512,16,192]{0,2,1:T(8,128)(2,1)}, u32[]{:S(2)}) copy-start(bf16[512,16,192]{0,2,1:T(8,128)(2,1)} %param.23) | copy-start | bytes 9437188
  19.7 35.2 %copy-start.6 = (f32[512,256]{1,0:T(8,128)S(1)}, f32[512,256]{1,0:T(8,128)}, u32[]{:S(2)}) copy-start(f32[512,256]{1,0:T(8,128)} %constant.38.clone.keep_ref) | copy-start | bytes 1572868
  19.7 35.2 %copy-start.10 = (bf16[256,256]{1,0:T(8,128)(2,1)S(1)}, bf16[256,256]{1,0:T(8,128)(2,1)}, u32[]{:S(2)}) copy-start(bf16[256,256]{1,0:T(8,128)(2,1)} %constant.35.clone.order_ref) | copy-start | bytes 393220
  19.8 35.2 %copy-start.15 = (f32[32,512]{1,0:T(8,128)S(1)}, f32[32,512]{1,0:T(8,128)}, u32[]{:S(2)}) copy-start(f32[32,512]{1,0:T(8,128)} %constant.39.clone.fold_ref) | copy-start | bytes 196612
  35.6 30.8 %copy-start.11 = (f32[256,16]{1,0:T(8,128)S(1)}, f32[256,16]{1,0:T(8,128)}, u32[]{:S(2)}) copy-start(f32[256,16]{1,0:T(8,128)} %constant.41.clone.fold_ref) | copy-start | bytes 49156
  35.6 30.8 %copy-start.17 = (f32[16,256]{1,0:T(8,128)S(1)}, f32[16,256]{1,0:T(8,128)}, u32[]{:S(2)}) copy-start(f32[16,256]{1,0:T(8,128)} %constant.40.clone.keep_ref) | copy-start | bytes 49156

commit v2 on v1

--- a/solution.py
+++ b/solution.py
@@ -48,16 +48,19 @@
 
 
 def y_table(grid, half):
+    theta = angles(grid, half)[: grid // 2 + 1]
+    table = np.zeros((2, LANES, half), np.float32)
+    table[0, : grid // 2 + 1] = np.cos(theta)
+    table[1, 1 : grid // 2] = np.sin(theta)[1:-1]
+    return table.reshape(2 * LANES, half).astype(BF16)
+
+
+def x_tables(grid, half):
     theta = angles(grid, half)
-    rows_re = np.concatenate([np.cos(theta), -np.sin(theta)], 1)
-    rows_im = np.concatenate([np.sin(theta), np.cos(theta)], 1)
-    both = np.stack([rows_re, rows_im], 0).reshape(2, grid // 64, 64, 2 * half)
-    return both.transpose(1, 0, 2, 3).reshape(2 * grid, 2 * half).astype(BF16)
-
-
-def x_table(grid, half):
-    theta = angles(grid, half)
-    return np.concatenate([np.cos(theta), np.sin(theta)], 1).astype(BF16)
+    cosine, sine = np.cos(theta), np.sin(theta)
+    real = np.concatenate([cosine, -sine], 1)
+    imag = np.concatenate([cosine, sine], 1)
+    return np.stack([real, imag, imag.T]).astype(BF16)
 
 
 def lane_iota(shape):
@@ -86,17 +89,31 @@
     return (freq >= -below) & (freq < length - below)
 
 
-def z_forward_kernel(coeffs_ref, length_ref, high_ref, low_ref, out_ref):
+def start_all(*copies):
+    for copy in copies:
+        copy.start()
+    return copies
+
+
+def z_forward_kernel(coeffs_hbm, length_hbm, table_hbm, out_ref, coeffs_ref, length_ref, table_ref, sem):
+    copies = start_all(
+        pltpu.make_async_copy(length_hbm, length_ref, sem.at[0]),
+        pltpu.make_async_copy(coeffs_hbm, coeffs_ref, sem.at[1]),
+        pltpu.make_async_copy(table_hbm, table_ref, sem.at[2]),
+    )
+    for copy in copies:
+        copy.wait()
     bands, sticks, width = coeffs_ref.shape
-    grid = high_ref.shape[0] // 2
+    grid = table_ref.shape[0] // 4
     parts = out_ref.shape[0]
     depth = grid // parts
+    high, low = table_ref[: 2 * grid], table_ref[2 * grid :]
     live = live_slots(length_ref[...], width // 2)
     masked = jnp.concatenate([jnp.where(live, coeffs_ref[b], 0.0) for b in range(bands)], 0)
     c_high = masked.astype(BF16)
     c_low = (masked - c_high.astype(F32)).astype(BF16)
     nt = ((1,), (1,))
-    sums = dot(high_ref[...], c_high, nt) + dot(high_ref[...], c_low, nt) + dot(low_ref[...], c_high, nt)
+    sums = dot(high, c_high, nt) + dot(high, c_low, nt) + dot(low, c_high, nt)
     real, imag = sums[:grid], sums[grid:]
     first = lane_iota(real.shape) < sticks
     values = [
@@ -108,92 +125,108 @@
         out_ref[part] = jnp.concatenate(rows, 0).astype(BF16)
 
 
-def stick_tables_kernel(column_ref, y_ref, back_ref, forward_ref, mask_ref):
-    half = y_ref.shape[1] // 2
+def tables_kernel(
+    column_hbm, y_hbm, x_hbm, pot_hbm, back_ref, forward_ref, mask_ref, x_ref, pot_ref, column_ref, y_ref, raw_ref, sem
+):
+    planes, grid, _ = raw_ref.shape
+    small = start_all(
+        pltpu.make_async_copy(column_hbm, column_ref, sem.at[0]),
+        pltpu.make_async_copy(y_hbm, y_ref, sem.at[1]),
+        pltpu.make_async_copy(x_hbm, x_ref, sem.at[2]),
+    )
+    group = [pl.ds(i, GROUP) for i in range(0, planes, GROUP)]
+    large = start_all(*[
+        pltpu.make_async_copy(pot_hbm.at[at], raw_ref.at[at], sem.at[3 + i]) for i, at in enumerate(group)
+    ])
+    for copy in small:
+        copy.wait()
+    half = y_ref.shape[1]
     for row in range(column_ref.shape[0]):
         column = column_ref[pl.ds(row, 1), :].astype(F32)
         x_pos = jnp.floor((column + 0.5) * (1.0 / half))
         y_pos = column - x_pos * half
-        low = lane_iota(column.shape) < LANES // 2
-        for odd in range(2):
-            part = 2 * row + odd
-
-            def twice(v):
-                other = pltpu.roll(v, LANES // 2, 1)
-                return jnp.where(low, other, v) if odd else jnp.where(low, v, other)
-
-            at = pl.ds(part * LANES, LANES)
-            x_row, y_row = twice(x_pos), twice(y_pos)
-            imag_row = jnp.where(low, 0.0, float(half))
-            shape = (2 * half, LANES)
-            onehot = jnp.where(row_iota(shape).astype(F32) == y_row + imag_row, 1.0, 0.0).astype(BF16)
-            back = dot(y_ref[...], onehot)
-            back_ref[:, at] = back.astype(BF16)
-            forward_ref[at, :] = back.T.astype(BF16)
-            mask = jnp.where(row_iota((half, LANES)).astype(F32) == x_row, 1.0, 0.0)
-            mask_ref[:, at] = mask.astype(BF16)
-
-
-def planes_kernel(recv_ref, pot_ref, back_ref, forward_ref, mask_ref, x_ref, xt_ref, out_ref, value_ref, placed_ref, picked_ref, sums_ref):
-    step = pl.program_id(0)
+        at = pl.ds(row * LANES, LANES)
+        index = row_iota((half, LANES)).astype(F32)
+        back = dot(y_ref[...], jnp.where(index == y_pos, 1.0, 0.0).astype(BF16))
+        back_ref[:, at] = back.astype(BF16)
+        forward_ref[at, :] = back.T.astype(BF16)
+        mask_ref[:, at] = jnp.where(index == x_pos, 1.0, 0.0)
+    lane = lane_iota((grid, LANES))
+    low_at = jnp.clip(grid - LANES - lane, 0, LANES - 1)
+    high_at = jnp.clip(grid - lane, 0, LANES - 1)
+    for i, copy in enumerate(large):
+        copy.wait()
+        for z in range(i * GROUP, (i + 1) * GROUP):
+            near = raw_ref[z, :, :LANES]
+            far = raw_ref[z, :, LANES:]
+            far = jnp.concatenate([far, jnp.zeros((grid, 2 * LANES - grid), F32)], 1)
+            pot_ref[z, :, :LANES] = jnp.where(lane <= grid // 2, near, 0.0)
+            from_far = jnp.take_along_axis(far, low_at, axis=1)
+            from_near = jnp.take_along_axis(near, high_at, axis=1)
+            mirrored = jnp.where(lane <= grid - LANES, from_far, from_near)
+            pot_ref[z, :, LANES:] = jnp.where((lane > 0) & (lane < grid // 2), mirrored, 0.0)
+
+
+def planes_kernel(recv_ref, pot_ref, back_ref, forward_ref, mask_ref, x_ref, out_ref, value_ref, sums_ref):
     parts, rows, _ = recv_ref.shape
-    group, grid, _ = pot_ref.shape
+    planes = pot_ref.shape[0]
     half = mask_ref.shape[0]
-    planes = group * pl.num_programs(0)
     bands = rows // planes
-    chunks = 2 * grid // LANES
-
-    @pl.when(step == 0)
-    def _():
-        for part in range(parts):
-            value_ref[:, part * LANES : (part + 1) * LANES] = recv_ref[part].astype(F32)
-
-    mask = mask_ref[...]
-    for p in range(group):
+    first = lane_iota((rows, LANES)) < LANES // 2
+
+    def halves(even, odd):
+        low = jnp.where(first, even, pltpu.roll(odd, LANES // 2, 1))
+        high = jnp.where(first, pltpu.roll(even, LANES // 2, 1), odd)
+        return low, high
+
+    for pair in range(parts // 2):
+        at = slice(pair * LANES, (pair + 1) * LANES)
+        value_ref[0, :, at], value_ref[1, :, at] = halves(
+            recv_ref[2 * pair].astype(F32), recv_ref[2 * pair + 1].astype(F32)
+        )
+
+    def one_plane(z):
+        mask = mask_ref[...].astype(BF16)
+        placed = []
         for b in range(bands):
-            row = value_ref[pl.ds(b * planes + step * group + p, 1), :].astype(BF16)
-            at = (p * bands + b) * half
-            placed_ref[at : at + half, :] = mask * row
-    spread = dot(placed_ref[...], forward_ref[...])
-
-    first = lane_iota((1, LANES)) < LANES // 2
-    sign = jnp.where(first, -1.0, 1.0)
-    for p in range(group):
-        pot = []
-        for k in range(chunks):
-            piece = pot_ref[p, :, k * 64 : (k + 1) * 64]
-            pot.append(jnp.concatenate([piece, piece], 1))
-        pieces = []
+            for c in range(2):
+                placed.append(mask * value_ref[c, pl.ds(b * planes + z, 1), :].astype(BF16))
+        spread = dot(jnp.concatenate(placed, 0), forward_ref[...])
+        pot = pot_ref[z]
+        folded = []
         for b in range(bands):
-            at = (p * bands + b) * half
-            for k in range(chunks):
-                top = spread[at : at + half, k * LANES : (k + 1) * LANES]
-                turned = sign * pltpu.roll(top, LANES // 2, 1)
-                pieces.append(jnp.concatenate([top, turned], 0).astype(BF16))
-        for j in range(0, bands * chunks, 2):
-            field = dot(x_ref[...], jnp.concatenate(pieces[j : j + 2], 1))
-            weight = jnp.concatenate([pot[j % chunks], pot[(j + 1) % chunks]], 1)
-            back = dot(xt_ref[...], (field * weight).astype(BF16))
-            for i in range(2):
-                b, k = (j + i) // chunks, (j + i) % chunks
-                at = (p * bands + b) * half
-                top = back[:half, i * LANES : (i + 1) * LANES]
-                low = back[half:, i * LANES : (i + 1) * LANES]
-                result = top - sign * pltpu.roll(low, LANES // 2, 1)
-                picked_ref[at : at + half, k * LANES : (k + 1) * LANES] = result.astype(BF16)
-
-    wide = 2 * LANES
-    pairs = group * bands
-    for n in range(parts * LANES // wide):
-        at = slice(n * wide, (n + 1) * wide)
-        full = dot(picked_ref[...], back_ref[:, at]).reshape(pairs, half, wide)
-        kept = jnp.sum(full * mask_ref[:, at].astype(F32)[None], axis=1)
-        sums_ref[pl.ds(pl.multiple_of(step * pairs, pairs), pairs), at] = kept
-
-    @pl.when(step == pl.num_programs(0) - 1)
-    def _():
-        for part in range(parts):
-            out_ref[part] = sums_ref[:, part * LANES : (part + 1) * LANES].astype(BF16)
+            at = 2 * b * half
+            real, imag = spread[at : at + half], spread[at + half : at + 2 * half]
+            rc, rs, ic, si = real[:, :LANES], real[:, LANES:], imag[:, :LANES], imag[:, LANES:]
+            y_re = jnp.concatenate([rc - si, rc + si], 1).astype(BF16)
+            y_im = jnp.concatenate([ic + rs, ic - rs], 1).astype(BF16)
+            p_re = dot(x_ref[0], jnp.concatenate([y_re, y_im], 0)) * pot
+            p_im = dot(x_ref[1], jnp.concatenate([y_im, y_re], 0)) * pot
+            s_re = dot(x_ref[2], p_re.astype(BF16))
+            s_im = dot(x_ref[2], p_im.astype(BF16))
+            q_re = s_re[:half] + s_im[half:]
+            q_im = s_im[:half] - s_re[half:]
+            rp, rm, ip, im = q_re[:, :LANES], q_re[:, LANES:], q_im[:, :LANES], q_im[:, LANES:]
+            folded.append(jnp.concatenate([rp + rm, ip - im], 1).astype(BF16))
+            folded.append(jnp.concatenate([ip + im, rm - rp], 1).astype(BF16))
+        full = dot(jnp.concatenate(folded, 0), back_ref[...])
+        for b in range(bands):
+            for c in range(2):
+                at = (2 * b + c) * half
+                kept = jnp.sum(full[at : at + half] * mask_ref[...], axis=0, keepdims=True)
+                sums_ref[c, pl.ds(z * bands + b, 1), :] = kept
+
+    def body(step, carry):
+        for p in range(GROUP):
+            one_plane(step * GROUP + p)
+        return carry
+
+    lax.fori_loop(0, planes // GROUP, body, 0)
+    for pair in range(parts // 2):
+        at = slice(pair * LANES, (pair + 1) * LANES)
+        even, odd = halves(sums_ref[0, :, at], sums_ref[1, :, at])
+        out_ref[2 * pair] = even.astype(BF16)
+        out_ref[2 * pair + 1] = odd.astype(BF16)
 
 
 def z_backward_kernel(norm, recv_ref, coeffs_ref, length_ref, column_ref, high_ref, low_ref, applied_ref, send_ref):
@@ -269,46 +302,61 @@
     lengths = stick_length.reshape(1, sticks)
     exchanged = shape((n_fft, bands * planes, LANES), BF16)
 
-    sent = call(z_forward_kernel, exchanged, band_coeffs, lengths, *z_forward_table(grid, half))
+    in_hbm = pl.BlockSpec(memory_space=pltpu.HBM)
+    dma = pltpu.SemaphoreType.DMA
+
+    z_table = np.concatenate(z_forward_table(grid, half), 0)
+    sent = call(
+        z_forward_kernel,
+        exchanged,
+        band_coeffs,
+        lengths,
+        z_table,
+        in_specs=[in_hbm] * 3,
+        scratch_shapes=[
+            pltpu.VMEM(band_coeffs.shape, F32),
+            pltpu.VMEM(lengths.shape, jnp.int32),
+            pltpu.VMEM(z_table.shape, BF16),
+            dma((3,)),
+        ],
+    )
     received = lax.all_to_all(sent, "fft", 0, 0, tiled=True)
 
-    span = n_fft * LANES
-    back, forward, mask = call(
-        stick_tables_kernel,
-        (shape((2 * grid, span), BF16), shape((span, 2 * grid), BF16), shape((half, span), BF16)),
+    wide = 2 * LANES
+    table_y, table_x = y_table(grid, half), x_tables(grid, half)
+    back, forward, mask, table_x, weights = call(
+        tables_kernel,
+        (
+            shape((wide, all_sticks), BF16),
+            shape((all_sticks, wide), BF16),
+            shape((half, all_sticks), F32),
+            shape(table_x.shape, BF16),
+            shape((planes, grid, wide), F32),
+        ),
         columns,
-        y_table(grid, half),
-    )
-
-    table = x_table(grid, half)
-    whole = lambda a: pl.BlockSpec(a, lambda i: (0,) * len(a))
-    pairs = GROUP * bands
+        table_y,
+        table_x,
+        potential,
+        in_specs=[in_hbm] * 4,
+        scratch_shapes=[
+            pltpu.VMEM(columns.shape, jnp.int32),
+            pltpu.VMEM(table_y.shape, BF16),
+            pltpu.VMEM(potential.shape, F32),
+            dma((3 + planes // GROUP,)),
+        ],
+    )
     sent = call(
         planes_kernel,
         exchanged,
         received,
-        potential,
+        weights,
         back,
         forward,
         mask,
-        table,
-        np.ascontiguousarray(table.T),
-        grid=(planes // GROUP,),
-        in_specs=[
-            whole(received.shape),
-            pl.BlockSpec((GROUP, grid, grid), lambda i: (i, 0, 0)),
-            whole(back.shape),
-            whole(forward.shape),
-            whole(mask.shape),
-            whole(table.shape),
-            whole(table.T.shape),
-        ],
-        out_specs=whole(exchanged.shape),
+        table_x,
         scratch_shapes=[
-            pltpu.VMEM((bands * planes, span), F32),
-            pltpu.VMEM((pairs * half, span), BF16),
-            pltpu.VMEM((pairs * half, 2 * grid), BF16),
-            pltpu.VMEM((bands * planes, span), F32),
+            pltpu.VMEM((2, bands * planes, all_sticks), F32),
+            pltpu.VMEM((2, bands * planes, all_sticks), F32),
         ],
     )
     received = lax.all_to_all(sent, "fft", 0, 0, tiled=True)

time: 67.8 us -> 84.4 us (1.24)
  local copies, waits for them, and re-layouts: 9.26 us -> 18.5 us
  Pallas kernels: 22.1 us -> 30.7 us
  waiting for transfers between devices: 2.84 us -> 0.01 us
  blocking collectives: 27.1 us -> 28.5 us
    unnamed x44 -> x60, local copies, waits for them, and re-layouts: 9.26 us -> 18.5 us
    pallas_call x6, Pallas kernels: 22.1 us -> 30.7 us  [call(): pl.pallas_call(kernel, out_shape=out_shape, compiler_params=pltpu.Compile...]
    all_to_all x1, waiting for transfers between devices: 2.84 us -> 0.01 us  [per_device(): received = lax.all_to_all(sent, 'fft', 0, 0, tiled=True)]
    all_to_all x1, blocking collectives: 7.71 us -> 9.17 us  [per_device(): received = lax.all_to_all(sent, 'fft', 0, 0, tiled=True)]
  transfers between devices with their start and end apart: 1 -> 1, of which waited for: 1 -> 0; matrix products, arithmetic and copies ran while one was open for 0% -> 0% of each run, Pallas kernels for 1% -> 3%
where the time goes in v2:
time: 84.4 us; the launch traced here: 83.7 us
  Pallas kernels  30.7 us (36%)
  blocking collectives  28.5 us (34%)
  local copies, waits for them, and re-layouts  18.5 us (22%)
  starting transfers between devices  5.18 us (6%)
    pallas_call x6, Pallas kernels, call(): pl.pallas_call(kernel, out_shape=out_shape, compiler_params=pltpu.Compile...  30.7 us
    unnamed x60, local copies, waits for them, and re-layouts  18.5 us
    all_to_all x1, blocking collectives, per_device(): received = lax.all_to_all(sent, 'band', 0, 0, tiled=True)  10.4 us
    all_to_all x1, blocking collectives, per_device(): received = lax.all_to_all(sent, 'fft', 0, 0, tiled=True)  9.17 us
    all_to_all x1, blocking collectives, per_device(): received = lax.all_to_all(sent, ('band', 'fft'), 0, 0, tiled=True)  8.95 us
    all_to_all x1, starting transfers between devices, per_device(): received = lax.all_to_all(sent, 'fft', 0, 0, tiled=True)  5.18 us
  transfers between devices with their start and end apart: 1, of which 0 were waited for; matrix products, arithmetic and copies ran while one was open for 0% of the time, Pallas kernels for 3%

profile of v2, /device:TPU:0, one launch (start us, length us, event | category | flops | bytes accessed | tf_op | source)
XLA Modules:
  0.0 83.7 jit_solution(9988390030998774831)
XLA Ops:
  0.6 0.0 copy-start.6
  0.6 0.9 %copy-done.6 = f32[2,64,192]{2,1,0:T(8,128)S(1)} copy-done((f32[2,64,192]{2,1,0:T(8,128)S(1)}, f32[2,64,192]{2,1,0:T(8,128)}, u32[]{:S(2)}) %copy-start.6) | copy-done | bytes 98328
  1.5 0.0 copy-start.9
  1.5 1.0 %copy-done.9 = bf16[768,192]{1,0:T(8,128)(2,1)S(1)} copy-done((bf16[768,192]{1,0:T(8,128)(2,1)S(1)}, bf16[768,192]{1,0:T(8,128)(2,1)}, u32[]{:S(2)}) %copy-start.9) | copy-done | bytes 294936
  2.5 0.0 copy-start.28
  2.5 0.7 copy-done.28
  3.2 1.5 %shard_map.176 = bf16[8,48,128]{2,1,0:T(8,128)(2,1)} custom-call(f32[2,64,192]{2,1,0:T(8,128)S(1)} %copy-done.6, s32[1,64]{1,0:T(1,128)S(1)} %bitcast.6, bf16[768,192]{1,0:T(8,128)(2,1)S(1)} %copy-done.9), custom_call_target="tpu_custom_call" | custom-call | tf_op jit(solution)/shard_map/pallas_call | solution.py:285
  4.7 5.2 %all-to-all-start = ((bf16[8,48,128]{2,1,0:T(8,128)(2,1)}), bf16[8,48,128]{2,1,0:T(8,128)(2,1)S(1)}, u32[]{:S(2)}, u32[]{:S(2)}) async-start(bf16[8,48,128]{2,1,0:T(8,128)(2,1)} %shard_map.176), calls=%async_computation | async-start | bytes 196608 | tf_op jit(solution)/shard_map/all_to_all | solution.py:323
  9.8 0.0 copy-start
  9.9 2.3 %copy-done = f32[24,192,192]{2,1,0:T(8,128)S(1)} copy-done((f32[24,192,192]{2,1,0:T(8,128)S(1)}, f32[24,192,192]{2,1,0:T(8,128)}, u32[]{:S(2)}) %copy-start) | copy-done | bytes 3538968
  12.2 0.0 copy-start.10
  12.2 1.0 %copy-done.10 = bf16[3,192,192]{2,1,0:T(8,128)(2,1)S(1)} copy-done((bf16[3,192,192]{2,1,0:T(8,128)(2,1)S(1)}, bf16[3,192,192]{2,1,0:T(8,128)(2,1)}, u32[]{:S(2)}) %copy-start.10) | copy-done | bytes 221208
  13.1 0.0 copy-start.23
  13.1 0.8 %copy-done.23 = bf16[256,96]{1,0:T(8,128)(2,1)S(1)} copy-done((bf16[256,96]{1,0:T(8,128)(2,1)S(1)}, bf16[256,96]{1,0:T(8,128)(2,1)}, u32[]{:S(2)}) %copy-start.23) | copy-done | bytes 49176
  14.0 0.0 copy-start.26
  14.0 0.7 copy-done.26
  14.7 0.0 copy-start.7
  14.7 0.0 copy-start.27
  14.7 0.0 copy-start.29
  14.7 0.0 copy-start.3
  14.7 0.0 copy-start.19
  14.7 0.0 copy-start.24
  14.7 2.6 %shard_map.177 = (bf16[256,512]{1,0:T(8,128)(2,1)S(1)}, bf16[512,256]{1,0:T(8,128)(2,1)S(1)}, f32[96,512]{1,0:T(8,128)S(1)}, bf16[3,192,192]{2,1,0:T(8,128)(2,1)S(1)}, f32[24,192,256]{2,1,0:T(8,128)S(1)}) custom-call(s32[4,128]{1,0:T(4,128)S(1)} %bitcast.4, bf16[256,96]{1,0:T(8,128)(2,1)S(1)} %copy-done.23, bf16[3,192,192]{2,1,0:T(8,128)(2,1)S(1)} %copy-done.10, ...), custom_call_target="tpu_custom_call" | custom-call | tf_op jit(solution)/shard_map/pallas_call | solution.py:285
  17.3 0.0 copy-start.1
  17.3 2.1 %copy-done.1 = f32[24,192,256]{2,1,0:T(8,128)} copy-done((f32[24,192,256]{2,1,0:T(8,128)}, f32[24,192,256]{2,1,0:T(8,128)S(1)}, u32[]{:S(2)}) %copy-start.1) | copy-done | bytes 4718616
  19.5 0.0 copy-start.11
  19.5 0.7 copy-done.11
  20.2 0.0 copy-start.13
  20.2 0.7 copy-done.13
  20.9 0.0 copy-start.15
  20.9 0.7 copy-done.15
  21.6 0.0 copy-start.17
  21.6 0.7 copy-done.17
  22.3 0.0 all-to-all-done.recv_ref
  22.3 0.0 copy-start.2
  22.3 2.3 %copy-done.2 = f32[24,192,256]{2,1,0:T(8,128)S(1)} copy-done((f32[24,192,256]{2,1,0:T(8,128)S(1)}, f32[24,192,256]{2,1,0:T(8,128)}, u32[]{:S(2)}) %copy-start.2) | copy-done | bytes 4718616
  24.7 1.0 %copy-done.12 = bf16[3,192,192]{2,1,0:T(8,128)(2,1)S(1)} copy-done((bf16[3,192,192]{2,1,0:T(8,128)(2,1)S(1)}, bf16[3,192,192]{2,1,0:T(8,128)(2,1)}, u32[]{:S(2)}) %copy-start.12) | copy-done | bytes 221208
  25.6 0.0 copy-start.14
  25.6 0.9 %copy-done.14 = bf16[256,512]{1,0:T(8,128)(2,1)S(1)} copy-done((bf16[256,512]{1,0:T(8,128)(2,1)S(1)}, bf16[256,512]{1,0:T(8,128)(2,1)}, u32[]{:S(2)}) %copy-start.14) | copy-done | bytes 262168
  26.6 0.9 %copy-done.16 = bf16[512,256]{1,0:T(8,128)(2,1)S(1)} copy-done((bf16[512,256]{1,0:T(8,128)(2,1)S(1)}, bf16[512,256]{1,0:T(8,128)(2,1)}, u32[]{:S(2)}) %copy-start.16) | copy-done | bytes 262168
  27.5 0.9 %copy-done.18 = f32[96,512]{1,0:T(8,128)S(1)} copy-done((f32[96,512]{1,0:T(8,128)S(1)}, f32[96,512]{1,0:T(8,128)}, u32[]{:S(2)}) %copy-start.18) | copy-done | bytes 196632
  28.5 0.0 copy-start.22
  28.5 0.0 copy-start.20
  28.5 0.0 copy-start.25
  28.5 22.2 %shard_map.178 = bf16[8,48,128]{2,1,0:T(8,128)(2,1)S(1)} custom-call(bf16[8,48,128]{2,1,0:T(8,128)(2,1)S(1)} %all-to-all-done.recv_ref, f32[24,192,256]{2,1,0:T(8,128)S(1)} %copy-done.2, bf16[256,512]{1,0:T(8,128)(2,1)S(1)} %copy-done.14, bf16[512,256]{1,0:T(8,128)(2,1)S(1)} %copy-done.16, f32[96,512]{1,0:T(8,128)S(1)} %copy-done.18, ...), custom_call_target="tpu_custom_call" | custom-call | tf_op jit(solution)/shard_map/pallas_call | solution.py:285
  50.7 9.2 %all_to_all.20.recv_ref = bf16[8,48,128]{2,1,0:T(8,128)(2,1)S(1)} all-to-all(bf16[8,48,128]{2,1,0:T(8,128)(2,1)S(1)} %shard_map.178), channel_id=1, replica_groups=mesh['band'=4,'fft'=8] {'fft'}, dimensions={0} | all-to-all | bytes 196608 | tf_op jit(solution)/shard_map/all_to_all | solution.py:362
  59.9 0.0 copy-done.7
  59.9 0.0 copy-done.27
  59.9 0.0 copy-done.29
  59.9 0.0 copy-done.4
  59.9 0.0 copy-done.5
  59.9 1.1 %shard_map.179 = (bf16[2,64,192]{2,1,0:T(8,128)(2,1)}, bf16[4,2,16,192]{3,2,1,0:T(8,128)(2,1)S(1)}) custom-call(bf16[8,48,128]{2,1,0:T(8,128)(2,1)S(1)} %all_to_all.20.recv_ref, f32[2,64,192]{2,1,0:T(8,128)S(1)} %copy-done.7, s32[1,64]{1,0:T(1,128)S(1)} %bitcast.7, s32[4,128]{1,0:T(4,128)S(1)} %bitcast.5, bf16[384,1024]{1,0:T(8,128)(2,1)S(1)} %copy-done.5, ...), custom_call_target="tpu_custom_call" | custom-call | tf_op jit(solution)/shard_map/pallas_call | solution.py:285
  61.0 10.4 %all_to_all.21.recv_ref = bf16[4,2,16,192]{3,2,1,0:T(8,128)(2,1)S(1)} all-to-all(bf16[4,2,16,192]{3,2,1,0:T(8,128)(2,1)S(1)} %get-tuple-element.15), channel_id=1, replica_groups=mesh['band'=4,'fft'=8] {'band'}, dimensions={0} | all-to-all | bytes 98304 | tf_op jit(solution)/shard_map/all_to_all | solution.py:373
  71.4 0.0 copy-done.3
  71.4 0.0 copy-done.19
  71.4 0.0 copy-done.24
  71.4 0.0 copy-done.8
  71.4 0.0 copy-done.21
  71.5 0.0 copy-done.22
  71.5 2.5 %shard_map.180 = f32[32,2,128]{2,1,0:T(2,128)S(1)} custom-call(bf16[4,2,16,192]{3,2,1,0:T(8,128)(2,1)S(1)} %all_to_all.21.recv_ref, bf16[16,192,512]{2,1,0:T(8,128)(2,1)S(1)} %bitcast.3, bf16[256,256]{1,0:T(8,128)(2,1)S(1)} %copy-done.19, bf16[192,192]{1,0:T(8,128)(2,1)S(1)} %copy-done.21, f32[16,256]{1,0:T(8,128)S(1)} %copy-done.24, ...), custom_call_target="tpu_custom_call" | custom-call | tf_op jit(solution)/shard_map/pallas_call | solution.py:285
  74.0 8.9 %all_to_all.22.recv_ref = f32[32,2,128]{2,1,0:T(2,128)S(1)} all-to-all(f32[32,2,128]{2,1,0:T(2,128)S(1)} %shard_map.180), channel_id=1, replica_groups=mesh['band'=4,'fft'=8] {'band','fft'}, dimensions={0} | all-to-all | bytes 65536 | tf_op jit(solution)/shard_map/all_to_all | solution.py:400
  82.9 0.0 copy-done.20
  82.9 0.0 copy-done.25
  82.9 0.8 shard_map.181
  (7 shorter events, 0.0 us)
Async XLA Ops:
  0.6 0.9 %copy-start.6 = (f32[2,64,192]{2,1,0:T(8,128)S(1)}, f32[2,64,192]{2,1,0:T(8,128)}, u32[]{:S(2)}) copy-start(f32[2,64,192]{2,1,0:T(8,128)} %coeffs_ref.1) | copy-start | bytes 294916
  1.5 1.0 %copy-start.9 = (bf16[768,192]{1,0:T(8,128)(2,1)S(1)}, bf16[768,192]{1,0:T(8,128)(2,1)}, u32[]{:S(2)}) copy-start(bf16[768,192]{1,0:T(8,128)(2,1)} %constant.24.clone.table_hbm) | copy-start | bytes 884740
  2.5 0.7 copy-start.28
  4.7 17.7 %all-to-all-start = ((bf16[8,48,128]{2,1,0:T(8,128)(2,1)}), bf16[8,48,128]{2,1,0:T(8,128)(2,1)S(1)}, u32[]{:S(2)}, u32[]{:S(2)}) async-start(bf16[8,48,128]{2,1,0:T(8,128)(2,1)} %shard_map.176), calls=%async_computation | async-start | bytes 196608 | tf_op jit(solution)/shard_map/all_to_all | solution.py:323
  9.8 2.3 %copy-start = (f32[24,192,192]{2,1,0:T(8,128)S(1)}, f32[24,192,192]{2,1,0:T(8,128)}, u32[]{:S(2)}) copy-start(f32[24,192,192]{2,1,0:T(8,128)} %pot_hbm.1) | copy-start | bytes 10616836
  12.2 1.0 %copy-start.10 = (bf16[3,192,192]{2,1,0:T(8,128)(2,1)S(1)}, bf16[3,192,192]{2,1,0:T(8,128)(2,1)}, u32[]{:S(2)}) copy-start(bf16[3,192,192]{2,1,0:T(8,128)(2,1)} %constant.26.clone.x_hbm) | copy-start | bytes 663556
  13.1 0.8 %copy-start.23 = (bf16[256,96]{1,0:T(8,128)(2,1)S(1)}, bf16[256,96]{1,0:T(8,128)(2,1)}, u32[]{:S(2)}) copy-start(bf16[256,96]{1,0:T(8,128)(2,1)} %constant.25.clone.y_hbm) | copy-start | bytes 147460
  14.0 0.7 copy-start.26
  14.7 45.2 %copy-start.7 = (f32[2,64,192]{2,1,0:T(8,128)S(1)}, f32[2,64,192]{2,1,0:T(8,128)}, u32[]{:S(2)}) copy-start(f32[2,64,192]{2,1,0:T(8,128)} %coeffs_ref.1) | copy-start | bytes 294916
  14.7 45.2 %copy-start.27 = (s32[512]{0:T(512)S(1)}, s32[512]{0:T(512)}, u32[]{:S(2)}) copy-start(s32[512]{0:T(512)} %param.19) | copy-start | bytes 6148
  14.7 45.2 %copy-start.29 = (s32[64]{0:T(128)S(1)}, s32[64]{0:T(128)}, u32[]{:S(2)}) copy-start(s32[64]{0:T(128)} %param.20) | copy-start | bytes 772
  14.7 56.8 %copy-start.3 = (bf16[512,16,192]{0,2,1:T(8,128)(2,1)S(1)}, bf16[512,16,192]{0,2,1:T(8,128)(2,1)}, u32[]{:S(2)}) copy-start(bf16[512,16,192]{0,2,1:T(8,128)(2,1)} %param.21) | copy-start | bytes 9437188
  14.7 56.7 %copy-start.19 = (bf16[256,256]{1,0:T(8,128)(2,1)S(1)}, bf16[256,256]{1,0:T(8,128)(2,1)}, u32[]{:S(2)}) copy-start(bf16[256,256]{1,0:T(8,128)(2,1)} %constant.29.clone.order_ref) | copy-start | bytes 393220
  14.7 56.7 %copy-start.24 = (f32[16,256]{1,0:T(8,128)S(1)}, f32[16,256]{1,0:T(8,128)}, u32[]{:S(2)}) copy-start(f32[16,256]{1,0:T(8,128)} %constant.31.clone.repeat_ref) | copy-start | bytes 49156
  17.3 2.1 %copy-start.1 = (f32[24,192,256]{2,1,0:T(8,128)}, f32[24,192,256]{2,1,0:T(8,128)S(1)}, u32[]{:S(2)}) copy-start(f32[24,192,256]{2,1,0:T(8,128)S(1)} %get-tuple-element.9.pot_ref) | copy-start | bytes 14155780
  19.5 0.7 copy-start.11
  20.2 0.7 copy-start.13
  20.9 0.7 copy-start.15
  21.6 0.7 copy-start.17
  22.3 2.3 %copy-start.2 = (f32[24,192,256]{2,1,0:T(8,128)S(1)}, f32[24,192,256]{2,1,0:T(8,128)}, u32[]{:S(2)}) copy-start(f32[24,192,256]{2,1,0:T(8,128)} %copy-done.1) | copy-start | bytes 14155780
  24.7 1.0 %copy-start.12 = (bf16[3,192,192]{2,1,0:T(8,128)(2,1)S(1)}, bf16[3,192,192]{2,1,0:T(8,128)(2,1)}, u32[]{:S(2)}) copy-start(bf16[3,192,192]{2,1,0:T(8,128)(2,1)} %copy-done.11) | copy-start | bytes 663556
  25.6 0.9 %copy-start.14 = (bf16[256,512]{1,0:T(8,128)(2,1)S(1)}, bf16[256,512]{1,0:T(8,128)(2,1)}, u32[]{:S(2)}) copy-start(bf16[256,512]{1,0:T(8,128)(2,1)} %copy-done.13) | copy-start | bytes 786436
  26.6 0.9 %copy-start.16 = (bf16[512,256]{1,0:T(8,128)(2,1)S(1)}, bf16[512,256]{1,0:T(8,128)(2,1)}, u32[]{:S(2)}) copy-start(bf16[512,256]{1,0:T(8,128)(2,1)} %copy-done.15) | copy-start | bytes 786436
  27.5 0.9 %copy-start.18 = (f32[96,512]{1,0:T(8,128)S(1)}, f32[96,512]{1,0:T(8,128)}, u32[]{:S(2)}) copy-start(f32[96,512]{1,0:T(8,128)} %copy-done.17) | copy-start | bytes 589828
  28.5 31.4 %copy-start.4 = (bf16[384,1024]{1,0:T(8,128)(2,1)S(1)}, bf16[384,1024]{1,0:T(8,128)(2,1)}, u32[]{:S(2)}) copy-start(bf16[384,1024]{1,0:T(8,128)(2,1)} %constant.28.clone.low_ref) | copy-start | bytes 2359300
  28.5 31.4 %copy-start.5 = (bf16[384,1024]{1,0:T(8,128)(2,1)S(1)}, bf16[384,1024]{1,0:T(8,128)(2,1)}, u32[]{:S(2)}) copy-start(bf16[384,1024]{1,0:T(8,128)(2,1)} %constant.27.clone.high_ref) | copy-start | bytes 2359300
  28.5 43.0 %copy-start.8 = (f32[512,256]{1,0:T(8,128)S(1)}, f32[512,256]{1,0:T(8,128)}, u32[]{:S(2)}) copy-start(f32[512,256]{1,0:T(8,128)} %constant.32.clone.keep_ref) | copy-start | bytes 1572868
  28.5 43.0 %copy-start.21 = (bf16[192,192]{1,0:T(8,128)(2,1)S(1)}, bf16[192,192]{1,0:T(8,128)(2,1)}, u32[]{:S(2)}) copy-start(bf16[192,192]{1,0:T(8,128)(2,1)} %constant.30.clone.swap_ref) | copy-start | bytes 221188
  28.5 43.0 %copy-start.22 = (f32[32,512]{1,0:T(8,128)S(1)}, f32[32,512]{1,0:T(8,128)}, u32[]{:S(2)}) copy-start(f32[32,512]{1,0:T(8,128)} %constant.33.clone.fold_ref) | copy-start | bytes 196612
  28.5 54.4 %copy-start.20 = (f32[256,16]{1,0:T(8,128)S(1)}, f32[256,16]{1,0:T(8,128)}, u32[]{:S(2)}) copy-start(f32[256,16]{1,0:T(8,128)} %constant.35.clone.fold_ref) | copy-start | bytes 49156
  28.5 54.4 %copy-start.25 = (f32[16,256]{1,0:T(8,128)S(1)}, f32[16,256]{1,0:T(8,128)}, u32[]{:S(2)}) copy-start(f32[16,256]{1,0:T(8,128)} %constant.34.clone.keep_ref) | copy-start | bytes 49156

commit v3 on v2

--- a/solution.py
+++ b/solution.py
@@ -12,8 +12,10 @@
 F32 = jnp.float32
 BF16 = jnp.bfloat16
 LANES = 128
-GROUP = 4
-VMEM_BYTES = 40 * 2**20
+GROUP = 8
+ALL_VMEM = 62 * 2**20
+MOST_VMEM = 57 * 2**20
+SOME_VMEM = 16 * 2**20
 
 
 def dot(a, b, dims=((1,), (0,)), precision=None):
@@ -125,20 +127,12 @@
         out_ref[part] = jnp.concatenate(rows, 0).astype(BF16)
 
 
-def tables_kernel(
-    column_hbm, y_hbm, x_hbm, pot_hbm, back_ref, forward_ref, mask_ref, x_ref, pot_ref, column_ref, y_ref, raw_ref, sem
-):
-    planes, grid, _ = raw_ref.shape
-    small = start_all(
+def tables_kernel(column_hbm, y_hbm, back_ref, forward_ref, mask_ref, column_ref, y_ref, sem):
+    copies = start_all(
         pltpu.make_async_copy(column_hbm, column_ref, sem.at[0]),
         pltpu.make_async_copy(y_hbm, y_ref, sem.at[1]),
-        pltpu.make_async_copy(x_hbm, x_ref, sem.at[2]),
-    )
-    group = [pl.ds(i, GROUP) for i in range(0, planes, GROUP)]
-    large = start_all(*[
-        pltpu.make_async_copy(pot_hbm.at[at], raw_ref.at[at], sem.at[3 + i]) for i, at in enumerate(group)
-    ])
-    for copy in small:
+    )
+    for copy in copies:
         copy.wait()
     half = y_ref.shape[1]
     for row in range(column_ref.shape[0]):
@@ -151,27 +145,37 @@
         back_ref[:, at] = back.astype(BF16)
         forward_ref[at, :] = back.T.astype(BF16)
         mask_ref[:, at] = jnp.where(index == x_pos, 1.0, 0.0)
-    lane = lane_iota((grid, LANES))
-    low_at = jnp.clip(grid - LANES - lane, 0, LANES - 1)
-    high_at = jnp.clip(grid - lane, 0, LANES - 1)
-    for i, copy in enumerate(large):
-        copy.wait()
-        for z in range(i * GROUP, (i + 1) * GROUP):
-            near = raw_ref[z, :, :LANES]
-            far = raw_ref[z, :, LANES:]
-            far = jnp.concatenate([far, jnp.zeros((grid, 2 * LANES - grid), F32)], 1)
-            pot_ref[z, :, :LANES] = jnp.where(lane <= grid // 2, near, 0.0)
-            from_far = jnp.take_along_axis(far, low_at, axis=1)
-            from_near = jnp.take_along_axis(near, high_at, axis=1)
-            mirrored = jnp.where(lane <= grid - LANES, from_far, from_near)
-            pot_ref[z, :, LANES:] = jnp.where((lane > 0) & (lane < grid // 2), mirrored, 0.0)
-
-
-def planes_kernel(recv_ref, pot_ref, back_ref, forward_ref, mask_ref, x_ref, out_ref, value_ref, sums_ref):
+
+
+def planes_kernel(
+    recv_hbm, back_hbm, forward_hbm, mask_hbm, x_hbm, pot_hbm, out_ref,
+    recv_ref, back_ref, forward_ref, mask_ref, x_ref, pot_ref, value_ref, sums_ref, y_buf, p_buf, q_buf, sem,
+):
     parts, rows, _ = recv_ref.shape
-    planes = pot_ref.shape[0]
+    planes, grid, _ = pot_ref.shape
     half = mask_ref.shape[0]
     bands = rows // planes
+    group = y_buf.shape[0] // bands
+    steps = planes // group
+    small = start_all(*[
+        pltpu.make_async_copy(source, target, sem.at[i])
+        for i, (source, target) in enumerate([
+            (recv_hbm, recv_ref),
+            (mask_hbm, mask_ref),
+            (forward_hbm, forward_ref),
+            (x_hbm, x_ref),
+            (back_hbm, back_ref),
+        ])
+    ])
+
+    def pot_copy(step):
+        at = pl.ds(step * group, group)
+        return pltpu.make_async_copy(pot_hbm.at[at], pot_ref.at[at], sem.at[len(small) + step])
+
+    for step in range(steps):
+        pot_copy(step).start()
+    for copy in small:
+        copy.wait()
     first = lane_iota((rows, LANES)) < LANES // 2
 
     def halves(even, odd):
@@ -185,43 +189,66 @@
             recv_ref[2 * pair].astype(F32), recv_ref[2 * pair + 1].astype(F32)
         )
 
-    def one_plane(z):
+    lane = lane_iota((grid, LANES))
+    low_at = jnp.clip(grid - LANES - lane, 0, LANES - 1)
+    high_at = jnp.clip(grid - lane, 0, LANES - 1)
+
+    def mirrored_potential(z):
+        near = pot_ref[z, :, :LANES]
+        far = pot_ref[z, :, LANES:]
+        far = jnp.concatenate([far, jnp.zeros((grid, 2 * LANES - grid), F32)], 1)
+        from_far = jnp.take_along_axis(far, low_at, axis=1)
+        from_near = jnp.take_along_axis(near, high_at, axis=1)
+        back = jnp.where(lane <= grid - LANES, from_far, from_near)
+        back = jnp.where((lane > 0) & (lane < grid // 2), back, 0.0)
+        return jnp.concatenate([jnp.where(lane <= grid // 2, near, 0.0), back], 1)
+
+    def body(step, carry):
         mask = mask_ref[...].astype(BF16)
-        placed = []
-        for b in range(bands):
-            for c in range(2):
-                placed.append(mask * value_ref[c, pl.ds(b * planes + z, 1), :].astype(BF16))
-        spread = dot(jnp.concatenate(placed, 0), forward_ref[...])
-        pot = pot_ref[z]
-        folded = []
-        for b in range(bands):
-            at = 2 * b * half
-            real, imag = spread[at : at + half], spread[at + half : at + 2 * half]
-            rc, rs, ic, si = real[:, :LANES], real[:, LANES:], imag[:, :LANES], imag[:, LANES:]
-            y_re = jnp.concatenate([rc - si, rc + si], 1).astype(BF16)
-            y_im = jnp.concatenate([ic + rs, ic - rs], 1).astype(BF16)
-            p_re = dot(x_ref[0], jnp.concatenate([y_re, y_im], 0)) * pot
-            p_im = dot(x_ref[1], jnp.concatenate([y_im, y_re], 0)) * pot
-            s_re = dot(x_ref[2], p_re.astype(BF16))
-            s_im = dot(x_ref[2], p_im.astype(BF16))
+        for p in range(group):
+            z = step * group + p
+            placed = []
+            for b in range(bands):
+                for c in range(2):
+                    placed.append(mask * value_ref[c, pl.ds(b * planes + z, 1), :].astype(BF16))
+            spread = dot(jnp.concatenate(placed, 0), forward_ref[...])
+            for b in range(bands):
+                at = 2 * b * half
+                real, imag = spread[at : at + half], spread[at + half : at + 2 * half]
+                rc, rs, ic, si = real[:, :LANES], real[:, LANES:], imag[:, :LANES], imag[:, LANES:]
+                y_re = jnp.concatenate([rc - si, rc + si], 1).astype(BF16)
+                y_im = jnp.concatenate([ic + rs, ic - rs], 1).astype(BF16)
+                i = p * bands + b
+                y_buf[i, 0, :half] = y_re
+                y_buf[i, 0, half:] = y_im
+                y_buf[i, 1, :half] = y_im
+                y_buf[i, 1, half:] = y_re
+        pot_copy(step).wait()
+        for p in range(group):
+            weight = mirrored_potential(step * group + p)
+            for b in range(bands):
+                for c in range(2):
+                    i = p * bands + b
+                    p_buf[i, c] = (dot(x_ref[c], y_buf[i, c]) * weight).astype(BF16)
+        for i in range(group * bands):
+            s_re = dot(x_ref[2], p_buf[i, 0])
+            s_im = dot(x_ref[2], p_buf[i, 1])
             q_re = s_re[:half] + s_im[half:]
             q_im = s_im[:half] - s_re[half:]
             rp, rm, ip, im = q_re[:, :LANES], q_re[:, LANES:], q_im[:, :LANES], q_im[:, LANES:]
-            folded.append(jnp.concatenate([rp + rm, ip - im], 1).astype(BF16))
-            folded.append(jnp.concatenate([ip + im, rm - rp], 1).astype(BF16))
-        full = dot(jnp.concatenate(folded, 0), back_ref[...])
-        for b in range(bands):
-            for c in range(2):
-                at = (2 * b + c) * half
-                kept = jnp.sum(full[at : at + half] * mask_ref[...], axis=0, keepdims=True)
-                sums_ref[c, pl.ds(z * bands + b, 1), :] = kept
-
-    def body(step, carry):
-        for p in range(GROUP):
-            one_plane(step * GROUP + p)
+            q_buf[i, :half] = jnp.concatenate([rp + rm, ip - im], 1).astype(BF16)
+            q_buf[i, half:] = jnp.concatenate([ip + im, rm - rp], 1).astype(BF16)
+        for p in range(group):
+            folded = q_buf[p * bands : (p + 1) * bands].reshape(bands * 2 * half, 2 * LANES)
+            full = dot(folded, back_ref[...])
+            for b in range(bands):
+                for c in range(2):
+                    at = (2 * b + c) * half
+                    kept = jnp.sum(full[at : at + half] * mask_ref[...], axis=0, keepdims=True)
+                    sums_ref[c, pl.ds((step * group + p) * bands + b, 1), :] = kept
         return carry
 
-    lax.fori_loop(0, planes // GROUP, body, 0)
+    lax.fori_loop(0, steps, body, 0)
     for pair in range(parts // 2):
         at = slice(pair * LANES, (pair + 1) * LANES)
         even, odd = halves(sums_ref[0, :, at], sums_ref[1, :, at])
@@ -281,11 +308,11 @@
     out_ref[...] = dot(spread, fold_ref[...], precision=lax.Precision.HIGHEST)
 
 
-def call(kernel, out_shape, *operands, **options):
+def call(kernel, out_shape, *operands, vmem=SOME_VMEM, **options):
     return pl.pallas_call(
         kernel,
         out_shape=out_shape,
-        compiler_params=pltpu.CompilerParams(vmem_limit_bytes=VMEM_BYTES),
+        compiler_params=pltpu.CompilerParams(vmem_limit_bytes=vmem),
         **options,
     )(*operands)
 
@@ -312,6 +339,7 @@
         band_coeffs,
         lengths,
         z_table,
+        vmem=ALL_VMEM,
         in_specs=[in_hbm] * 3,
         scratch_shapes=[
             pltpu.VMEM(band_coeffs.shape, F32),
@@ -324,39 +352,49 @@
 
     wide = 2 * LANES
     table_y, table_x = y_table(grid, half), x_tables(grid, half)
-    back, forward, mask, table_x, weights = call(
+    tables = (
+        shape((wide, all_sticks), BF16),
+        shape((all_sticks, wide), BF16),
+        shape((half, all_sticks), F32),
+    )
+    back, forward, mask = call(
         tables_kernel,
-        (
-            shape((wide, all_sticks), BF16),
-            shape((all_sticks, wide), BF16),
-            shape((half, all_sticks), F32),
-            shape(table_x.shape, BF16),
-            shape((planes, grid, wide), F32),
-        ),
+        tables,
         columns,
         table_y,
-        table_x,
-        potential,
-        in_specs=[in_hbm] * 4,
+        vmem=ALL_VMEM,
+        in_specs=[in_hbm] * 2,
         scratch_shapes=[
             pltpu.VMEM(columns.shape, jnp.int32),
             pltpu.VMEM(table_y.shape, BF16),
-            pltpu.VMEM(potential.shape, F32),
-            dma((3 + planes // GROUP,)),
+            dma((2,)),
         ],
     )
+    group = math.gcd(GROUP, planes)
+    values = pltpu.VMEM((2, bands * planes, all_sticks), F32)
+    pairs = group * bands
     sent = call(
         planes_kernel,
         exchanged,
         received,
-        weights,
         back,
         forward,
         mask,
         table_x,
+        potential,
+        vmem=MOST_VMEM,
+        in_specs=[in_hbm] * 6,
         scratch_shapes=[
-            pltpu.VMEM((2, bands * planes, all_sticks), F32),
-            pltpu.VMEM((2, bands * planes, all_sticks), F32),
+            pltpu.VMEM(exchanged.shape, BF16),
+            *(pltpu.VMEM(t.shape, t.dtype) for t in tables),
+            pltpu.VMEM(table_x.shape, BF16),
+            pltpu.VMEM(potential.shape, F32),
+            values,
+            values,
+            pltpu.VMEM((pairs, 2, 2 * half, wide), BF16),
+            pltpu.VMEM((pairs, 2, grid, wide), BF16),
+            pltpu.VMEM((pairs, 2 * half, wide), BF16),
+            dma((5 + planes // group,)),
         ],
     )
     received = lax.all_to_all(sent, "fft", 0, 0, tiled=True)

time: 84.4 us -> 60 us (0.71)
  local copies, waits for them, and re-layouts: 18.5 us -> 0.07 us
  Pallas kernels: 30.7 us -> 22.3 us
  waiting for transfers between devices: 0.01 us -> 3.32 us
    unnamed x60 -> x26, local copies, waits for them, and re-layouts: 18.5 us -> 0.07 us
    pallas_call x6, Pallas kernels: 30.7 us -> 22.3 us  [call(): pl.pallas_call(kernel, out_shape=out_shape, compiler_params=pltpu.Compile...]
    all_to_all x1, waiting for transfers between devices: 0.01 us -> 3.32 us  [per_device(): received = lax.all_to_all(sent, 'fft', 0, 0, tiled=True)]
  transfers between devices with their start and end apart: 1 -> 1, of which waited for: 0 -> 1; matrix products, arithmetic and copies ran while one was open for 0% -> 0% of each run, Pallas kernels for 3% -> 3%
where the time goes in v3:
time: 60 us; the launch traced here: 59.6 us
  blocking collectives  28 us (47%)
  Pallas kernels  22.3 us (37%)
  starting transfers between devices  5.18 us (9%)
  waiting for transfers between devices  3.32 us (6%)
  between operations  0.79 us (1%)
    pallas_call x6, Pallas kernels, call(): pl.pallas_call(kernel, out_shape=out_shape, compiler_params=pltpu.Compile...  22.3 us
    all_to_all x1, blocking collectives, per_device(): received = lax.all_to_all(sent, 'band', 0, 0, tiled=True)  10.5 us
    all_to_all x1, blocking collectives, per_device(): received = lax.all_to_all(sent, ('band', 'fft'), 0, 0, tiled=True)  8.95 us
    all_to_all x1, blocking collectives, per_device(): received = lax.all_to_all(sent, 'fft', 0, 0, tiled=True)  8.47 us
    all_to_all x1, starting transfers between devices, per_device(): received = lax.all_to_all(sent, 'fft', 0, 0, tiled=True)  5.18 us
    all_to_all x1, waiting for transfers between devices, per_device(): received = lax.all_to_all(sent, 'fft', 0, 0, tiled=True)  3.32 us
  transfers between devices with their start and end apart: 1, of which 1 were waited for; matrix products, arithmetic and copies ran while one was open for 0% of the time, Pallas kernels for 3%

profile of v3, /device:TPU:0, one launch (start us, length us, event | category | flops | bytes accessed | tf_op | source)
XLA Modules:
  0.0 59.6 jit_solution(15407434466984676651)
XLA Ops:
  0.6 0.0 copy-start.9
  0.6 0.0 copy-start.7
  0.7 0.0 copy-start.5
  0.7 0.0 copy-start.3
  0.7 0.0 copy-start.12
  0.7 0.0 copy-start.11
  0.7 2.3 %shard_map.176 = bf16[8,48,128]{2,1,0:T(8,128)(2,1)} custom-call(f32[2,64,192]{2,1,0:T(8,128)} %coeffs_ref.1, s32[1,64]{1,0:T(1,128)} %bitcast.6, bf16[768,192]{1,0:T(8,128)(2,1)} %constant.24.clone.table_hbm), custom_call_target="tpu_custom_call" | custom-call | tf_op jit(solution)/shard_map/pallas_call | solution.py:312
  3.0 5.2 %all-to-all-start = ((bf16[8,48,128]{2,1,0:T(8,128)(2,1)}), bf16[8,48,128]{2,1,0:T(8,128)(2,1)}, u32[]{:S(2)}, u32[]{:S(2)}) async-start(bf16[8,48,128]{2,1,0:T(8,128)(2,1)} %shard_map.176), calls=%async_computation | async-start | bytes 196608 | tf_op jit(solution)/shard_map/all_to_all | solution.py:351
  8.2 2.0 %shard_map.177 = (bf16[256,512]{1,0:T(8,128)(2,1)}, bf16[512,256]{1,0:T(8,128)(2,1)}, f32[96,512]{1,0:T(8,128)}) custom-call(s32[4,128]{1,0:T(4,128)} %bitcast.4, bf16[256,96]{1,0:T(8,128)(2,1)} %constant.25.clone.y_hbm), custom_call_target="tpu_custom_call" | custom-call | tf_op jit(solution)/shard_map/pallas_call | solution.py:312
  10.2 0.0 copy-start
  10.2 3.3 %all-to-all-done.recv_hbm = bf16[8,48,128]{2,1,0:T(8,128)(2,1)} async-done(((bf16[8,48,128]{2,1,0:T(8,128)(2,1)}), bf16[8,48,128]{2,1,0:T(8,128)(2,1)}, u32[]{:S(2)}, u32[]{:S(2)}) %all-to-all-start) | async-done | bytes 98336 | tf_op jit(solution)/shard_map/all_to_all | solution.py:351
  13.5 0.0 copy-start.1
  13.5 0.0 copy-start.2
  13.5 0.0 copy-start.4
  13.5 0.0 copy-start.8
  13.5 0.0 copy-start.6
  13.5 0.0 copy-start.10
  13.5 13.6 %shard_map.178 = bf16[8,48,128]{2,1,0:T(8,128)(2,1)} custom-call(bf16[8,48,128]{2,1,0:T(8,128)(2,1)} %all-to-all-done.recv_hbm, bf16[256,512]{1,0:T(8,128)(2,1)} %get-tuple-element.7.back_hbm, bf16[512,256]{1,0:T(8,128)(2,1)} %get-tuple-element.8.forward_hbm, f32[96,512]{1,0:T(8,128)} %get-tuple-element.9.mask_hbm, ...), custom_call_target="tpu_custom_call" | custom-call | tf_op jit(solution)/shard_map/pallas_call | solution.py:312
  27.1 8.5 %all_to_all.20.recv_ref = bf16[8,48,128]{2,1,0:T(8,128)(2,1)S(1)} all-to-all(bf16[8,48,128]{2,1,0:T(8,128)(2,1)} %shard_map.178), channel_id=1, replica_groups=mesh['band'=4,'fft'=8] {'fft'}, dimensions={0} | all-to-all | bytes 196608 | tf_op jit(solution)/shard_map/all_to_all | solution.py:400
  35.6 0.0 copy-done.3
  35.6 0.0 copy-done.12
  35.6 0.0 copy-done.11
  35.6 0.0 copy-done.1
  35.6 0.0 copy-done.2
  35.6 1.1 %shard_map.179 = (bf16[2,64,192]{2,1,0:T(8,128)(2,1)}, bf16[4,2,16,192]{3,2,1,0:T(8,128)(2,1)S(1)}) custom-call(bf16[8,48,128]{2,1,0:T(8,128)(2,1)S(1)} %all_to_all.20.recv_ref, f32[2,64,192]{2,1,0:T(8,128)S(1)} %copy-done.3, s32[1,64]{1,0:T(1,128)S(1)} %bitcast.7, s32[4,128]{1,0:T(4,128)S(1)} %bitcast.5, bf16[384,1024]{1,0:T(8,128)(2,1)S(1)} %copy-done.2, ...), custom_call_target="tpu_custom_call" | custom-call | tf_op jit(solution)/shard_map/pallas_call | solution.py:312
  36.7 10.5 %all_to_all.21.recv_ref = bf16[4,2,16,192]{3,2,1,0:T(8,128)(2,1)S(1)} all-to-all(bf16[4,2,16,192]{3,2,1,0:T(8,128)(2,1)S(1)} %get-tuple-element.11), channel_id=1, replica_groups=mesh['band'=4,'fft'=8] {'band'}, dimensions={0} | all-to-all | bytes 98304 | tf_op jit(solution)/shard_map/all_to_all | solution.py:411
  47.3 0.0 copy-done.9
  47.3 0.0 copy-done.7
  47.3 0.0 copy-done.5
  47.3 0.0 copy-done
  47.3 0.0 copy-done.4
  47.3 0.0 copy-done.8
  47.3 2.5 %shard_map.180 = f32[32,2,128]{2,1,0:T(2,128)S(1)} custom-call(bf16[4,2,16,192]{3,2,1,0:T(8,128)(2,1)S(1)} %all_to_all.21.recv_ref, bf16[16,192,512]{2,1,0:T(8,128)(2,1)S(1)} %bitcast.3, bf16[256,256]{1,0:T(8,128)(2,1)S(1)} %copy-done.5, bf16[192,192]{1,0:T(8,128)(2,1)S(1)} %copy-done.7, f32[16,256]{1,0:T(8,128)S(1)} %copy-done.9, f32[512,256]{1,0:T(8,128)S(1)} %copy-done.4, ...), custom_call_target="tpu_custom_call" | custom-call | tf_op jit(solution)/shard_map/pallas_call | solution.py:312
  49.8 8.9 %all_to_all.22.recv_ref = f32[32,2,128]{2,1,0:T(2,128)S(1)} all-to-all(f32[32,2,128]{2,1,0:T(2,128)S(1)} %shard_map.180), channel_id=1, replica_groups=mesh['band'=4,'fft'=8] {'band','fft'}, dimensions={0} | all-to-all | bytes 65536 | tf_op jit(solution)/shard_map/all_to_all | solution.py:438
  58.7 0.0 copy-done.6
  58.8 0.0 copy-done.10
  58.8 0.8 %shard_map.181 = f32[16,16]{1,0:T(8,128)} custom-call(f32[32,2,128]{2,1,0:T(2,128)S(1)} %all_to_all.22.recv_ref, f32[16,256]{1,0:T(8,128)S(1)} %copy-done.10, f32[256,16]{1,0:T(8,128)S(1)} %copy-done.6), custom_call_target="tpu_custom_call" | custom-call | tf_op jit(solution)/shard_map/pallas_call | solution.py:312
Async XLA Ops:
  0.6 46.6 %copy-start.9 = (f32[16,256]{1,0:T(8,128)S(1)}, f32[16,256]{1,0:T(8,128)}, u32[]{:S(2)}) copy-start(f32[16,256]{1,0:T(8,128)} %constant.31.clone.repeat_ref) | copy-start | bytes 49156
  0.6 46.6 %copy-start.7 = (bf16[192,192]{1,0:T(8,128)(2,1)S(1)}, bf16[192,192]{1,0:T(8,128)(2,1)}, u32[]{:S(2)}) copy-start(bf16[192,192]{1,0:T(8,128)(2,1)} %constant.30.clone.swap_ref) | copy-start | bytes 221188
  0.7 46.6 %copy-start.5 = (bf16[256,256]{1,0:T(8,128)(2,1)S(1)}, bf16[256,256]{1,0:T(8,128)(2,1)}, u32[]{:S(2)}) copy-start(bf16[256,256]{1,0:T(8,128)(2,1)} %constant.29.clone.order_ref) | copy-start | bytes 393220
  0.7 34.9 %copy-start.3 = (f32[2,64,192]{2,1,0:T(8,128)S(1)}, f32[2,64,192]{2,1,0:T(8,128)}, u32[]{:S(2)}) copy-start(f32[2,64,192]{2,1,0:T(8,128)} %coeffs_ref.1) | copy-start | bytes 294916
  0.7 34.9 %copy-start.12 = (s32[64]{0:T(128)S(1)}, s32[64]{0:T(128)}, u32[]{:S(2)}) copy-start(s32[64]{0:T(128)} %param.20) | copy-start | bytes 772
  0.7 34.9 %copy-start.11 = (s32[512]{0:T(512)S(1)}, s32[512]{0:T(512)}, u32[]{:S(2)}) copy-start(s32[512]{0:T(512)} %param.19) | copy-start | bytes 6148
  3.0 10.5 %all-to-all-start = ((bf16[8,48,128]{2,1,0:T(8,128)(2,1)}), bf16[8,48,128]{2,1,0:T(8,128)(2,1)}, u32[]{:S(2)}, u32[]{:S(2)}) async-start(bf16[8,48,128]{2,1,0:T(8,128)(2,1)} %shard_map.176), calls=%async_computation | async-start | bytes 196608 | tf_op jit(solution)/shard_map/all_to_all | solution.py:351
  10.2 37.1 %copy-start = (bf16[512,16,192]{0,2,1:T(8,128)(2,1)S(1)}, bf16[512,16,192]{0,2,1:T(8,128)(2,1)}, u32[]{:S(2)}) copy-start(bf16[512,16,192]{0,2,1:T(8,128)(2,1)} %param.21) | copy-start | bytes 9437188
  13.5 22.1 %copy-start.1 = (bf16[384,1024]{1,0:T(8,128)(2,1)S(1)}, bf16[384,1024]{1,0:T(8,128)(2,1)}, u32[]{:S(2)}) copy-start(bf16[384,1024]{1,0:T(8,128)(2,1)} %constant.28.clone.low_ref) | copy-start | bytes 2359300
  13.5 22.1 %copy-start.2 = (bf16[384,1024]{1,0:T(8,128)(2,1)S(1)}, bf16[384,1024]{1,0:T(8,128)(2,1)}, u32[]{:S(2)}) copy-start(bf16[384,1024]{1,0:T(8,128)(2,1)} %constant.27.clone.high_ref) | copy-start | bytes 2359300
  13.5 33.8 %copy-start.4 = (f32[512,256]{1,0:T(8,128)S(1)}, f32[512,256]{1,0:T(8,128)}, u32[]{:S(2)}) copy-start(f32[512,256]{1,0:T(8,128)} %constant.32.clone.keep_ref) | copy-start | bytes 1572868
  13.5 33.8 %copy-start.8 = (f32[32,512]{1,0:T(8,128)S(1)}, f32[32,512]{1,0:T(8,128)}, u32[]{:S(2)}) copy-start(f32[32,512]{1,0:T(8,128)} %constant.33.clone.fold_ref) | copy-start | bytes 196612
  13.5 45.3 %copy-start.6 = (f32[256,16]{1,0:T(8,128)S(1)}, f32[256,16]{1,0:T(8,128)}, u32[]{:S(2)}) copy-start(f32[256,16]{1,0:T(8,128)} %constant.35.clone.fold_ref) | copy-start | bytes 49156
  13.5 45.2 %copy-start.10 = (f32[16,256]{1,0:T(8,128)S(1)}, f32[16,256]{1,0:T(8,128)}, u32[]{:S(2)}) copy-start(f32[16,256]{1,0:T(8,128)} %constant.34.clone.keep_ref) | copy-start | bytes 49156

commit v4 on v3

--- a/solution.py
+++ b/solution.py
@@ -12,7 +12,8 @@
 F32 = jnp.float32
 BF16 = jnp.bfloat16
 LANES = 128
-GROUP = 8
+GROUP = 12
+BLOCK = 16
 ALL_VMEM = 62 * 2**20
 MOST_VMEM = 57 * 2**20
 SOME_VMEM = 16 * 2**20
@@ -57,12 +58,10 @@
     return table.reshape(2 * LANES, half).astype(BF16)
 
 
-def x_tables(grid, half):
+def x_table(grid, half):
     theta = angles(grid, half)
     cosine, sine = np.cos(theta), np.sin(theta)
-    real = np.concatenate([cosine, -sine], 1)
-    imag = np.concatenate([cosine, sine], 1)
-    return np.stack([real, imag, imag.T]).astype(BF16)
+    return np.block([[cosine, -sine], [sine, cosine]]).astype(BF16)
 
 
 def lane_iota(shape):
@@ -73,10 +72,10 @@
     return lax.broadcasted_iota(jnp.int32, shape, len(shape) - 2)
 
 
-def to_column(row):
-    n = row.shape[1]
-    square = jnp.broadcast_to(row, (n, n))
-    return jnp.sum(jnp.where(lane_iota((n, n)) == row_iota((n, n)), square, 0.0), axis=1, keepdims=True)
+def to_column(row, count):
+    shape = (count, row.shape[1])
+    square = jnp.broadcast_to(row, shape)
+    return jnp.sum(jnp.where(lane_iota(shape) == row_iota(shape), square, 0.0), axis=1, keepdims=True)
 
 
 def slot_freq(shape, half):
@@ -85,7 +84,7 @@
 
 
 def live_slots(length_row, half):
-    length = to_column(length_row.astype(F32))
+    length = to_column(length_row.astype(F32), length_row.shape[1])
     below = jnp.floor(length * 0.5)
     freq = slot_freq((length.shape[0], 2 * half), half)
     return (freq >= -below) & (freq < length - below)
@@ -103,18 +102,19 @@
         pltpu.make_async_copy(coeffs_hbm, coeffs_ref, sem.at[1]),
         pltpu.make_async_copy(table_hbm, table_ref, sem.at[2]),
     )
-    for copy in copies:
-        copy.wait()
     bands, sticks, width = coeffs_ref.shape
     grid = table_ref.shape[0] // 4
     parts = out_ref.shape[0]
     depth = grid // parts
-    high, low = table_ref[: 2 * grid], table_ref[2 * grid :]
+    copies[0].wait()
     live = live_slots(length_ref[...], width // 2)
+    copies[1].wait()
     masked = jnp.concatenate([jnp.where(live, coeffs_ref[b], 0.0) for b in range(bands)], 0)
     c_high = masked.astype(BF16)
     c_low = (masked - c_high.astype(F32)).astype(BF16)
     nt = ((1,), (1,))
+    copies[2].wait()
+    high, low = table_ref[: 2 * grid], table_ref[2 * grid :]
     sums = dot(high, c_high, nt) + dot(high, c_low, nt) + dot(low, c_high, nt)
     real, imag = sums[:grid], sums[grid:]
     first = lane_iota(real.shape) < sticks
@@ -127,55 +127,65 @@
         out_ref[part] = jnp.concatenate(rows, 0).astype(BF16)
 
 
-def tables_kernel(column_hbm, y_hbm, back_ref, forward_ref, mask_ref, column_ref, y_ref, sem):
+def tables_kernel(column_hbm, y_hbm, sort_ref, back_ref, forward_ref, mask_ref, column_ref, y_ref, sem):
     copies = start_all(
         pltpu.make_async_copy(column_hbm, column_ref, sem.at[0]),
         pltpu.make_async_copy(y_hbm, y_ref, sem.at[1]),
     )
-    for copy in copies:
-        copy.wait()
     half = y_ref.shape[1]
-    for row in range(column_ref.shape[0]):
-        column = column_ref[pl.ds(row, 1), :].astype(F32)
-        x_pos = jnp.floor((column + 0.5) * (1.0 / half))
-        y_pos = column - x_pos * half
-        at = pl.ds(row * LANES, LANES)
-        index = row_iota((half, LANES)).astype(F32)
-        back = dot(y_ref[...], jnp.where(index == y_pos, 1.0, 0.0).astype(BF16))
-        back_ref[:, at] = back.astype(BF16)
-        forward_ref[at, :] = back.T.astype(BF16)
-        mask_ref[:, at] = jnp.where(index == x_pos, 1.0, 0.0)
+    tiles, blocks, block, wide = mask_ref.shape
+    n = tiles * wide
+    copies[0].wait()
+    column = column_ref[...].astype(F32)
+    column = jnp.concatenate([column[i : i + 1] for i in range(column.shape[0])], 1)
+    x_pos = jnp.floor((column + 0.5) * (1.0 / half))
+    y_pos = column - x_pos * half
+    key = x_pos * n + lane_iota(column.shape).astype(F32)
+    rank = jnp.sum(jnp.where(to_column(key, n) < key, 1.0, 0.0), axis=0, keepdims=True)
+    sort = jnp.where(row_iota((n, n)).astype(F32) == rank, 1.0, 0.0).astype(BF16)
+    sort_ref[...] = sort
+    nt = ((1,), (1,))
+    index = row_iota((half, n)).astype(F32)
+    at_x = jnp.where(index == x_pos, 1.0, 0.0).astype(BF16)
+    at_y = jnp.where(index == y_pos, 1.0, 0.0).astype(BF16)
+    mask = dot(at_x, sort, nt)
+    at_y = dot(at_y, sort, nt).astype(BF16)
+    copies[1].wait()
+    back = dot(y_ref[...], at_y)
+    for tile in range(tiles):
+        at = slice(tile * wide, (tile + 1) * wide)
+        back_ref[tile] = back[:, at].astype(BF16)
+        forward_ref[tile] = back[:, at].T.astype(BF16)
+        for g in range(blocks):
+            mask_ref[tile, g] = mask[g * block : (g + 1) * block, at].astype(BF16)
 
 
 def planes_kernel(
-    recv_hbm, back_hbm, forward_hbm, mask_hbm, x_hbm, pot_hbm, out_ref,
-    recv_ref, back_ref, forward_ref, mask_ref, x_ref, pot_ref, value_ref, sums_ref, y_buf, p_buf, q_buf, sem,
+    recv_hbm, sort_hbm, back_hbm, forward_hbm, mask_hbm, x_hbm, xt_hbm, pot_hbm, out_ref,
+    recv_ref, sort_ref, back_ref, forward_ref, mask_ref, x_ref, xt_ref, pot_ref,
+    value_ref, sums_ref, spread_buf, y_buf, p_buf, q_buf, sem,
 ):
     parts, rows, _ = recv_ref.shape
     planes, grid, _ = pot_ref.shape
-    half = mask_ref.shape[0]
+    tiles, blocks, block, wide = mask_ref.shape
+    half = blocks * block
     bands = rows // planes
-    group = y_buf.shape[0] // bands
+    pairs = y_buf.shape[0]
+    group = pairs // bands
     steps = planes // group
-    small = start_all(*[
-        pltpu.make_async_copy(source, target, sem.at[i])
-        for i, (source, target) in enumerate([
-            (recv_hbm, recv_ref),
-            (mask_hbm, mask_ref),
-            (forward_hbm, forward_ref),
-            (x_hbm, x_ref),
-            (back_hbm, back_ref),
-        ])
-    ])
-
-    def pot_copy(step):
-        at = pl.ds(step * group, group)
-        return pltpu.make_async_copy(pot_hbm.at[at], pot_ref.at[at], sem.at[len(small) + step])
-
-    for step in range(steps):
-        pot_copy(step).start()
-    for copy in small:
-        copy.wait()
+    sources = [
+        (recv_hbm, recv_ref),
+        (sort_hbm, sort_ref),
+        (mask_hbm, mask_ref),
+        (forward_hbm, forward_ref),
+        (x_hbm, x_ref),
+        (xt_hbm, xt_ref),
+        (back_hbm, back_ref),
+    ]
+    n_small = len(sources)
+    for z in range(0, planes, group):
+        sources.append((pot_hbm.at[z : z + group], pot_ref.at[z : z + group]))
+    copies = start_all(*[pltpu.make_async_copy(a, b, sem.at[i]) for i, (a, b) in enumerate(sources)])
     first = lane_iota((rows, LANES)) < LANES // 2
 
     def halves(even, odd):
@@ -183,11 +193,34 @@
         high = jnp.where(first, pltpu.roll(even, LANES // 2, 1), odd)
         return low, high
 
+    copies[0].wait()
+    natural = ([], [])
     for pair in range(parts // 2):
-        at = slice(pair * LANES, (pair + 1) * LANES)
-        value_ref[0, :, at], value_ref[1, :, at] = halves(
-            recv_ref[2 * pair].astype(F32), recv_ref[2 * pair + 1].astype(F32)
-        )
+        both = halves(recv_ref[2 * pair].astype(F32), recv_ref[2 * pair + 1].astype(F32))
+        for c in range(2):
+            natural[c].append(both[c].astype(BF16))
+    copies[1].wait()
+    for c in range(2):
+        values = dot(jnp.concatenate(natural[c], 1), sort_ref[...], ((1,), (1,)))
+        for tile in range(tiles):
+            value_ref[c, tile] = values[:, tile * wide : (tile + 1) * wide]
+    for copy in copies[2:n_small]:
+        copy.wait()
+
+    row = row_iota((block, LANES)).astype(F32)
+    starts = []
+    for tile in range(1, tiles):
+        at = jnp.float32(0.0)
+        for g in range(blocks):
+            here = mask_ref[tile, g, :, :LANES].astype(F32)
+            at = at + jnp.sum(jnp.where(lane_iota((block, LANES)) == 0, here * float(g), 0.0))
+        starts.append(at.astype(jnp.int32) + tile)
+    runs = []
+    for i in range(blocks + tiles - 1):
+        tile = jnp.int32(0)
+        for start in starts:
+            tile = tile + (i >= start).astype(jnp.int32)
+        runs.append((tile, i - tile))
 
     lane = lane_iota((grid, LANES))
     low_at = jnp.clip(grid - LANES - lane, 0, LANES - 1)
@@ -203,55 +236,68 @@
         back = jnp.where((lane > 0) & (lane < grid // 2), back, 0.0)
         return jnp.concatenate([jnp.where(lane <= grid // 2, near, 0.0), back], 1)
 
-    def body(step, carry):
-        mask = mask_ref[...].astype(BF16)
-        for p in range(group):
-            z = step * group + p
+    def at_pair(i, c):
+        return slice((c * pairs + i) * block, (c * pairs + i + 1) * block)
+
+    def spread_at(g, i, c):
+        total = 0.0
+        for t in range(tiles):
+            total = total + jnp.where(runs[g + t][0] == t, spread_buf[g + t, at_pair(i, c)], 0.0)
+        return total
+
+    for step in range(steps):
+        for i, (tile, g) in enumerate(runs):
+            mask = mask_ref[tile, g]
             placed = []
-            for b in range(bands):
-                for c in range(2):
-                    placed.append(mask * value_ref[c, pl.ds(b * planes + z, 1), :].astype(BF16))
-            spread = dot(jnp.concatenate(placed, 0), forward_ref[...])
-            for b in range(bands):
-                at = 2 * b * half
-                real, imag = spread[at : at + half], spread[at + half : at + 2 * half]
+            for c in range(2):
+                for p in range(group):
+                    for b in range(bands):
+                        row = value_ref[c, tile, pl.ds(b * planes + step * group + p, 1), :]
+                        placed.append(mask * row.astype(BF16))
+            spread_buf[i] = dot(jnp.concatenate(placed, 0), forward_ref[tile])
+        for i in range(pairs):
+            for g in range(blocks):
+                real, imag = spread_at(g, i, 0), spread_at(g, i, 1)
                 rc, rs, ic, si = real[:, :LANES], real[:, LANES:], imag[:, :LANES], imag[:, LANES:]
                 y_re = jnp.concatenate([rc - si, rc + si], 1).astype(BF16)
                 y_im = jnp.concatenate([ic + rs, ic - rs], 1).astype(BF16)
-                i = p * bands + b
-                y_buf[i, 0, :half] = y_re
-                y_buf[i, 0, half:] = y_im
-                y_buf[i, 1, :half] = y_im
-                y_buf[i, 1, half:] = y_re
-        pot_copy(step).wait()
+                y_buf[i, g * block : (g + 1) * block] = y_re
+                y_buf[i, half + g * block : half + (g + 1) * block] = y_im
+        copies[n_small + step].wait()
         for p in range(group):
             weight = mirrored_potential(step * group + p)
-            for b in range(bands):
-                for c in range(2):
-                    i = p * bands + b
-                    p_buf[i, c] = (dot(x_ref[c], y_buf[i, c]) * weight).astype(BF16)
-        for i in range(group * bands):
-            s_re = dot(x_ref[2], p_buf[i, 0])
-            s_im = dot(x_ref[2], p_buf[i, 1])
-            q_re = s_re[:half] + s_im[half:]
-            q_im = s_im[:half] - s_re[half:]
+            for i in range(p * bands, (p + 1) * bands):
+                field = dot(x_ref[...], y_buf[i])
+                p_buf[i, :grid] = (field[:grid] * weight).astype(BF16)
+                p_buf[i, grid:] = (field[grid:] * weight).astype(BF16)
+        for i in range(pairs):
+            both = dot(xt_ref[...], p_buf[i])
+            q_re, q_im = both[:half], both[half:]
             rp, rm, ip, im = q_re[:, :LANES], q_re[:, LANES:], q_im[:, :LANES], q_im[:, LANES:]
-            q_buf[i, :half] = jnp.concatenate([rp + rm, ip - im], 1).astype(BF16)
-            q_buf[i, half:] = jnp.concatenate([ip + im, rm - rp], 1).astype(BF16)
-        for p in range(group):
-            folded = q_buf[p * bands : (p + 1) * bands].reshape(bands * 2 * half, 2 * LANES)
-            full = dot(folded, back_ref[...])
-            for b in range(bands):
-                for c in range(2):
-                    at = (2 * b + c) * half
-                    kept = jnp.sum(full[at : at + half] * mask_ref[...], axis=0, keepdims=True)
-                    sums_ref[c, pl.ds((step * group + p) * bands + b, 1), :] = kept
-        return carry
-
-    lax.fori_loop(0, steps, body, 0)
+            real = jnp.concatenate([rp + rm, ip - im], 1).astype(BF16)
+            imag = jnp.concatenate([ip + im, rm - rp], 1).astype(BF16)
+            for g in range(blocks):
+                q_buf[g, at_pair(i, 0)] = real[g * block : (g + 1) * block]
+                q_buf[g, at_pair(i, 1)] = imag[g * block : (g + 1) * block]
+        sums = [0.0] * tiles
+        for tile, g in runs:
+            full = dot(q_buf[g], back_ref[tile]).reshape(2 * pairs, block // 8, 8, wide)
+            mask = mask_ref[tile, g].astype(F32).reshape(block // 8, 8, wide)
+            kept = jnp.sum(full * mask[None], axis=1)
+            sums = [total + jnp.where(tile == t, kept, 0.0) for t, total in enumerate(sums)]
+        at = pl.ds(step * pairs, pairs)
+        for t, total in enumerate(sums):
+            total = jnp.sum(total, axis=1)
+            for c in range(2):
+                sums_ref[c, t, at] = total[c * pairs : (c + 1) * pairs]
+
+    natural = []
+    for c in range(2):
+        values = jnp.concatenate([sums_ref[c, tile] for tile in range(tiles)], 1)
+        natural.append(dot(values.astype(BF16), sort_ref[...]))
     for pair in range(parts // 2):
         at = slice(pair * LANES, (pair + 1) * LANES)
-        even, odd = halves(sums_ref[0, :, at], sums_ref[1, :, at])
+        even, odd = halves(natural[0][:, at], natural[1][:, at])
         out_ref[2 * pair] = even.astype(BF16)
         out_ref[2 * pair + 1] = odd.astype(BF16)
 
@@ -265,7 +311,7 @@
     at_me = row_iota(column_ref.shape) == me // 2
     column = jnp.sum(jnp.where(at_me, column_ref[...].astype(F32), 0.0), axis=0, keepdims=True)
     column = jnp.where(me % 2 == 1, pltpu.roll(column, LANES // 2, 1), column)[:, :sticks]
-    column = to_column(column)
+    column = to_column(column, sticks)
     x_pos = jnp.floor((column + 0.5) * (1.0 / half))
     x_freq = x_pos - half // 2
     y_freq = column - x_pos * half - half // 2
@@ -284,7 +330,7 @@
             send_ref[r, b] = h[r * own_sticks : (r + 1) * own_sticks].astype(BF16)
 
 
-def margin_kernel(recv_ref, orbitals_ref, order_ref, swap_ref, repeat_ref, keep_ref, fold_ref, out_ref):
+def margin_kernel(recv_ref, orbitals_ref, order_ref, swap_ref, out_ref):
     own_sticks, width, n_orbitals = orbitals_ref.shape
     h = recv_ref[...].astype(F32).reshape(-1, width).astype(BF16)
     swapped = dot(h, swap_ref[...])
@@ -294,11 +340,21 @@
     total = jnp.zeros((columns, n_orbitals), F32)
     for j in range(own_sticks):
         total = total + dot(ordered[j * columns : (j + 1) * columns], orbitals_ref[j])
-    exact = lax.Precision.HIGHEST
-    spread = dot(total.T, repeat_ref[...], precision=exact) * keep_ref[...]
-    packed = dot(fold_ref[...], spread, precision=exact)
-    for k in range(out_ref.shape[1]):
-        out_ref[:, k, :] = packed[:, k * LANES : (k + 1) * LANES]
+    turned = jnp.concatenate([total, jnp.zeros((LANES - columns, n_orbitals), F32)], 0).T
+    joined = LANES // columns
+    if joined == 8:
+        spread = pltpu.roll(turned, 0, 1, stride=columns, stride_axis=0)
+        packed = jnp.sum(spread.reshape(n_orbitals // joined, joined, LANES), axis=1)
+    else:
+        place = row_iota(turned.shape) & (joined - 1)
+        spread = turned
+        for k in range(1, joined):
+            spread = jnp.where(place == k, pltpu.roll(turned, k * columns, 1), spread)
+        shape = (n_orbitals // joined, n_orbitals)
+        owner = lax.shift_right_logical(lane_iota(shape), joined.bit_length() - 1)
+        fold = jnp.where(owner == row_iota(shape), 1.0, 0.0)
+        packed = dot(fold, spread, precision=lax.Precision.HIGHEST)
+    out_ref[...] = packed.reshape(out_ref.shape)
 
 
 def margin_sum_kernel(recv_ref, keep_ref, fold_ref, out_ref):
@@ -351,13 +407,16 @@
     received = lax.all_to_all(sent, "fft", 0, 0, tiled=True)
 
     wide = 2 * LANES
-    table_y, table_x = y_table(grid, half), x_tables(grid, half)
+    table_y, table_x = y_table(grid, half), x_table(grid, half)
+    table_xt = np.ascontiguousarray(table_x.T)
+    tiles, blocks = all_sticks // wide, half // BLOCK
     tables = (
-        shape((wide, all_sticks), BF16),
-        shape((all_sticks, wide), BF16),
-        shape((half, all_sticks), F32),
-    )
-    back, forward, mask = call(
+        shape((all_sticks, all_sticks), BF16),
+        shape((tiles, wide, wide), BF16),
+        shape((tiles, wide, wide), BF16),
+        shape((tiles, blocks, BLOCK, wide), BF16),
+    )
+    sort, back, forward, mask = call(
         tables_kernel,
         tables,
         columns,
@@ -371,30 +430,34 @@
         ],
     )
     group = math.gcd(GROUP, planes)
-    values = pltpu.VMEM((2, bands * planes, all_sticks), F32)
     pairs = group * bands
+    values = pltpu.VMEM((2, tiles, bands * planes, wide), F32)
     sent = call(
         planes_kernel,
         exchanged,
         received,
+        sort,
         back,
         forward,
         mask,
         table_x,
+        table_xt,
         potential,
         vmem=MOST_VMEM,
-        in_specs=[in_hbm] * 6,
+        in_specs=[in_hbm] * 8,
         scratch_shapes=[
             pltpu.VMEM(exchanged.shape, BF16),
             *(pltpu.VMEM(t.shape, t.dtype) for t in tables),
             pltpu.VMEM(table_x.shape, BF16),
+            pltpu.VMEM(table_xt.shape, BF16),
             pltpu.VMEM(potential.shape, F32),
             values,
             values,
-            pltpu.VMEM((pairs, 2, 2 * half, wide), BF16),
-            pltpu.VMEM((pairs, 2, grid, wide), BF16),
+            pltpu.VMEM((blocks + tiles - 1, 2 * pairs * BLOCK, wide), F32),
             pltpu.VMEM((pairs, 2 * half, wide), BF16),
-            dma((5 + planes // group,)),
+            pltpu.VMEM((pairs, 2 * grid, wide), BF16),
+            pltpu.VMEM((blocks, 2 * pairs * BLOCK, wide), BF16),
+            dma((7 + planes // group,)),
         ],
     )
     received = lax.all_to_all(sent, "fft", 0, 0, tiled=True)
@@ -421,9 +484,8 @@
     swap[np.arange(half) + half, np.arange(half)] = 1.0
     swap[np.arange(half), np.arange(half) + half] = -1.0
     slot = np.arange(packed)
-    repeat = (np.arange(n_columns)[:, None] == slot[None] % n_columns).astype(np.float32)
     keep = (np.arange(own)[:, None] == slot[None] // n_columns).astype(np.float32)
-    fold = (np.arange(n_dev)[:, None] == np.arange(n_orbitals)[None] // own).astype(np.float32)
+    fold = (slot[:, None] % n_columns == np.arange(n_columns)[None]).astype(np.float32)
     sent = call(
         margin_kernel,
         shape((n_dev, packed // LANES, LANES), F32),
@@ -431,14 +493,9 @@
         orbitals.transpose(1, 2, 0),
         order.astype(BF16),
         swap.astype(BF16),
-        repeat,
-        np.tile(keep, (n_dev, 1)),
-        fold,
     )
     received = lax.all_to_all(sent, ("band", "fft"), 0, 0, tiled=True)
-    margin = call(
-        margin_sum_kernel, shape((own, n_columns), F32), received, keep, np.ascontiguousarray(repeat.T)
-    )
+    margin = call(margin_sum_kernel, shape((own, n_columns), F32), received, keep, fold)
     return applied, margin
 
 

time: 60 us -> 57.6 us (0.960)
  Pallas kernels: 22.3 us -> 20.5 us
  waiting for transfers between devices: 3.32 us -> 2.66 us
    pallas_call x6, Pallas kernels: 22.3 us -> 20.5 us  [call(): pl.pallas_call(kernel, out_shape=out_shape, compiler_params=pltpu.Compile...]
    all_to_all x1, waiting for transfers between devices: 3.32 us -> 2.66 us  [per_device(): received = lax.all_to_all(sent, 'fft', 0, 0, tiled=True)]
  transfers between devices with their start and end apart: 1 -> 1, of which waited for: 1 -> 1; matrix products, arithmetic and copies ran while one was open for 0% -> 0% of each run, Pallas kernels for 3% -> 5%
where the time goes in v4:
time: 57.6 us; the launch traced here: 57.2 us
  blocking collectives  28 us (49%)
  Pallas kernels  20.5 us (36%)
  starting transfers between devices  5.18 us (9%)
  waiting for transfers between devices  2.66 us (5%)
  between operations  0.74 us (1%)
    pallas_call x6, Pallas kernels, call(): pl.pallas_call(kernel, out_shape=out_shape, compiler_params=pltpu.Compile...  20.5 us
    all_to_all x1, blocking collectives, per_device(): received = lax.all_to_all(sent, 'band', 0, 0, tiled=True)  10.6 us
    all_to_all x1, blocking collectives, per_device(): received = lax.all_to_all(sent, ('band', 'fft'), 0, 0, tiled=True)  8.95 us
    all_to_all x1, blocking collectives, per_device(): received = lax.all_to_all(sent, 'fft', 0, 0, tiled=True)  8.47 us
    all_to_all x1, starting transfers between devices, per_device(): received = lax.all_to_all(sent, 'fft', 0, 0, tiled=True)  5.18 us
    all_to_all x1, waiting for transfers between devices, per_device(): received = lax.all_to_all(sent, 'fft', 0, 0, tiled=True)  2.66 us
  transfers between devices with their start and end apart: 1, of which 1 were waited for; matrix products, arithmetic and copies ran while one was open for 0% of the time, Pallas kernels for 5%

profile of v4, /device:TPU:0, one launch (start us, length us, event | category | flops | bytes accessed | tf_op | source)
XLA Modules:
  0.0 57.2 jit_solution(4768042401711868042)
XLA Ops:
  0.6 0.0 copy-start.3
  0.6 0.0 copy-start.9
  0.6 0.0 copy-start.8
  0.7 0.0 copy-start.5
  0.7 0.0 copy-start.6
  0.7 2.2 %shard_map.158 = bf16[8,48,128]{2,1,0:T(8,128)(2,1)} custom-call(f32[2,64,192]{2,1,0:T(8,128)} %coeffs_ref.1, s32[1,64]{1,0:T(1,128)} %bitcast.6, bf16[768,192]{1,0:T(8,128)(2,1)} %constant.20.clone.table_hbm), custom_call_target="tpu_custom_call" | custom-call | tf_op jit(solution)/shard_map/pallas_call | solution.py:368
  2.9 5.2 %all-to-all-start = ((bf16[8,48,128]{2,1,0:T(8,128)(2,1)}), bf16[8,48,128]{2,1,0:T(8,128)(2,1)}, u32[]{:S(2)}, u32[]{:S(2)}) async-start(bf16[8,48,128]{2,1,0:T(8,128)(2,1)} %shard_map.158), calls=%async_computation | async-start | bytes 196608 | tf_op jit(solution)/shard_map/all_to_all | solution.py:407
  8.1 2.6 %shard_map.159 = (bf16[512,512]{1,0:T(8,128)(2,1)}, bf16[2,256,256]{2,1,0:T(8,128)(2,1)}, bf16[2,256,256]{2,1,0:T(8,128)(2,1)}, bf16[2,6,16,256]{3,2,1,0:T(8,128)(2,1)}) custom-call(s32[4,128]{1,0:T(4,128)} %bitcast.4, bf16[256,96]{1,0:T(8,128)(2,1)} %constant.21.clone.y_hbm), custom_call_target="tpu_custom_call" | custom-call | tf_op jit(solution)/shard_map/pallas_call | solution.py:368
  10.7 0.0 copy-start
  10.7 2.7 %all-to-all-done.recv_hbm = bf16[8,48,128]{2,1,0:T(8,128)(2,1)} async-done(((bf16[8,48,128]{2,1,0:T(8,128)(2,1)}), bf16[8,48,128]{2,1,0:T(8,128)(2,1)}, u32[]{:S(2)}, u32[]{:S(2)}) %all-to-all-start) | async-done | bytes 98336 | tf_op jit(solution)/shard_map/all_to_all | solution.py:407
  13.4 0.0 copy-start.1
  13.4 0.0 copy-start.2
  13.4 0.0 copy-start.4
  13.4 0.0 copy-start.7
  13.4 12.7 %shard_map.160 = bf16[8,48,128]{2,1,0:T(8,128)(2,1)} custom-call(bf16[8,48,128]{2,1,0:T(8,128)(2,1)} %all-to-all-done.recv_hbm, bf16[512,512]{1,0:T(8,128)(2,1)} %get-tuple-element.8.sort_hbm, bf16[2,256,256]{2,1,0:T(8,128)(2,1)} %get-tuple-element.9.back_hbm, bf16[2,256,256]{2,1,0:T(8,128)(2,1)} %get-tuple-element.10.forward_hbm, ...), custom_call_target="tpu_custom_call" | custom-call | tf_op jit(solution)/shard_map/pallas_call | solution.py:368
  26.1 8.5 %all_to_all.20.recv_ref = bf16[8,48,128]{2,1,0:T(8,128)(2,1)S(1)} all-to-all(bf16[8,48,128]{2,1,0:T(8,128)(2,1)} %shard_map.160), channel_id=1, replica_groups=mesh['band'=4,'fft'=8] {'fft'}, dimensions={0} | all-to-all | bytes 196608 | tf_op jit(solution)/shard_map/all_to_all | solution.py:463
  34.6 0.0 copy-done.3
  34.6 0.0 copy-done.9
  34.6 0.0 copy-done.8
  34.6 0.0 copy-done.1
  34.6 0.0 copy-done.2
  34.6 1.1 %shard_map.161 = (bf16[2,64,192]{2,1,0:T(8,128)(2,1)}, bf16[4,2,16,192]{3,2,1,0:T(8,128)(2,1)S(1)}) custom-call(bf16[8,48,128]{2,1,0:T(8,128)(2,1)S(1)} %all_to_all.20.recv_ref, f32[2,64,192]{2,1,0:T(8,128)S(1)} %copy-done.3, s32[1,64]{1,0:T(1,128)S(1)} %bitcast.7, s32[4,128]{1,0:T(4,128)S(1)} %bitcast.5, bf16[384,1024]{1,0:T(8,128)(2,1)S(1)} %copy-done.2, ...), custom_call_target="tpu_custom_call" | custom-call | tf_op jit(solution)/shard_map/pallas_call | solution.py:368
  35.7 10.6 %all_to_all.21.recv_ref = bf16[4,2,16,192]{3,2,1,0:T(8,128)(2,1)S(1)} all-to-all(bf16[4,2,16,192]{3,2,1,0:T(8,128)(2,1)S(1)} %get-tuple-element.13), channel_id=1, replica_groups=mesh['band'=4,'fft'=8] {'band'}, dimensions={0} | all-to-all | bytes 98304 | tf_op jit(solution)/shard_map/all_to_all | solution.py:474
  46.3 0.0 copy-done.5
  46.3 0.0 copy-done.6
  46.3 0.0 copy-done
  46.3 1.1 %shard_map.162 = f32[32,2,128]{2,1,0:T(2,128)S(1)} custom-call(bf16[4,2,16,192]{3,2,1,0:T(8,128)(2,1)S(1)} %all_to_all.21.recv_ref, bf16[16,192,512]{2,1,0:T(8,128)(2,1)S(1)} %bitcast.3, bf16[256,256]{1,0:T(8,128)(2,1)S(1)} %copy-done.5, bf16[192,192]{1,0:T(8,128)(2,1)S(1)} %copy-done.6), custom_call_target="tpu_custom_call" | custom-call | tf_op jit(solution)/shard_map/pallas_call | solution.py:368
  47.4 8.9 %all_to_all.22.recv_ref = f32[32,2,128]{2,1,0:T(2,128)S(1)} all-to-all(f32[32,2,128]{2,1,0:T(2,128)S(1)} %shard_map.162), channel_id=1, replica_groups=mesh['band'=4,'fft'=8] {'band','fft'}, dimensions={0} | all-to-all | bytes 65536 | tf_op jit(solution)/shard_map/all_to_all | solution.py:497
  56.3 0.0 copy-done.4
  56.3 0.0 copy-done.7
  56.3 0.8 %shard_map.163 = f32[16,16]{1,0:T(8,128)} custom-call(f32[32,2,128]{2,1,0:T(2,128)S(1)} %all_to_all.22.recv_ref, f32[16,256]{1,0:T(8,128)S(1)} %copy-done.7, f32[256,16]{1,0:T(8,128)S(1)} %copy-done.4), custom_call_target="tpu_custom_call" | custom-call | tf_op jit(solution)/shard_map/pallas_call | solution.py:368
Async XLA Ops:
  0.6 33.9 %copy-start.3 = (f32[2,64,192]{2,1,0:T(8,128)S(1)}, f32[2,64,192]{2,1,0:T(8,128)}, u32[]{:S(2)}) copy-start(f32[2,64,192]{2,1,0:T(8,128)} %coeffs_ref.1) | copy-start | bytes 294916
  0.6 33.9 %copy-start.9 = (s32[64]{0:T(128)S(1)}, s32[64]{0:T(128)}, u32[]{:S(2)}) copy-start(s32[64]{0:T(128)} %param.18) | copy-start | bytes 772
  0.6 33.9 %copy-start.8 = (s32[512]{0:T(512)S(1)}, s32[512]{0:T(512)}, u32[]{:S(2)}) copy-start(s32[512]{0:T(512)} %param.17) | copy-start | bytes 6148
  0.7 45.6 %copy-start.5 = (bf16[256,256]{1,0:T(8,128)(2,1)S(1)}, bf16[256,256]{1,0:T(8,128)(2,1)}, u32[]{:S(2)}) copy-start(bf16[256,256]{1,0:T(8,128)(2,1)} %constant.26.clone.order_ref) | copy-start | bytes 393220
  0.7 45.6 %copy-start.6 = (bf16[192,192]{1,0:T(8,128)(2,1)S(1)}, bf16[192,192]{1,0:T(8,128)(2,1)}, u32[]{:S(2)}) copy-start(bf16[192,192]{1,0:T(8,128)(2,1)} %constant.27.clone.swap_ref) | copy-start | bytes 221188
  2.9 10.5 %all-to-all-start = ((bf16[8,48,128]{2,1,0:T(8,128)(2,1)}), bf16[8,48,128]{2,1,0:T(8,128)(2,1)}, u32[]{:S(2)}, u32[]{:S(2)}) async-start(bf16[8,48,128]{2,1,0:T(8,128)(2,1)} %shard_map.158), calls=%async_computation | async-start | bytes 196608 | tf_op jit(solution)/shard_map/all_to_all | solution.py:407
  10.7 35.6 %copy-start = (bf16[512,16,192]{0,2,1:T(8,128)(2,1)S(1)}, bf16[512,16,192]{0,2,1:T(8,128)(2,1)}, u32[]{:S(2)}) copy-start(bf16[512,16,192]{0,2,1:T(8,128)(2,1)} %param.19) | copy-start | bytes 9437188
  13.4 21.2 %copy-start.1 = (bf16[384,1024]{1,0:T(8,128)(2,1)S(1)}, bf16[384,1024]{1,0:T(8,128)(2,1)}, u32[]{:S(2)}) copy-start(bf16[384,1024]{1,0:T(8,128)(2,1)} %constant.25.clone.low_ref) | copy-start | bytes 2359300
  13.4 21.2 %copy-start.2 = (bf16[384,1024]{1,0:T(8,128)(2,1)S(1)}, bf16[384,1024]{1,0:T(8,128)(2,1)}, u32[]{:S(2)}) copy-start(bf16[384,1024]{1,0:T(8,128)(2,1)} %constant.24.clone.high_ref) | copy-start | bytes 2359300
  13.4 42.9 %copy-start.4 = (f32[256,16]{1,0:T(8,128)S(1)}, f32[256,16]{1,0:T(8,128)}, u32[]{:S(2)}) copy-start(f32[256,16]{1,0:T(8,128)} %constant.29.clone.fold_ref) | copy-start | bytes 49156
  13.4 42.9 %copy-start.7 = (f32[16,256]{1,0:T(8,128)S(1)}, f32[16,256]{1,0:T(8,128)}, u32[]{:S(2)}) copy-start(f32[16,256]{1,0:T(8,128)} %constant.28.clone.keep_ref) | copy-start | bytes 49156

commit v5 on v4

--- a/solution.py
+++ b/solution.py
@@ -15,7 +15,7 @@
 GROUP = 12
 BLOCK = 16
 ALL_VMEM = 62 * 2**20
-MOST_VMEM = 57 * 2**20
+MOST_VMEM = 53 * 2**20
 SOME_VMEM = 16 * 2**20
 
 
@@ -50,18 +50,28 @@
     return split_bf16(table.reshape(grid * bands, 2 * bands * width))
 
 
-def y_table(grid, half):
-    theta = angles(grid, half)[: grid // 2 + 1]
-    table = np.zeros((2, LANES, half), np.float32)
-    table[0, : grid // 2 + 1] = np.cos(theta)
-    table[1, 1 : grid // 2] = np.sin(theta)[1:-1]
-    return table.reshape(2 * LANES, half).astype(BF16)
-
-
-def x_table(grid, half):
+def plane_tables(grid, half):
     theta = angles(grid, half)
+    wide = 2 * LANES
+    table_y = np.zeros((2, LANES, wide), np.float32)
+    table_y[0, : grid // 2 + 1, :half] = np.cos(theta[: grid // 2 + 1])
+    table_y[1, 1 : grid // 2, :half] = np.sin(theta[1 : grid // 2])
     cosine, sine = np.cos(theta), np.sin(theta)
-    return np.block([[cosine, -sine], [sine, cosine]]).astype(BF16)
+    table_x = np.block([[cosine, -sine], [sine, cosine]])
+    padded = np.zeros((2 * grid, wide), np.float32)
+    padded[:, : 2 * half] = table_x
+    turned = np.zeros((2 * half, 2, wide), np.float32)
+    turned.reshape(2 * half, 2 * wide)[:, : 2 * grid] = table_x.T
+    turned = turned.swapaxes(0, 1)
+    parts = [table_y.reshape(wide, wide), padded, turned.reshape(-1, wide)]
+    return np.concatenate(parts, 0).astype(BF16)
+
+
+def table_rows(grid, half, n_sticks):
+    wide = 2 * LANES
+    tiles = n_sticks // wide
+    sizes = (tiles * n_sticks, tiles * half, n_sticks, n_sticks, 2 * grid, 4 * half)
+    return [sum(sizes[:i]) for i in range(len(sizes) + 1)]
 
 
 def lane_iota(shape):
@@ -127,14 +137,16 @@
         out_ref[part] = jnp.concatenate(rows, 0).astype(BF16)
 
 
-def tables_kernel(column_hbm, y_hbm, sort_ref, back_ref, forward_ref, mask_ref, column_ref, y_ref, sem):
+def tables_kernel(grid, half, column_hbm, const_hbm, out_ref, column_ref, y_ref, sem):
+    wide = 2 * LANES
+    n = column_ref.shape[0] * LANES
+    tiles = n // wide
+    sort_at, mask_at, forward_at, back_at, x_at, _, end = table_rows(grid, half, n)
     copies = start_all(
         pltpu.make_async_copy(column_hbm, column_ref, sem.at[0]),
-        pltpu.make_async_copy(y_hbm, y_ref, sem.at[1]),
-    )
-    half = y_ref.shape[1]
-    tiles, blocks, block, wide = mask_ref.shape
-    n = tiles * wide
+        pltpu.make_async_copy(const_hbm.at[:wide], y_ref, sem.at[1]),
+        pltpu.make_async_copy(const_hbm.at[wide:], out_ref.at[x_at:end], sem.at[2]),
+    )
     copies[0].wait()
     column = column_ref[...].astype(F32)
     column = jnp.concatenate([column[i : i + 1] for i in range(column.shape[0])], 1)
@@ -143,49 +155,61 @@
     key = x_pos * n + lane_iota(column.shape).astype(F32)
     rank = jnp.sum(jnp.where(to_column(key, n) < key, 1.0, 0.0), axis=0, keepdims=True)
     sort = jnp.where(row_iota((n, n)).astype(F32) == rank, 1.0, 0.0).astype(BF16)
-    sort_ref[...] = sort
     nt = ((1,), (1,))
     index = row_iota((half, n)).astype(F32)
     at_x = jnp.where(index == x_pos, 1.0, 0.0).astype(BF16)
     at_y = jnp.where(index == y_pos, 1.0, 0.0).astype(BF16)
-    mask = dot(at_x, sort, nt)
+    mask = dot(at_x, sort, nt).astype(BF16)
     at_y = dot(at_y, sort, nt).astype(BF16)
     copies[1].wait()
-    back = dot(y_ref[...], at_y)
+    back = dot(y_ref[:, :half], at_y)
     for tile in range(tiles):
         at = slice(tile * wide, (tile + 1) * wide)
-        back_ref[tile] = back[:, at].astype(BF16)
-        forward_ref[tile] = back[:, at].T.astype(BF16)
-        for g in range(blocks):
-            mask_ref[tile, g] = mask[g * block : (g + 1) * block, at].astype(BF16)
+        out_ref[sort_at + tile * n : sort_at + (tile + 1) * n] = sort[:, at]
+        out_ref[mask_at + tile * half : mask_at + (tile + 1) * half] = mask[:, at]
+        out_ref[forward_at + tile * wide : forward_at + (tile + 1) * wide] = back[:, at].T.astype(BF16)
+        out_ref[back_at + tile * wide : back_at + (tile + 1) * wide] = back[:, at].astype(BF16)
+    copies[2].wait()
 
 
 def planes_kernel(
-    recv_hbm, sort_hbm, back_hbm, forward_hbm, mask_hbm, x_hbm, xt_hbm, pot_hbm, out_ref,
-    recv_ref, sort_ref, back_ref, forward_ref, mask_ref, x_ref, xt_ref, pot_ref,
-    value_ref, sums_ref, spread_buf, y_buf, p_buf, q_buf, sem,
+    recv_hbm, table_hbm, pot_hbm, out_ref,
+    recv_ref, table_ref, pot_ref, value_ref, sums_ref, spread_buf, y_buf, p_buf, q_buf, sem,
 ):
     parts, rows, _ = recv_ref.shape
     planes, grid, _ = pot_ref.shape
-    tiles, blocks, block, wide = mask_ref.shape
+    blocks, _, wide = q_buf.shape
+    block = BLOCK
     half = blocks * block
+    tiles = value_ref.shape[1]
+    n_sticks = tiles * wide
     bands = rows // planes
     pairs = y_buf.shape[0]
     group = pairs // bands
     steps = planes // group
+    sort_at, mask_at, forward_at, back_at, x_at, turned_at, _ = table_rows(grid, half, n_sticks)
     sources = [
         (recv_hbm, recv_ref),
-        (sort_hbm, sort_ref),
-        (mask_hbm, mask_ref),
-        (forward_hbm, forward_ref),
-        (x_hbm, x_ref),
-        (xt_hbm, xt_ref),
-        (back_hbm, back_ref),
+        (table_hbm.at[:mask_at], table_ref.at[:mask_at]),
+        (table_hbm.at[mask_at:], table_ref.at[mask_at:]),
     ]
     n_small = len(sources)
     for z in range(0, planes, group):
         sources.append((pot_hbm.at[z : z + group], pot_ref.at[z : z + group]))
     copies = start_all(*[pltpu.make_async_copy(a, b, sem.at[i]) for i, (a, b) in enumerate(sources)])
+
+    def sort_tile(tile):
+        return table_ref[sort_at + tile * n_sticks : sort_at + (tile + 1) * n_sticks]
+
+    def mask_block(tile, g):
+        start = mask_at + tile * half + g * block
+        if not isinstance(start, int):
+            start = pl.multiple_of(start, block)
+        return table_ref[pl.ds(start, block)]
+
+    def tile_at(first_row, tile):
+        return table_ref[pl.ds(pl.multiple_of(first_row + tile * wide, wide // 4), wide)]
+
     first = lane_iota((rows, LANES)) < LANES // 2
 
     def halves(even, odd):
@@ -201,7 +225,10 @@
             natural[c].append(both[c].astype(BF16))
     copies[1].wait()
     for c in range(2):
-        values = dot(jnp.concatenate(natural[c], 1), sort_ref[...], ((1,), (1,)))
+        values = jnp.concatenate(natural[c], 1)
+        values = sum(
+            dot(values[:, tile * wide : (tile + 1) * wide], sort_tile(tile), ((1,), (1,))) for tile in range(tiles)
+        )
         for tile in range(tiles):
             value_ref[c, tile] = values[:, tile * wide : (tile + 1) * wide]
     for copy in copies[2:n_small]:
@@ -212,7 +239,7 @@
     for tile in range(1, tiles):
         at = jnp.float32(0.0)
         for g in range(blocks):
-            here = mask_ref[tile, g, :, :LANES].astype(F32)
+            here = mask_block(tile, g)[:, :LANES].astype(F32)
             at = at + jnp.sum(jnp.where(lane_iota((block, LANES)) == 0, here * float(g), 0.0))
         starts.append(at.astype(jnp.int32) + tile)
     runs = []
@@ -222,6 +249,9 @@
             tile = tile + (i >= start).astype(jnp.int32)
         runs.append((tile, i - tile))
 
+    table_x = table_ref[x_at:turned_at, : 2 * half]
+    table_xt = [table_ref[turned_at + 2 * half * i : turned_at + 2 * half * (i + 1)] for i in range(2)]
+    table_xt = jnp.concatenate(table_xt, 1)[:, : 2 * grid]
     lane = lane_iota((grid, LANES))
     low_at = jnp.clip(grid - LANES - lane, 0, LANES - 1)
     high_at = jnp.clip(grid - lane, 0, LANES - 1)
@@ -247,14 +277,14 @@
 
     for step in range(steps):
         for i, (tile, g) in enumerate(runs):
-            mask = mask_ref[tile, g]
+            mask = mask_block(tile, g)
             placed = []
             for c in range(2):
                 for p in range(group):
                     for b in range(bands):
                         row = value_ref[c, tile, pl.ds(b * planes + step * group + p, 1), :]
                         placed.append(mask * row.astype(BF16))
-            spread_buf[i] = dot(jnp.concatenate(placed, 0), forward_ref[tile])
+            spread_buf[i] = dot(jnp.concatenate(placed, 0), tile_at(forward_at, tile))
         for i in range(pairs):
             for g in range(blocks):
                 real, imag = spread_at(g, i, 0), spread_at(g, i, 1)
@@ -267,11 +297,11 @@
         for p in range(group):
             weight = mirrored_potential(step * group + p)
             for i in range(p * bands, (p + 1) * bands):
-                field = dot(x_ref[...], y_buf[i])
+                field = dot(table_x, y_buf[i])
                 p_buf[i, :grid] = (field[:grid] * weight).astype(BF16)
                 p_buf[i, grid:] = (field[grid:] * weight).astype(BF16)
         for i in range(pairs):
-            both = dot(xt_ref[...], p_buf[i])
+            both = dot(table_xt, p_buf[i])
             q_re, q_im = both[:half], both[half:]
             rp, rm, ip, im = q_re[:, :LANES], q_re[:, LANES:], q_im[:, :LANES], q_im[:, LANES:]
             real = jnp.concatenate([rp + rm, ip - im], 1).astype(BF16)
@@ -281,8 +311,8 @@
                 q_buf[g, at_pair(i, 1)] = imag[g * block : (g + 1) * block]
         sums = [0.0] * tiles
         for tile, g in runs:
-            full = dot(q_buf[g], back_ref[tile]).reshape(2 * pairs, block // 8, 8, wide)
-            mask = mask_ref[tile, g].astype(F32).reshape(block // 8, 8, wide)
+            full = dot(q_buf[g], tile_at(back_at, tile)).reshape(2 * pairs, block // 8, 8, wide)
+            mask = mask_block(tile, g).astype(F32).reshape(block // 8, 8, wide)
             kept = jnp.sum(full * mask[None], axis=1)
             sums = [total + jnp.where(tile == t, kept, 0.0) for t, total in enumerate(sums)]
         at = pl.ds(step * pairs, pairs)
@@ -294,7 +324,8 @@
     natural = []
     for c in range(2):
         values = jnp.concatenate([sums_ref[c, tile] for tile in range(tiles)], 1)
-        natural.append(dot(values.astype(BF16), sort_ref[...]))
+        values = values.astype(BF16)
+        natural.append(jnp.concatenate([dot(values, sort_tile(tile)) for tile in range(tiles)], 1))
     for pair in range(parts // 2):
         at = slice(pair * LANES, (pair + 1) * LANES)
         even, odd = halves(natural[0][:, at], natural[1][:, at])
@@ -407,26 +438,20 @@
     received = lax.all_to_all(sent, "fft", 0, 0, tiled=True)
 
     wide = 2 * LANES
-    table_y, table_x = y_table(grid, half), x_table(grid, half)
-    table_xt = np.ascontiguousarray(table_x.T)
+    const = plane_tables(grid, half)
     tiles, blocks = all_sticks // wide, half // BLOCK
-    tables = (
-        shape((all_sticks, all_sticks), BF16),
-        shape((tiles, wide, wide), BF16),
-        shape((tiles, wide, wide), BF16),
-        shape((tiles, blocks, BLOCK, wide), BF16),
-    )
-    sort, back, forward, mask = call(
-        tables_kernel,
-        tables,
+    table = shape((table_rows(grid, half, all_sticks)[-1], wide), BF16)
+    tables = call(
+        functools.partial(tables_kernel, grid, half),
+        table,
         columns,
-        table_y,
+        const,
         vmem=ALL_VMEM,
         in_specs=[in_hbm] * 2,
         scratch_shapes=[
             pltpu.VMEM(columns.shape, jnp.int32),
-            pltpu.VMEM(table_y.shape, BF16),
-            dma((2,)),
+            pltpu.VMEM((wide, wide), BF16),
+            dma((3,)),
         ],
     )
     group = math.gcd(GROUP, planes)
@@ -436,20 +461,13 @@
         planes_kernel,
         exchanged,
         received,
-        sort,
-        back,
-        forward,
-        mask,
-        table_x,
-        table_xt,
+        tables,
         potential,
         vmem=MOST_VMEM,
-        in_specs=[in_hbm] * 8,
+        in_specs=[in_hbm] * 3,
         scratch_shapes=[
             pltpu.VMEM(exchanged.shape, BF16),
-            *(pltpu.VMEM(t.shape, t.dtype) for t in tables),
-            pltpu.VMEM(table_x.shape, BF16),
-            pltpu.VMEM(table_xt.shape, BF16),
+            pltpu.VMEM(table.shape, BF16),
             pltpu.VMEM(potential.shape, F32),
             values,
             values,
@@ -457,7 +475,7 @@
             pltpu.VMEM((pairs, 2 * half, wide), BF16),
             pltpu.VMEM((pairs, 2 * grid, wide), BF16),
             pltpu.VMEM((blocks, 2 * pairs * BLOCK, wide), BF16),
-            dma((7 + planes // group,)),
+            dma((3 + planes // group,)),
         ],
     )
     received = lax.all_to_all(sent, "fft", 0, 0, tiled=True)

time: 57.6 us -> 55.8 us (0.969)
  blocking collectives: 28 us -> 27.1 us
    all_to_all x1, blocking collectives: 8.47 us -> 7.71 us  [per_device(): received = lax.all_to_all(sent, 'fft', 0, 0, tiled=True)]
where the time goes in v5:
time: 55.8 us; the launch traced here: 55.5 us
  blocking collectives  27.1 us (49%)
  Pallas kernels  20.2 us (36%)
  starting transfers between devices  5.18 us (9%)
  waiting for transfers between devices  2.23 us (4%)
  between operations  0.74 us (1%)
    pallas_call x6, Pallas kernels, call(): pl.pallas_call(kernel, out_shape=out_shape, compiler_params=pltpu.Compile...  20.2 us
    all_to_all x1, blocking collectives, per_device(): received = lax.all_to_all(sent, 'band', 0, 0, tiled=True)  10.4 us
    all_to_all x1, blocking collectives, per_device(): received = lax.all_to_all(sent, ('band', 'fft'), 0, 0, tiled=True)  8.95 us
    all_to_all x1, blocking collectives, per_device(): received = lax.all_to_all(sent, 'fft', 0, 0, tiled=True)  7.71 us
    all_to_all x1, starting transfers between devices, per_device(): received = lax.all_to_all(sent, 'fft', 0, 0, tiled=True)  5.18 us
    all_to_all x1, waiting for transfers between devices, per_device(): received = lax.all_to_all(sent, 'fft', 0, 0, tiled=True)  2.23 us
  transfers between devices with their start and end apart: 1, of which 1 were waited for; matrix products, arithmetic and copies ran while one was open for 0% of the time, Pallas kernels for 5%

profile of v5, /device:TPU:0, one launch (start us, length us, event | category | flops | bytes accessed | tf_op | source)
XLA Modules:
  0.0 55.5 jit_solution(17311133133370583624)
XLA Ops:
  0.6 2.1 %shard_map.140 = bf16[8,48,128]{2,1,0:T(8,128)(2,1)} custom-call(f32[2,64,192]{2,1,0:T(8,128)} %coeffs_ref.1, s32[1,64]{1,0:T(1,128)} %bitcast.6, bf16[768,192]{1,0:T(8,128)(2,1)} %constant.16.clone.table_hbm), custom_call_target="tpu_custom_call" | custom-call | tf_op jit(solution)/shard_map/pallas_call | solution.py:399
  2.8 5.2 %all-to-all-start = ((bf16[8,48,128]{2,1,0:T(8,128)(2,1)}), bf16[8,48,128]{2,1,0:T(8,128)(2,1)S(1)}, u32[]{:S(2)}, u32[]{:S(2)}) async-start(bf16[8,48,128]{2,1,0:T(8,128)(2,1)} %shard_map.140), calls=%async_computation | async-start | bytes 196608 | tf_op jit(solution)/shard_map/all_to_all | solution.py:438
  8.0 2.9 %shard_map.141.table_hbm = bf16[3008,256]{1,0:T(8,128)(2,1)} custom-call(s32[4,128]{1,0:T(4,128)} %bitcast.4, bf16[1024,256]{1,0:T(8,128)(2,1)} %constant.17.clone.const_hbm), custom_call_target="tpu_custom_call" | custom-call | tf_op jit(solution)/shard_map/pallas_call | solution.py:399
  10.9 0.0 copy-start.3
  10.9 0.0 copy-start.8
  10.9 0.0 copy-start.9
  10.9 0.0 copy-start
  10.9 0.0 copy-start.5
  10.9 2.2 %all-to-all-done.recv_hbm = bf16[8,48,128]{2,1,0:T(8,128)(2,1)S(1)} async-done(((bf16[8,48,128]{2,1,0:T(8,128)(2,1)}), bf16[8,48,128]{2,1,0:T(8,128)(2,1)S(1)}, u32[]{:S(2)}, u32[]{:S(2)}) %all-to-all-start) | async-done | bytes 98336 | tf_op jit(solution)/shard_map/all_to_all | solution.py:438
  13.2 0.0 copy-start.1
  13.2 0.0 copy-start.2
  13.2 0.0 copy-start.6
  13.2 12.1 %shard_map.142 = bf16[8,48,128]{2,1,0:T(8,128)(2,1)S(1)} custom-call(bf16[8,48,128]{2,1,0:T(8,128)(2,1)S(1)} %all-to-all-done.recv_hbm, bf16[3008,256]{1,0:T(8,128)(2,1)} %shard_map.141.table_hbm, f32[24,192,192]{2,1,0:T(8,128)} %pot_hbm.1), custom_call_target="tpu_custom_call" | custom-call | tf_op jit(solution)/shard_map/pallas_call | solution.py:399
  25.3 0.0 copy-start.4
  25.3 0.0 copy-start.7
  25.3 7.7 %all_to_all.20.recv_ref = bf16[8,48,128]{2,1,0:T(8,128)(2,1)S(1)} all-to-all(bf16[8,48,128]{2,1,0:T(8,128)(2,1)S(1)} %shard_map.142), channel_id=1, replica_groups=mesh['band'=4,'fft'=8] {'fft'}, dimensions={0} | all-to-all | bytes 196608 | tf_op jit(solution)/shard_map/all_to_all | solution.py:481
  33.0 0.0 copy-done.3
  33.0 0.0 copy-done.8
  33.1 0.0 copy-done.9
  33.1 0.0 copy-done.1
  33.1 0.0 copy-done.2
  33.1 1.1 %shard_map.143 = (bf16[2,64,192]{2,1,0:T(8,128)(2,1)}, bf16[4,2,16,192]{3,2,1,0:T(8,128)(2,1)S(1)}) custom-call(bf16[8,48,128]{2,1,0:T(8,128)(2,1)S(1)} %all_to_all.20.recv_ref, f32[2,64,192]{2,1,0:T(8,128)S(1)} %copy-done.3, s32[1,64]{1,0:T(1,128)S(1)} %bitcast.7, s32[4,128]{1,0:T(4,128)S(1)} %bitcast.5, bf16[384,1024]{1,0:T(8,128)(2,1)S(1)} %copy-done.2, ...), custom_call_target="tpu_custom_call" | custom-call | tf_op jit(solution)/shard_map/pallas_call | solution.py:399
  34.2 10.4 %all_to_all.21.recv_ref = bf16[4,2,16,192]{3,2,1,0:T(8,128)(2,1)S(1)} all-to-all(bf16[4,2,16,192]{3,2,1,0:T(8,128)(2,1)S(1)} %get-tuple-element.5), channel_id=1, replica_groups=mesh['band'=4,'fft'=8] {'band'}, dimensions={0} | all-to-all | bytes 98304 | tf_op jit(solution)/shard_map/all_to_all | solution.py:492
  44.6 0.0 copy-done
  44.6 0.0 copy-done.5
  44.6 0.0 copy-done.6
  44.6 1.1 %shard_map.144 = f32[32,2,128]{2,1,0:T(2,128)S(1)} custom-call(bf16[4,2,16,192]{3,2,1,0:T(8,128)(2,1)S(1)} %all_to_all.21.recv_ref, bf16[16,192,512]{2,1,0:T(8,128)(2,1)S(1)} %bitcast.3, bf16[256,256]{1,0:T(8,128)(2,1)S(1)} %copy-done.5, bf16[192,192]{1,0:T(8,128)(2,1)S(1)} %copy-done.6), custom_call_target="tpu_custom_call" | custom-call | tf_op jit(solution)/shard_map/pallas_call | solution.py:399
  45.7 8.9 %all_to_all.22.recv_ref = f32[32,2,128]{2,1,0:T(2,128)S(1)} all-to-all(f32[32,2,128]{2,1,0:T(2,128)S(1)} %shard_map.144), channel_id=1, replica_groups=mesh['band'=4,'fft'=8] {'band','fft'}, dimensions={0} | all-to-all | bytes 65536 | tf_op jit(solution)/shard_map/all_to_all | solution.py:515
  54.6 0.0 copy-done.4
  54.6 0.0 copy-done.7
  54.6 0.8 %shard_map.145 = f32[16,16]{1,0:T(8,128)} custom-call(f32[32,2,128]{2,1,0:T(2,128)S(1)} %all_to_all.22.recv_ref, f32[16,256]{1,0:T(8,128)S(1)} %copy-done.7, f32[256,16]{1,0:T(8,128)S(1)} %copy-done.4), custom_call_target="tpu_custom_call" | custom-call | tf_op jit(solution)/shard_map/pallas_call | solution.py:399
Async XLA Ops:
  2.8 10.4 %all-to-all-start = ((bf16[8,48,128]{2,1,0:T(8,128)(2,1)}), bf16[8,48,128]{2,1,0:T(8,128)(2,1)S(1)}, u32[]{:S(2)}, u32[]{:S(2)}) async-start(bf16[8,48,128]{2,1,0:T(8,128)(2,1)} %shard_map.140), calls=%async_computation | async-start | bytes 196608 | tf_op jit(solution)/shard_map/all_to_all | solution.py:438
  10.9 22.2 %copy-start.3 = (f32[2,64,192]{2,1,0:T(8,128)S(1)}, f32[2,64,192]{2,1,0:T(8,128)}, u32[]{:S(2)}) copy-start(f32[2,64,192]{2,1,0:T(8,128)} %coeffs_ref.1) | copy-start | bytes 294916
  10.9 22.2 %copy-start.8 = (s32[512]{0:T(512)S(1)}, s32[512]{0:T(512)}, u32[]{:S(2)}) copy-start(s32[512]{0:T(512)} %param.15) | copy-start | bytes 6148
  10.9 22.2 %copy-start.9 = (s32[64]{0:T(128)S(1)}, s32[64]{0:T(128)}, u32[]{:S(2)}) copy-start(s32[64]{0:T(128)} %param.16) | copy-start | bytes 772
  10.9 33.7 %copy-start = (bf16[512,16,192]{0,2,1:T(8,128)(2,1)S(1)}, bf16[512,16,192]{0,2,1:T(8,128)(2,1)}, u32[]{:S(2)}) copy-start(bf16[512,16,192]{0,2,1:T(8,128)(2,1)} %param.17) | copy-start | bytes 9437188
  10.9 33.7 %copy-start.5 = (bf16[256,256]{1,0:T(8,128)(2,1)S(1)}, bf16[256,256]{1,0:T(8,128)(2,1)}, u32[]{:S(2)}) copy-start(bf16[256,256]{1,0:T(8,128)(2,1)} %constant.20.clone.order_ref) | copy-start | bytes 393220
  13.2 19.9 %copy-start.1 = (bf16[384,1024]{1,0:T(8,128)(2,1)S(1)}, bf16[384,1024]{1,0:T(8,128)(2,1)}, u32[]{:S(2)}) copy-start(bf16[384,1024]{1,0:T(8,128)(2,1)} %constant.19.clone.low_ref) | copy-start | bytes 2359300
  13.2 19.9 %copy-start.2 = (bf16[384,1024]{1,0:T(8,128)(2,1)S(1)}, bf16[384,1024]{1,0:T(8,128)(2,1)}, u32[]{:S(2)}) copy-start(bf16[384,1024]{1,0:T(8,128)(2,1)} %constant.18.clone.high_ref) | copy-start | bytes 2359300
  13.2 31.4 %copy-start.6 = (bf16[192,192]{1,0:T(8,128)(2,1)S(1)}, bf16[192,192]{1,0:T(8,128)(2,1)}, u32[]{:S(2)}) copy-start(bf16[192,192]{1,0:T(8,128)(2,1)} %constant.21.clone.swap_ref) | copy-start | bytes 221188
  25.3 29.3 %copy-start.4 = (f32[256,16]{1,0:T(8,128)S(1)}, f32[256,16]{1,0:T(8,128)}, u32[]{:S(2)}) copy-start(f32[256,16]{1,0:T(8,128)} %constant.23.clone.fold_ref) | copy-start | bytes 49156
  25.3 29.3 %copy-start.7 = (f32[16,256]{1,0:T(8,128)S(1)}, f32[16,256]{1,0:T(8,128)}, u32[]{:S(2)}) copy-start(f32[16,256]{1,0:T(8,128)} %constant.22.clone.keep_ref) | copy-start | bytes 49156

commit v6 on v5

--- a/solution.py
+++ b/solution.py
@@ -12,7 +12,7 @@
 F32 = jnp.float32
 BF16 = jnp.bfloat16
 LANES = 128
-GROUP = 12
+GROUP = 24
 BLOCK = 16
 ALL_VMEM = 62 * 2**20
 MOST_VMEM = 53 * 2**20
@@ -53,9 +53,13 @@
 def plane_tables(grid, half):
     theta = angles(grid, half)
     wide = 2 * LANES
+    lane = np.arange(LANES)
+    mirrored = lane >= grid // 2
+    half_step = np.where(mirrored, lane - (LANES - grid // 2), lane) + 0.5
+    half_step = np.outer(half_step, np.arange(half) - half // 2) * (2.0 * math.pi / grid)
     table_y = np.zeros((2, LANES, wide), np.float32)
-    table_y[0, : grid // 2 + 1, :half] = np.cos(theta[: grid // 2 + 1])
-    table_y[1, 1 : grid // 2, :half] = np.sin(theta[1 : grid // 2])
+    table_y[0, :, :half] = np.cos(half_step)
+    table_y[1, :, :half] = np.sin(half_step) * np.where(mirrored, -1.0, 1.0)[:, None]
     cosine, sine = np.cos(theta), np.sin(theta)
     table_x = np.block([[cosine, -sine], [sine, cosine]])
     padded = np.zeros((2 * grid, wide), np.float32)
@@ -83,9 +87,19 @@
 
 
 def to_column(row, count):
-    shape = (count, row.shape[1])
-    square = jnp.broadcast_to(row, shape)
-    return jnp.sum(jnp.where(lane_iota(shape) == row_iota(shape), square, 0.0), axis=1, keepdims=True)
+    if row.shape[1] < LANES:
+        row = jnp.concatenate([row] * (LANES // row.shape[1]), 1)
+    return jnp.broadcast_to(row, (8, row.shape[1])).T[:count, :1]
+
+
+def cosine_sine(angle):
+    square = angle * angle
+    cosine, sine = 0.0, 0.0
+    for n in range(6, 0, -1):
+        cosine = (cosine + (-1.0) ** n / math.factorial(2 * n)) * square
+    for n in range(5, 0, -1):
+        sine = (sine + (-1.0) ** n / math.factorial(2 * n + 1)) * square
+    return 1.0 + cosine, angle * (1.0 + sine)
 
 
 def slot_freq(shape, half):
@@ -106,27 +120,46 @@
     return copies
 
 
-def z_forward_kernel(coeffs_hbm, length_hbm, table_hbm, out_ref, coeffs_ref, length_ref, table_ref, sem):
+def own_column(column_ref):
+    me = lax.axis_index("fft")
+    at_me = row_iota(column_ref.shape) == me // 2
+    column = jnp.sum(jnp.where(at_me, column_ref[...].astype(F32), 0.0), axis=0, keepdims=True)
+    other = pltpu.roll(column, LANES // 2, 1)
+    return jnp.where((lane_iota(column.shape) < LANES // 2) == (me % 2 == 0), column, other)
+
+
+def turn_angle(column, half, grid):
+    y_freq = column - jnp.floor((column + 0.5) * (1.0 / half)) * half - half // 2
+    return y_freq * (math.pi / grid)
+
+
+def z_forward_kernel(
+    column_hbm, coeffs_hbm, length_hbm, table_hbm, out_ref, column_ref, coeffs_ref, length_ref, table_ref, sem
+):
     copies = start_all(
         pltpu.make_async_copy(length_hbm, length_ref, sem.at[0]),
-        pltpu.make_async_copy(coeffs_hbm, coeffs_ref, sem.at[1]),
-        pltpu.make_async_copy(table_hbm, table_ref, sem.at[2]),
+        pltpu.make_async_copy(column_hbm, column_ref, sem.at[1]),
+        pltpu.make_async_copy(coeffs_hbm, coeffs_ref, sem.at[2]),
+        pltpu.make_async_copy(table_hbm, table_ref, sem.at[3]),
     )
     bands, sticks, width = coeffs_ref.shape
     grid = table_ref.shape[0] // 4
     parts = out_ref.shape[0]
     depth = grid // parts
     copies[0].wait()
+    copies[1].wait()
+    cosine, sine = cosine_sine(turn_angle(own_column(column_ref), width // 2, grid))
     live = live_slots(length_ref[...], width // 2)
-    copies[1].wait()
+    copies[2].wait()
     masked = jnp.concatenate([jnp.where(live, coeffs_ref[b], 0.0) for b in range(bands)], 0)
     c_high = masked.astype(BF16)
     c_low = (masked - c_high.astype(F32)).astype(BF16)
     nt = ((1,), (1,))
-    copies[2].wait()
+    copies[3].wait()
     high, low = table_ref[: 2 * grid], table_ref[2 * grid :]
     sums = dot(high, c_high, nt) + dot(high, c_low, nt) + dot(low, c_high, nt)
     real, imag = sums[:grid], sums[grid:]
+    real, imag = real * cosine + imag * sine, imag * cosine - real * sine
     first = lane_iota(real.shape) < sticks
     values = [
         jnp.where(first, real, pltpu.roll(imag, sticks, 1)),
@@ -137,7 +170,7 @@
         out_ref[part] = jnp.concatenate(rows, 0).astype(BF16)
 
 
-def tables_kernel(grid, half, column_hbm, const_hbm, out_ref, column_ref, y_ref, sem):
+def tables_kernel(grid, half, column_hbm, const_hbm, out_hbm, table_ref, column_ref, y_ref, sem):
     wide = 2 * LANES
     n = column_ref.shape[0] * LANES
     tiles = n // wide
@@ -145,8 +178,12 @@
     copies = start_all(
         pltpu.make_async_copy(column_hbm, column_ref, sem.at[0]),
         pltpu.make_async_copy(const_hbm.at[:wide], y_ref, sem.at[1]),
-        pltpu.make_async_copy(const_hbm.at[wide:], out_ref.at[x_at:end], sem.at[2]),
-    )
+        pltpu.make_async_copy(const_hbm.at[wide:], table_ref.at[x_at:end], sem.at[2]),
+    )
+
+    def send(first, last, i):
+        return start_all(pltpu.make_async_copy(table_ref.at[first:last], out_hbm.at[first:last], sem.at[i]))[0]
+
     copies[0].wait()
     column = column_ref[...].astype(F32)
     column = jnp.concatenate([column[i : i + 1] for i in range(column.shape[0])], 1)
@@ -155,21 +192,27 @@
     key = x_pos * n + lane_iota(column.shape).astype(F32)
     rank = jnp.sum(jnp.where(to_column(key, n) < key, 1.0, 0.0), axis=0, keepdims=True)
     sort = jnp.where(row_iota((n, n)).astype(F32) == rank, 1.0, 0.0).astype(BF16)
+    for tile in range(tiles):
+        at = slice(tile * wide, (tile + 1) * wide)
+        table_ref[sort_at + tile * n : sort_at + (tile + 1) * n] = sort[:, at]
+    copies[1].wait()
+    copies[2].wait()
+    sent = [send(sort_at, mask_at, 3), send(x_at, end, 4)]
     nt = ((1,), (1,))
     index = row_iota((half, n)).astype(F32)
     at_x = jnp.where(index == x_pos, 1.0, 0.0).astype(BF16)
     at_y = jnp.where(index == y_pos, 1.0, 0.0).astype(BF16)
     mask = dot(at_x, sort, nt).astype(BF16)
     at_y = dot(at_y, sort, nt).astype(BF16)
-    copies[1].wait()
     back = dot(y_ref[:, :half], at_y)
     for tile in range(tiles):
         at = slice(tile * wide, (tile + 1) * wide)
-        out_ref[sort_at + tile * n : sort_at + (tile + 1) * n] = sort[:, at]
-        out_ref[mask_at + tile * half : mask_at + (tile + 1) * half] = mask[:, at]
-        out_ref[forward_at + tile * wide : forward_at + (tile + 1) * wide] = back[:, at].T.astype(BF16)
-        out_ref[back_at + tile * wide : back_at + (tile + 1) * wide] = back[:, at].astype(BF16)
-    copies[2].wait()
+        table_ref[mask_at + tile * half : mask_at + (tile + 1) * half] = mask[:, at]
+        table_ref[forward_at + tile * wide : forward_at + (tile + 1) * wide] = back[:, at].T.astype(BF16)
+        table_ref[back_at + tile * wide : back_at + (tile + 1) * wide] = back[:, at].astype(BF16)
+    sent.append(send(mask_at, x_at, 5))
+    for copy in sent:
+        copy.wait()
 
 
 def planes_kernel(
@@ -184,8 +227,8 @@
     tiles = value_ref.shape[1]
     n_sticks = tiles * wide
     bands = rows // planes
-    pairs = y_buf.shape[0]
-    group = pairs // bands
+    group = 2 * y_buf.shape[0]
+    pairs = group * bands
     steps = planes // group
     sort_at, mask_at, forward_at, back_at, x_at, turned_at, _ = table_rows(grid, half, n_sticks)
     sources = [
@@ -252,19 +295,28 @@
     table_x = table_ref[x_at:turned_at, : 2 * half]
     table_xt = [table_ref[turned_at + 2 * half * i : turned_at + 2 * half * (i + 1)] for i in range(2)]
     table_xt = jnp.concatenate(table_xt, 1)[:, : 2 * grid]
+    assert bands == 2 and 4 * (LANES - grid // 2) == LANES
+    middle = LANES // 2
+
+    def pack(b0, b0_mirror, b1, b1_mirror):
+        low = lane_iota(b0.shape) < middle
+        return [b0, b1, jnp.where(low, b0_mirror, pltpu.roll(b1_mirror, middle, 1))]
+
+    def mirrors(shared):
+        low = lane_iota(shared.shape) < middle
+        return [jnp.where(low, shared, 0.0), jnp.where(low, pltpu.roll(shared, middle, 1), 0.0)]
+
     lane = lane_iota((grid, LANES))
-    low_at = jnp.clip(grid - LANES - lane, 0, LANES - 1)
-    high_at = jnp.clip(grid - lane, 0, LANES - 1)
-
-    def mirrored_potential(z):
+    source = jnp.where(lane < middle, lane, lane - (LANES - grid // 2))
+    mirrored = (grid - 1 - source) & (LANES - 1)
+
+    def packed_potential(z):
         near = pot_ref[z, :, :LANES]
         far = pot_ref[z, :, LANES:]
         far = jnp.concatenate([far, jnp.zeros((grid, 2 * LANES - grid), F32)], 1)
-        from_far = jnp.take_along_axis(far, low_at, axis=1)
-        from_near = jnp.take_along_axis(near, high_at, axis=1)
-        back = jnp.where(lane <= grid - LANES, from_far, from_near)
-        back = jnp.where((lane > 0) & (lane < grid // 2), back, 0.0)
-        return jnp.concatenate([jnp.where(lane <= grid // 2, near, 0.0), back], 1)
+        mirror = jnp.take_along_axis(jnp.where(lane < middle, far, near), mirrored, axis=1)
+        own = jnp.where(lane < grid // 2, near, mirror)
+        return jnp.concatenate(pack(own, mirror, own, mirror), 1)
 
     def at_pair(i, c):
         return slice((c * pairs + i) * block, (c * pairs + i + 1) * block)
@@ -285,30 +337,40 @@
                         row = value_ref[c, tile, pl.ds(b * planes + step * group + p, 1), :]
                         placed.append(mask * row.astype(BF16))
             spread_buf[i] = dot(jnp.concatenate(placed, 0), tile_at(forward_at, tile))
-        for i in range(pairs):
+        for p in range(group):
+            at = slice(p % 2 * 3 * LANES, (p % 2 + 1) * 3 * LANES)
             for g in range(blocks):
-                real, imag = spread_at(g, i, 0), spread_at(g, i, 1)
-                rc, rs, ic, si = real[:, :LANES], real[:, LANES:], imag[:, :LANES], imag[:, LANES:]
-                y_re = jnp.concatenate([rc - si, rc + si], 1).astype(BF16)
-                y_im = jnp.concatenate([ic + rs, ic - rs], 1).astype(BF16)
-                y_buf[i, g * block : (g + 1) * block] = y_re
-                y_buf[i, half + g * block : half + (g + 1) * block] = y_im
+                real, imag = [], []
+                for b in range(bands):
+                    re, im = spread_at(g, p * bands + b, 0), spread_at(g, p * bands + b, 1)
+                    rc, rs, ic, si = re[:, :LANES], re[:, LANES:], im[:, :LANES], im[:, LANES:]
+                    real += [rc - si, rc + si]
+                    imag += [ic + rs, ic - rs]
+                y_buf[p // 2, g * block : (g + 1) * block, at] = jnp.concatenate(pack(*real), 1).astype(BF16)
+                y_buf[p // 2, half + g * block : half + (g + 1) * block, at] = jnp.concatenate(pack(*imag), 1).astype(BF16)
         copies[n_small + step].wait()
-        for p in range(group):
-            weight = mirrored_potential(step * group + p)
-            for i in range(p * bands, (p + 1) * bands):
-                field = dot(table_x, y_buf[i])
-                p_buf[i, :grid] = (field[:grid] * weight).astype(BF16)
-                p_buf[i, grid:] = (field[grid:] * weight).astype(BF16)
-        for i in range(pairs):
-            both = dot(table_xt, p_buf[i])
-            q_re, q_im = both[:half], both[half:]
-            rp, rm, ip, im = q_re[:, :LANES], q_re[:, LANES:], q_im[:, :LANES], q_im[:, LANES:]
-            real = jnp.concatenate([rp + rm, ip - im], 1).astype(BF16)
-            imag = jnp.concatenate([ip + im, rm - rp], 1).astype(BF16)
-            for g in range(blocks):
-                q_buf[g, at_pair(i, 0)] = real[g * block : (g + 1) * block]
-                q_buf[g, at_pair(i, 1)] = imag[g * block : (g + 1) * block]
+        for p in range(0, group, 2):
+            weight = [packed_potential(step * group + p + i) for i in range(2)]
+            weight = jnp.concatenate(weight, 1)
+            field = dot(table_x, y_buf[p // 2])
+            p_buf[p // 2, :grid] = (field[:grid] * weight).astype(BF16)
+            p_buf[p // 2, grid:] = (field[grid:] * weight).astype(BF16)
+        for p in range(0, group, 2):
+            both = dot(table_xt, p_buf[p // 2])
+            for i in range(2):
+                tiles_at = [slice((3 * i + k) * LANES, (3 * i + k + 1) * LANES) for k in range(3)]
+                real = [both[:half, at] for at in tiles_at]
+                imag = [both[half:, at] for at in tiles_at]
+                real_mirrors, imag_mirrors = mirrors(real[bands]), mirrors(imag[bands])
+                for b in range(bands):
+                    rp, rm = real[b], real_mirrors[b]
+                    ip, im = imag[b], imag_mirrors[b]
+                    folded_re = jnp.concatenate([rp + rm, ip - im], 1).astype(BF16)
+                    folded_im = jnp.concatenate([ip + im, rm - rp], 1).astype(BF16)
+                    for g in range(blocks):
+                        at = slice(g * block, (g + 1) * block)
+                        q_buf[g, at_pair((p + i) * bands + b, 0)] = folded_re[at]
+                        q_buf[g, at_pair((p + i) * bands + b, 1)] = folded_im[at]
         sums = [0.0] * tiles
         for tile, g in runs:
             full = dot(q_buf[g], tile_at(back_at, tile)).reshape(2 * pairs, block // 8, 8, wide)
@@ -333,16 +395,16 @@
         out_ref[2 * pair + 1] = odd.astype(BF16)
 
 
-def z_backward_kernel(norm, recv_ref, coeffs_ref, length_ref, column_ref, high_ref, low_ref, applied_ref, send_ref):
+def z_backward_kernel(grid, recv_ref, coeffs_ref, length_ref, column_ref, high_ref, low_ref, applied_ref, send_ref):
+    norm = 1.0 / float(grid) ** 3
     bands, sticks, width = coeffs_ref.shape
     half = width // 2
     wide = 2 * LANES
     owners, _, own_sticks, _ = send_ref.shape
-    me = lax.axis_index("fft")
-    at_me = row_iota(column_ref.shape) == me // 2
-    column = jnp.sum(jnp.where(at_me, column_ref[...].astype(F32), 0.0), axis=0, keepdims=True)
-    column = jnp.where(me % 2 == 1, pltpu.roll(column, LANES // 2, 1), column)[:, :sticks]
+    column = own_column(column_ref)
     column = to_column(column, sticks)
+    cosine, sine = cosine_sine(turn_angle(column, half, grid))
+    cosine, sine = cosine * norm, sine * norm
     x_pos = jnp.floor((column + 0.5) * (1.0 / half))
     x_freq = x_pos - half // 2
     y_freq = column - x_pos * half - half // 2
@@ -352,10 +414,12 @@
     values = recv_ref[...].astype(F32).reshape(-1, LANES).T.astype(BF16)
     sums = dot(values, high_ref[...]) + dot(values, low_ref[...])
     for b in range(bands):
-        real_at = b * wide
-        imag_at = (bands + b) * wide
-        local = sums[:sticks, real_at : real_at + wide] + sums[sticks:, imag_at : imag_at + wide]
-        h = jnp.where(live, kinetic * coeffs_ref[b] + local[:, :width] * norm, 0.0)
+        at = slice(b * wide, (b + 1) * wide)
+        at_turned = slice((bands + b) * wide, (bands + b + 1) * wide)
+        local = sums[:sticks, at] + sums[sticks:, at_turned]
+        turned = sums[:sticks, at_turned] - sums[sticks:, at]
+        local = (local * cosine + turned * sine)[:, :width]
+        h = jnp.where(live, kinetic * coeffs_ref[b] + local, 0.0)
         applied_ref[b] = h.astype(BF16)
         for r in range(owners):
             send_ref[r, b] = h[r * own_sticks : (r + 1) * own_sticks].astype(BF16)
@@ -423,16 +487,18 @@
     sent = call(
         z_forward_kernel,
         exchanged,
+        columns,
         band_coeffs,
         lengths,
         z_table,
         vmem=ALL_VMEM,
-        in_specs=[in_hbm] * 3,
+        in_specs=[in_hbm] * 4,
         scratch_shapes=[
+            pltpu.VMEM(columns.shape, jnp.int32),
             pltpu.VMEM(band_coeffs.shape, F32),
             pltpu.VMEM(lengths.shape, jnp.int32),
             pltpu.VMEM(z_table.shape, BF16),
-            dma((3,)),
+            dma((4,)),
         ],
     )
     received = lax.all_to_all(sent, "fft", 0, 0, tiled=True)
@@ -448,10 +514,12 @@
         const,
         vmem=ALL_VMEM,
         in_specs=[in_hbm] * 2,
+        out_specs=in_hbm,
         scratch_shapes=[
+            pltpu.VMEM(table.shape, BF16),
             pltpu.VMEM(columns.shape, jnp.int32),
             pltpu.VMEM((wide, wide), BF16),
-            dma((3,)),
+            dma((6,)),
         ],
     )
     group = math.gcd(GROUP, planes)
@@ -472,8 +540,8 @@
             values,
             values,
             pltpu.VMEM((blocks + tiles - 1, 2 * pairs * BLOCK, wide), F32),
-            pltpu.VMEM((pairs, 2 * half, wide), BF16),
-            pltpu.VMEM((pairs, 2 * grid, wide), BF16),
+            pltpu.VMEM((group // 2, 2 * half, 6 * LANES), BF16),
+            pltpu.VMEM((group // 2, 2 * grid, 6 * LANES), BF16),
             pltpu.VMEM((blocks, 2 * pairs * BLOCK, wide), BF16),
             dma((3 + planes // group,)),
         ],
@@ -481,7 +549,7 @@
     received = lax.all_to_all(sent, "fft", 0, 0, tiled=True)
 
     applied, sent = call(
-        functools.partial(z_backward_kernel, 1.0 / float(grid) ** 3),
+        functools.partial(z_backward_kernel, grid),
         (shape((bands, sticks, width), BF16), shape((n_band, bands, own_sticks, width), BF16)),
         received,
         band_coeffs,

time: 55.8 us -> 55.5 us (level)
  no operation moved by 1% of the time
where the time goes in v6:
time: 55.5 us; the launch traced here: 55.2 us
  blocking collectives  27.1 us (49%)
  Pallas kernels  19.7 us (35%)
  starting transfers between devices  5.18 us (9%)
  waiting for transfers between devices  2.39 us (4%)
  between operations  0.74 us (1%)
    pallas_call x6, Pallas kernels, call(): pl.pallas_call(kernel, out_shape=out_shape, compiler_params=pltpu.Compile...  19.7 us
    all_to_all x1, blocking collectives, per_device(): received = lax.all_to_all(sent, 'band', 0, 0, tiled=True)  10.4 us
    all_to_all x1, blocking collectives, per_device(): received = lax.all_to_all(sent, ('band', 'fft'), 0, 0, tiled=True)  8.95 us
    all_to_all x1, blocking collectives, per_device(): received = lax.all_to_all(sent, 'fft', 0, 0, tiled=True)  7.71 us
    all_to_all x1, starting transfers between devices, per_device(): received = lax.all_to_all(sent, 'fft', 0, 0, tiled=True)  5.18 us
    all_to_all x1, waiting for transfers between devices, per_device(): received = lax.all_to_all(sent, 'fft', 0, 0, tiled=True)  2.39 us
  transfers between devices with their start and end apart: 1, of which 1 were waited for; matrix products, arithmetic and copies ran while one was open for 0% of the time, Pallas kernels for 5%

profile of v6, /device:TPU:0, one launch (start us, length us, event | category | flops | bytes accessed | tf_op | source)
XLA Modules:
  0.0 55.2 jit_solution(18049754199233046332)
XLA Ops:
  0.6 2.2 %shard_map.140 = bf16[8,48,128]{2,1,0:T(8,128)(2,1)} custom-call(s32[4,128]{1,0:T(4,128)} %bitcast.4, f32[2,64,192]{2,1,0:T(8,128)} %coeffs_ref.1, s32[1,64]{1,0:T(1,128)} %bitcast.7, bf16[768,192]{1,0:T(8,128)(2,1)} %constant.16.clone.table_hbm), custom_call_target="tpu_custom_call" | custom-call | tf_op jit(solution)/shard_map/pallas_call | solution.py:463
  2.8 5.2 %all-to-all-start = ((bf16[8,48,128]{2,1,0:T(8,128)(2,1)}), bf16[8,48,128]{2,1,0:T(8,128)(2,1)S(1)}, u32[]{:S(2)}, u32[]{:S(2)}) async-start(bf16[8,48,128]{2,1,0:T(8,128)(2,1)} %shard_map.140), calls=%async_computation | async-start | bytes 196608 | tf_op jit(solution)/shard_map/all_to_all | solution.py:504
  8.0 2.7 %shard_map.141.table_hbm = bf16[3008,256]{1,0:T(8,128)(2,1)} custom-call(s32[4,128]{1,0:T(4,128)} %bitcast.5, bf16[1024,256]{1,0:T(8,128)(2,1)} %constant.17.clone.const_hbm), custom_call_target="tpu_custom_call" | custom-call | tf_op jit(solution)/shard_map/pallas_call | solution.py:463
  10.7 0.0 copy-start.3
  10.7 0.0 copy-start.7
  10.8 0.0 copy-start.9
  10.8 0.0 copy-start
  10.8 0.0 copy-start.5
  10.8 2.4 %all-to-all-done.recv_hbm = bf16[8,48,128]{2,1,0:T(8,128)(2,1)S(1)} async-done(((bf16[8,48,128]{2,1,0:T(8,128)(2,1)}), bf16[8,48,128]{2,1,0:T(8,128)(2,1)S(1)}, u32[]{:S(2)}, u32[]{:S(2)}) %all-to-all-start) | async-done | bytes 98336 | tf_op jit(solution)/shard_map/all_to_all | solution.py:504
  13.2 0.0 copy-start.1
  13.2 0.0 copy-start.2
  13.2 0.0 copy-start.6
  13.2 11.8 %shard_map.142 = bf16[8,48,128]{2,1,0:T(8,128)(2,1)S(1)} custom-call(bf16[8,48,128]{2,1,0:T(8,128)(2,1)S(1)} %all-to-all-done.recv_hbm, bf16[3008,256]{1,0:T(8,128)(2,1)} %shard_map.141.table_hbm, f32[24,192,192]{2,1,0:T(8,128)} %pot_hbm.1), custom_call_target="tpu_custom_call" | custom-call | tf_op jit(solution)/shard_map/pallas_call | solution.py:463
  25.0 0.0 copy-start.4
  25.0 0.0 copy-start.8
  25.0 7.7 %all_to_all.20.recv_ref = bf16[8,48,128]{2,1,0:T(8,128)(2,1)S(1)} all-to-all(bf16[8,48,128]{2,1,0:T(8,128)(2,1)S(1)} %shard_map.142), channel_id=1, replica_groups=mesh['band'=4,'fft'=8] {'fft'}, dimensions={0} | all-to-all | bytes 196608 | tf_op jit(solution)/shard_map/all_to_all | solution.py:549
  32.7 0.0 copy-done.3
  32.7 0.0 copy-done.7
  32.7 0.0 copy-done.9
  32.8 0.0 copy-done.1
  32.8 0.0 copy-done.2
  32.8 1.1 %shard_map.143 = (bf16[2,64,192]{2,1,0:T(8,128)(2,1)}, bf16[4,2,16,192]{3,2,1,0:T(8,128)(2,1)S(1)}) custom-call(bf16[8,48,128]{2,1,0:T(8,128)(2,1)S(1)} %all_to_all.20.recv_ref, f32[2,64,192]{2,1,0:T(8,128)S(1)} %copy-done.3, s32[1,64]{1,0:T(1,128)S(1)} %bitcast.8, s32[4,128]{1,0:T(4,128)S(1)} %bitcast.6, bf16[384,1024]{1,0:T(8,128)(2,1)S(1)} %copy-done.2, ...), custom_call_target="tpu_custom_call" | custom-call | tf_op jit(solution)/shard_map/pallas_call | solution.py:463
  33.9 10.4 %all_to_all.21.recv_ref = bf16[4,2,16,192]{3,2,1,0:T(8,128)(2,1)S(1)} all-to-all(bf16[4,2,16,192]{3,2,1,0:T(8,128)(2,1)S(1)} %get-tuple-element.5), channel_id=1, replica_groups=mesh['band'=4,'fft'=8] {'band'}, dimensions={0} | all-to-all | bytes 98304 | tf_op jit(solution)/shard_map/all_to_all | solution.py:560
  44.3 0.0 copy-done
  44.3 0.0 copy-done.5
  44.3 0.0 copy-done.6
  44.3 1.1 %shard_map.144 = f32[32,2,128]{2,1,0:T(2,128)S(1)} custom-call(bf16[4,2,16,192]{3,2,1,0:T(8,128)(2,1)S(1)} %all_to_all.21.recv_ref, bf16[16,192,512]{2,1,0:T(8,128)(2,1)S(1)} %bitcast.3, bf16[256,256]{1,0:T(8,128)(2,1)S(1)} %copy-done.5, bf16[192,192]{1,0:T(8,128)(2,1)S(1)} %copy-done.6), custom_call_target="tpu_custom_call" | custom-call | tf_op jit(solution)/shard_map/pallas_call | solution.py:463
  45.4 8.9 %all_to_all.22.recv_ref = f32[32,2,128]{2,1,0:T(2,128)S(1)} all-to-all(f32[32,2,128]{2,1,0:T(2,128)S(1)} %shard_map.144), channel_id=1, replica_groups=mesh['band'=4,'fft'=8] {'band','fft'}, dimensions={0} | all-to-all | bytes 65536 | tf_op jit(solution)/shard_map/all_to_all | solution.py:583
  54.4 0.0 copy-done.4
  54.4 0.0 copy-done.8
  54.4 0.8 %shard_map.145 = f32[16,16]{1,0:T(8,128)} custom-call(f32[32,2,128]{2,1,0:T(2,128)S(1)} %all_to_all.22.recv_ref, f32[16,256]{1,0:T(8,128)S(1)} %copy-done.8, f32[256,16]{1,0:T(8,128)S(1)} %copy-done.4), custom_call_target="tpu_custom_call" | custom-call | tf_op jit(solution)/shard_map/pallas_call | solution.py:463
Async XLA Ops:
  2.8 10.4 %all-to-all-start = ((bf16[8,48,128]{2,1,0:T(8,128)(2,1)}), bf16[8,48,128]{2,1,0:T(8,128)(2,1)S(1)}, u32[]{:S(2)}, u32[]{:S(2)}) async-start(bf16[8,48,128]{2,1,0:T(8,128)(2,1)} %shard_map.140), calls=%async_computation | async-start | bytes 196608 | tf_op jit(solution)/shard_map/all_to_all | solution.py:504
  10.7 22.0 %copy-start.3 = (f32[2,64,192]{2,1,0:T(8,128)S(1)}, f32[2,64,192]{2,1,0:T(8,128)}, u32[]{:S(2)}) copy-start(f32[2,64,192]{2,1,0:T(8,128)} %coeffs_ref.1) | copy-start | bytes 294916
  10.7 22.0 %copy-start.7 = (s32[512]{0:T(512)S(1)}, s32[512]{0:T(512)}, u32[]{:S(2)}) copy-start(s32[512]{0:T(512)} %param.15) | copy-start | bytes 6148
  10.8 22.0 %copy-start.9 = (s32[64]{0:T(128)S(1)}, s32[64]{0:T(128)}, u32[]{:S(2)}) copy-start(s32[64]{0:T(128)} %param.16) | copy-start | bytes 772
  10.8 33.6 %copy-start = (bf16[512,16,192]{0,2,1:T(8,128)(2,1)S(1)}, bf16[512,16,192]{0,2,1:T(8,128)(2,1)}, u32[]{:S(2)}) copy-start(bf16[512,16,192]{0,2,1:T(8,128)(2,1)} %param.17) | copy-start | bytes 9437188
  10.8 33.5 %copy-start.5 = (bf16[256,256]{1,0:T(8,128)(2,1)S(1)}, bf16[256,256]{1,0:T(8,128)(2,1)}, u32[]{:S(2)}) copy-start(bf16[256,256]{1,0:T(8,128)(2,1)} %constant.20.clone.order_ref) | copy-start | bytes 393220
  13.2 19.6 %copy-start.1 = (bf16[384,1024]{1,0:T(8,128)(2,1)S(1)}, bf16[384,1024]{1,0:T(8,128)(2,1)}, u32[]{:S(2)}) copy-start(bf16[384,1024]{1,0:T(8,128)(2,1)} %constant.19.clone.low_ref) | copy-start | bytes 2359300
  13.2 19.6 %copy-start.2 = (bf16[384,1024]{1,0:T(8,128)(2,1)S(1)}, bf16[384,1024]{1,0:T(8,128)(2,1)}, u32[]{:S(2)}) copy-start(bf16[384,1024]{1,0:T(8,128)(2,1)} %constant.18.clone.high_ref) | copy-start | bytes 2359300
  13.2 31.1 %copy-start.6 = (bf16[192,192]{1,0:T(8,128)(2,1)S(1)}, bf16[192,192]{1,0:T(8,128)(2,1)}, u32[]{:S(2)}) copy-start(bf16[192,192]{1,0:T(8,128)(2,1)} %constant.21.clone.swap_ref) | copy-start | bytes 221188
  25.0 29.3 %copy-start.4 = (f32[256,16]{1,0:T(8,128)S(1)}, f32[256,16]{1,0:T(8,128)}, u32[]{:S(2)}) copy-start(f32[256,16]{1,0:T(8,128)} %constant.23.clone.fold_ref) | copy-start | bytes 49156
  25.0 29.3 %copy-start.8 = (f32[16,256]{1,0:T(8,128)S(1)}, f32[16,256]{1,0:T(8,128)}, u32[]{:S(2)}) copy-start(f32[16,256]{1,0:T(8,128)} %constant.22.clone.keep_ref) | copy-start | bytes 49156

commit v7 on v6

--- a/solution.py
+++ b/solution.py
@@ -12,7 +12,6 @@
 F32 = jnp.float32
 BF16 = jnp.bfloat16
 LANES = 128
-GROUP = 24
 BLOCK = 16
 ALL_VMEM = 62 * 2**20
 MOST_VMEM = 53 * 2**20
@@ -40,14 +39,12 @@
     return split_bf16(np.concatenate([rows_re, rows_im], 0).astype(np.float32))
 
 
-def z_backward_table(grid, half, bands):
+def z_backward_table(grid, half):
     theta = angles(grid, half)
-    width = 2 * LANES
-    table = np.zeros((grid, bands, 2, bands, width), np.float32)
-    for band in range(bands):
-        table[:, band, 0, band, : 2 * half] = np.concatenate([np.cos(theta), -np.sin(theta)], 1)
-        table[:, band, 1, band, : 2 * half] = np.concatenate([np.sin(theta), np.cos(theta)], 1)
-    return split_bf16(table.reshape(grid * bands, 2 * bands * width))
+    table = np.zeros((grid, 2, 2 * LANES), np.float32)
+    table[:, 0, : 2 * half] = np.concatenate([np.cos(theta), -np.sin(theta)], 1)
+    table[:, 1, : 2 * half] = np.concatenate([np.sin(theta), np.cos(theta)], 1)
+    return split_bf16(table.reshape(grid, 4 * LANES))
 
 
 def plane_tables(grid, half):
@@ -227,9 +224,7 @@
     tiles = value_ref.shape[1]
     n_sticks = tiles * wide
     bands = rows // planes
-    group = 2 * y_buf.shape[0]
-    pairs = group * bands
-    steps = planes // group
+    pairs = planes * bands
     sort_at, mask_at, forward_at, back_at, x_at, turned_at, _ = table_rows(grid, half, n_sticks)
     sources = [
         (recv_hbm, recv_ref),
@@ -237,8 +232,7 @@
         (table_hbm.at[mask_at:], table_ref.at[mask_at:]),
     ]
     n_small = len(sources)
-    for z in range(0, planes, group):
-        sources.append((pot_hbm.at[z : z + group], pot_ref.at[z : z + group]))
+    sources.append((pot_hbm, pot_ref))
     copies = start_all(*[pltpu.make_async_copy(a, b, sem.at[i]) for i, (a, b) in enumerate(sources)])
 
     def sort_tile(tile):
@@ -321,68 +315,69 @@
     def at_pair(i, c):
         return slice((c * pairs + i) * block, (c * pairs + i + 1) * block)
 
-    def spread_at(g, i, c):
-        total = 0.0
-        for t in range(tiles):
-            total = total + jnp.where(runs[g + t][0] == t, spread_buf[g + t, at_pair(i, c)], 0.0)
-        return total
-
-    for step in range(steps):
-        for i, (tile, g) in enumerate(runs):
-            mask = mask_block(tile, g)
-            placed = []
-            for c in range(2):
-                for p in range(group):
-                    for b in range(bands):
-                        row = value_ref[c, tile, pl.ds(b * planes + step * group + p, 1), :]
-                        placed.append(mask * row.astype(BF16))
-            spread_buf[i] = dot(jnp.concatenate(placed, 0), tile_at(forward_at, tile))
-        for p in range(group):
-            at = slice(p % 2 * 3 * LANES, (p % 2 + 1) * 3 * LANES)
-            for g in range(blocks):
-                real, imag = [], []
-                for b in range(bands):
-                    re, im = spread_at(g, p * bands + b, 0), spread_at(g, p * bands + b, 1)
-                    rc, rs, ic, si = re[:, :LANES], re[:, LANES:], im[:, :LANES], im[:, LANES:]
-                    real += [rc - si, rc + si]
-                    imag += [ic + rs, ic - rs]
-                y_buf[p // 2, g * block : (g + 1) * block, at] = jnp.concatenate(pack(*real), 1).astype(BF16)
-                y_buf[p // 2, half + g * block : half + (g + 1) * block, at] = jnp.concatenate(pack(*imag), 1).astype(BF16)
-        copies[n_small + step].wait()
-        for p in range(0, group, 2):
-            weight = [packed_potential(step * group + p + i) for i in range(2)]
-            weight = jnp.concatenate(weight, 1)
-            field = dot(table_x, y_buf[p // 2])
-            p_buf[p // 2, :grid] = (field[:grid] * weight).astype(BF16)
-            p_buf[p // 2, grid:] = (field[grid:] * weight).astype(BF16)
-        for p in range(0, group, 2):
-            both = dot(table_xt, p_buf[p // 2])
-            for i in range(2):
-                tiles_at = [slice((3 * i + k) * LANES, (3 * i + k + 1) * LANES) for k in range(3)]
-                real = [both[:half, at] for at in tiles_at]
-                imag = [both[half:, at] for at in tiles_at]
-                real_mirrors, imag_mirrors = mirrors(real[bands]), mirrors(imag[bands])
-                for b in range(bands):
-                    rp, rm = real[b], real_mirrors[b]
-                    ip, im = imag[b], imag_mirrors[b]
-                    folded_re = jnp.concatenate([rp + rm, ip - im], 1).astype(BF16)
-                    folded_im = jnp.concatenate([ip + im, rm - rp], 1).astype(BF16)
-                    for g in range(blocks):
-                        at = slice(g * block, (g + 1) * block)
-                        q_buf[g, at_pair((p + i) * bands + b, 0)] = folded_re[at]
-                        q_buf[g, at_pair((p + i) * bands + b, 1)] = folded_im[at]
-        sums = [0.0] * tiles
-        for tile, g in runs:
-            full = dot(q_buf[g], tile_at(back_at, tile)).reshape(2 * pairs, block // 8, 8, wide)
-            mask = mask_block(tile, g).astype(F32).reshape(block // 8, 8, wide)
-            kept = jnp.sum(full * mask[None], axis=1)
-            sums = [total + jnp.where(tile == t, kept, 0.0) for t, total in enumerate(sums)]
-        at = pl.ds(step * pairs, pairs)
-        for t, total in enumerate(sums):
-            total = jnp.sum(total, axis=1)
-            for c in range(2):
-                sums_ref[c, t, at] = total[c * pairs : (c + 1) * pairs]
-
+    def spread_at(slot, i, c):
+        return spread_buf[slot, at_pair(i, c)]
+
+    for i, (tile, g) in enumerate(runs):
+        mask = mask_block(tile, g)
+        placed = []
+        for c in range(2):
+            for i_pair in range(pairs):
+                placed.append(mask * value_ref[c, tile, pl.ds(i_pair, 1), :].astype(BF16))
+        spread_buf[i] = dot(jnp.concatenate(placed, 0), tile_at(forward_at, tile))
+    for start in starts:
+        spread_buf[start] = spread_buf[start] + spread_buf[start - 1]
+    last = []
+    for g in range(blocks):
+        slot = jnp.int32(g)
+        for t, start in enumerate(starts):
+            slot = slot + (start - (t + 1) <= g).astype(jnp.int32)
+        last.append(slot)
+    for p in range(planes):
+        at = slice(p % 2 * 3 * LANES, (p % 2 + 1) * 3 * LANES)
+        for g in range(blocks):
+            real, imag = [], []
+            for b in range(bands):
+                re, im = spread_at(last[g], b * planes + p, 0), spread_at(last[g], b * planes + p, 1)
+                rc, rs, ic, si = re[:, :LANES], re[:, LANES:], im[:, :LANES], im[:, LANES:]
+                real += [rc - si, rc + si]
+                imag += [ic + rs, ic - rs]
+            y_buf[p // 2, g * block : (g + 1) * block, at] = jnp.concatenate(pack(*real), 1).astype(BF16)
+            y_buf[p // 2, half + g * block : half + (g + 1) * block, at] = jnp.concatenate(pack(*imag), 1).astype(BF16)
+    copies[n_small].wait()
+    for p in range(0, planes, 2):
+        weight = [packed_potential(p + i) for i in range(2)]
+        weight = jnp.concatenate(weight, 1)
+        field = dot(table_x, y_buf[p // 2])
+        p_buf[p // 2, :grid] = (field[:grid] * weight).astype(BF16)
+        p_buf[p // 2, grid:] = (field[grid:] * weight).astype(BF16)
+    for p in range(0, planes, 2):
+        both = dot(table_xt, p_buf[p // 2])
+        for i in range(2):
+            tiles_at = [slice((3 * i + k) * LANES, (3 * i + k + 1) * LANES) for k in range(3)]
+            real = [both[:half, at] for at in tiles_at]
+            imag = [both[half:, at] for at in tiles_at]
+            real_mirrors, imag_mirrors = mirrors(real[bands]), mirrors(imag[bands])
+            for b in range(bands):
+                rp, rm = real[b], real_mirrors[b]
+                ip, im = imag[b], imag_mirrors[b]
+                folded_re = jnp.concatenate([rp + rm, ip - im], 1).astype(BF16)
+                folded_im = jnp.concatenate([ip + im, rm - rp], 1).astype(BF16)
+                for g in range(blocks):
+                    at = slice(g * block, (g + 1) * block)
+                    q_buf[g, at_pair(b * planes + p + i, 0)] = folded_re[at]
+                    q_buf[g, at_pair(b * planes + p + i, 1)] = folded_im[at]
+    for i, (tile, g) in enumerate(runs):
+        full = dot(q_buf[g], tile_at(back_at, tile)).reshape(2 * pairs, block // 8, 8, wide)
+        mask = mask_block(tile, g).astype(F32).reshape(block // 8, 8, wide)
+        kept = jnp.sum(full * mask[None], axis=1).reshape(2 * pairs * 8, wide)
+        if i:
+            kept = kept + jnp.where(tile == runs[i - 1][0], spread_buf[i - 1, : 2 * pairs * 8], 0.0)
+        spread_buf[i, : 2 * pairs * 8] = kept
+    for t, end in enumerate([*starts, blocks + tiles - 1]):
+        total = jnp.sum(spread_buf[end - 1, : 2 * pairs * 8].reshape(2 * pairs, 8, wide), axis=1)
+        for c in range(2):
+            sums_ref[c, t] = total[c * pairs : (c + 1) * pairs]
     natural = []
     for c in range(2):
         values = jnp.concatenate([sums_ref[c, tile] for tile in range(tiles)], 1)
@@ -411,23 +406,34 @@
     z_freq = slot_freq((sticks, width), half)
     kinetic = (x_freq * x_freq + y_freq * y_freq + z_freq * z_freq) * (2.0 / (half * half))
     live = live_slots(length_ref[...], half)
-    values = recv_ref[...].astype(F32).reshape(-1, LANES).T.astype(BF16)
-    sums = dot(values, high_ref[...]) + dot(values, low_ref[...])
+    planes = recv_ref.shape[1] // bands
+    received = [recv_ref[i].astype(F32) for i in range(recv_ref.shape[0])]
+    results = []
     for b in range(bands):
-        at = slice(b * wide, (b + 1) * wide)
-        at_turned = slice((bands + b) * wide, (bands + b + 1) * wide)
-        local = sums[:sticks, at] + sums[sticks:, at_turned]
-        turned = sums[:sticks, at_turned] - sums[sticks:, at]
+        values = jnp.concatenate([v[b * planes : (b + 1) * planes] for v in received], 0).T.astype(BF16)
+        sums = dot(values, high_ref[...]) + dot(values, low_ref[...])
+        local = sums[:sticks, :wide] + sums[sticks:, wide:]
+        turned = sums[:sticks, wide:] - sums[sticks:, :wide]
         local = (local * cosine + turned * sine)[:, :width]
         h = jnp.where(live, kinetic * coeffs_ref[b] + local, 0.0)
         applied_ref[b] = h.astype(BF16)
+        results.append(h)
+    tails = jnp.concatenate([h[:, LANES:] for h in results], 1)
+    for i, part in enumerate([h[:, :LANES] for h in results] + [tails]):
         for r in range(owners):
-            send_ref[r, b] = h[r * own_sticks : (r + 1) * own_sticks].astype(BF16)
+            send_ref[r, i] = part[r * own_sticks : (r + 1) * own_sticks].astype(BF16)
 
 
 def margin_kernel(recv_ref, orbitals_ref, order_ref, swap_ref, out_ref):
     own_sticks, width, n_orbitals = orbitals_ref.shape
-    h = recv_ref[...].astype(F32).reshape(-1, width).astype(BF16)
+    owners, parts = recv_ref.shape[:2]
+    tail = width - LANES
+    h = []
+    for r in range(owners):
+        tails = recv_ref[r, parts - 1].astype(F32)
+        for b in range(parts - 1):
+            h.append(jnp.concatenate([recv_ref[r, b].astype(F32), tails[:, b * tail : (b + 1) * tail]], 1))
+    h = jnp.concatenate(h, 0).astype(BF16)
     swapped = dot(h, swap_ref[...])
     both = jnp.concatenate([h.astype(F32), swapped], 0).astype(BF16)
     ordered = dot(order_ref[...], both).astype(BF16)
@@ -522,8 +528,7 @@
             dma((6,)),
         ],
     )
-    group = math.gcd(GROUP, planes)
-    pairs = group * bands
+    pairs = planes * bands
     values = pltpu.VMEM((2, tiles, bands * planes, wide), F32)
     sent = call(
         planes_kernel,
@@ -540,22 +545,22 @@
             values,
             values,
             pltpu.VMEM((blocks + tiles - 1, 2 * pairs * BLOCK, wide), F32),
-            pltpu.VMEM((group // 2, 2 * half, 6 * LANES), BF16),
-            pltpu.VMEM((group // 2, 2 * grid, 6 * LANES), BF16),
+            pltpu.VMEM((planes // 2, 2 * half, 6 * LANES), BF16),
+            pltpu.VMEM((planes // 2, 2 * grid, 6 * LANES), BF16),
             pltpu.VMEM((blocks, 2 * pairs * BLOCK, wide), BF16),
-            dma((3 + planes // group,)),
+            dma((4,)),
         ],
     )
     received = lax.all_to_all(sent, "fft", 0, 0, tiled=True)
 
     applied, sent = call(
         functools.partial(z_backward_kernel, grid),
-        (shape((bands, sticks, width), BF16), shape((n_band, bands, own_sticks, width), BF16)),
+        (shape((bands, sticks, width), BF16), shape((n_band, bands * width // LANES, own_sticks, LANES), BF16)),
         received,
         band_coeffs,
         lengths,
         columns,
-        *z_backward_table(grid, half, bands),
+        *z_backward_table(grid, half),
     )
     received = lax.all_to_all(sent, "band", 0, 0, tiled=True)
 

time: 55.5 us -> 55 us (level)
  no operation moved by 1% of the time
where the time goes in v7:
time: 55 us; the launch traced here: 54.6 us
  blocking collectives  27 us (49%)
  Pallas kernels  19.2 us (35%)
  starting transfers between devices  5.18 us (9%)
  waiting for transfers between devices  2.39 us (4%)
  between operations  0.74 us (1%)
    pallas_call x6, Pallas kernels, call(): pl.pallas_call(kernel, out_shape=out_shape, compiler_params=pltpu.Compile...  19.2 us
    all_to_all x1, blocking collectives, per_device(): received = lax.all_to_all(sent, 'band', 0, 0, tiled=True)  10.4 us
    all_to_all x1, blocking collectives, per_device(): received = lax.all_to_all(sent, ('band', 'fft'), 0, 0, tiled=True)  8.95 us
    all_to_all x1, blocking collectives, per_device(): received = lax.all_to_all(sent, 'fft', 0, 0, tiled=True)  7.71 us
    all_to_all x1, starting transfers between devices, per_device(): received = lax.all_to_all(sent, 'fft', 0, 0, tiled=True)  5.18 us
    all_to_all x1, waiting for transfers between devices, per_device(): received = lax.all_to_all(sent, 'fft', 0, 0, tiled=True)  2.39 us
  transfers between devices with their start and end apart: 1, of which 1 were waited for; matrix products, arithmetic and copies ran while one was open for 0% of the time, Pallas kernels for 5%

profile of v7, /device:TPU:0, one launch (start us, length us, event | category | flops | bytes accessed | tf_op | source)
XLA Modules:
  0.0 54.6 jit_solution(6670432271407364208)
XLA Ops:
  0.6 2.2 %shard_map.140 = bf16[8,48,128]{2,1,0:T(8,128)(2,1)} custom-call(s32[4,128]{1,0:T(4,128)} %bitcast.4, f32[2,64,192]{2,1,0:T(8,128)} %coeffs_ref.1, s32[1,64]{1,0:T(1,128)} %bitcast.7, bf16[768,192]{1,0:T(8,128)(2,1)} %constant.16.clone.table_hbm), custom_call_target="tpu_custom_call" | custom-call | tf_op jit(solution)/shard_map/pallas_call | solution.py:469
  2.8 5.2 %all-to-all-start = ((bf16[8,48,128]{2,1,0:T(8,128)(2,1)}), bf16[8,48,128]{2,1,0:T(8,128)(2,1)S(1)}, u32[]{:S(2)}, u32[]{:S(2)}) async-start(bf16[8,48,128]{2,1,0:T(8,128)(2,1)} %shard_map.140), calls=%async_computation | async-start | bytes 196608 | tf_op jit(solution)/shard_map/all_to_all | solution.py:510
  8.0 2.7 %shard_map.141.table_hbm = bf16[3008,256]{1,0:T(8,128)(2,1)} custom-call(s32[4,128]{1,0:T(4,128)} %bitcast.5, bf16[1024,256]{1,0:T(8,128)(2,1)} %constant.17.clone.const_hbm), custom_call_target="tpu_custom_call" | custom-call | tf_op jit(solution)/shard_map/pallas_call | solution.py:469
  10.7 0.0 copy-start.1
  10.7 0.0 copy-start.7
  10.8 0.0 copy-start.9
  10.8 0.0 copy-start
  10.8 0.0 copy-start.5
  10.8 2.4 %all-to-all-done.recv_hbm = bf16[8,48,128]{2,1,0:T(8,128)(2,1)S(1)} async-done(((bf16[8,48,128]{2,1,0:T(8,128)(2,1)}), bf16[8,48,128]{2,1,0:T(8,128)(2,1)S(1)}, u32[]{:S(2)}, u32[]{:S(2)}) %all-to-all-start) | async-done | bytes 98336 | tf_op jit(solution)/shard_map/all_to_all | solution.py:510
  13.2 0.0 copy-start.2
  13.2 0.0 copy-start.3
  13.2 0.0 copy-start.6
  13.2 11.3 %shard_map.142 = bf16[8,48,128]{2,1,0:T(8,128)(2,1)S(1)} custom-call(bf16[8,48,128]{2,1,0:T(8,128)(2,1)S(1)} %all-to-all-done.recv_hbm, bf16[3008,256]{1,0:T(8,128)(2,1)} %shard_map.141.table_hbm, f32[24,192,192]{2,1,0:T(8,128)} %pot_hbm.1), custom_call_target="tpu_custom_call" | custom-call | tf_op jit(solution)/shard_map/pallas_call | solution.py:469
  24.5 0.0 copy-start.4
  24.5 0.0 copy-start.8
  24.5 7.7 %all_to_all.20.recv_ref = bf16[8,48,128]{2,1,0:T(8,128)(2,1)S(1)} all-to-all(bf16[8,48,128]{2,1,0:T(8,128)(2,1)S(1)} %shard_map.142), channel_id=1, replica_groups=mesh['band'=4,'fft'=8] {'fft'}, dimensions={0} | all-to-all | bytes 196608 | tf_op jit(solution)/shard_map/all_to_all | solution.py:554
  32.2 0.0 copy-done.1
  32.2 0.0 copy-done.7
  32.2 0.0 copy-done.9
  32.2 0.0 copy-done.2
  32.3 0.0 copy-done.3
  32.3 1.1 %shard_map.143 = (bf16[2,64,192]{2,1,0:T(8,128)(2,1)}, bf16[4,3,16,128]{3,2,1,0:T(8,128)(2,1)S(1)}) custom-call(bf16[8,48,128]{2,1,0:T(8,128)(2,1)S(1)} %all_to_all.20.recv_ref, f32[2,64,192]{2,1,0:T(8,128)S(1)} %copy-done.1, s32[1,64]{1,0:T(1,128)S(1)} %bitcast.8, s32[4,128]{1,0:T(4,128)S(1)} %bitcast.6, bf16[192,512]{1,0:T(8,128)(2,1)S(1)} %copy-done.3, ...), custom_call_target="tpu_custom_call" | custom-call | tf_op jit(solution)/shard_map/pallas_call | solution.py:469
  33.3 10.4 %all_to_all.21.recv_ref = bf16[4,3,16,128]{3,2,1,0:T(8,128)(2,1)S(1)} all-to-all(bf16[4,3,16,128]{3,2,1,0:T(8,128)(2,1)S(1)} %get-tuple-element.5), channel_id=1, replica_groups=mesh['band'=4,'fft'=8] {'band'}, dimensions={0} | all-to-all | bytes 98304 | tf_op jit(solution)/shard_map/all_to_all | solution.py:565
  43.7 0.0 copy-done
  43.7 0.0 copy-done.5
  43.7 0.0 copy-done.6
  43.7 1.1 %shard_map.144 = f32[32,2,128]{2,1,0:T(2,128)S(1)} custom-call(bf16[4,3,16,128]{3,2,1,0:T(8,128)(2,1)S(1)} %all_to_all.21.recv_ref, bf16[16,192,512]{2,1,0:T(8,128)(2,1)S(1)} %bitcast.3, bf16[256,256]{1,0:T(8,128)(2,1)S(1)} %copy-done.5, bf16[192,192]{1,0:T(8,128)(2,1)S(1)} %copy-done.6), custom_call_target="tpu_custom_call" | custom-call | tf_op jit(solution)/shard_map/pallas_call | solution.py:469
  44.8 8.9 %all_to_all.22.recv_ref = f32[32,2,128]{2,1,0:T(2,128)S(1)} all-to-all(f32[32,2,128]{2,1,0:T(2,128)S(1)} %shard_map.144), channel_id=1, replica_groups=mesh['band'=4,'fft'=8] {'band','fft'}, dimensions={0} | all-to-all | bytes 65536 | tf_op jit(solution)/shard_map/all_to_all | solution.py:588
  53.8 0.0 copy-done.4
  53.8 0.0 copy-done.8
  53.8 0.8 %shard_map.145 = f32[16,16]{1,0:T(8,128)} custom-call(f32[32,2,128]{2,1,0:T(2,128)S(1)} %all_to_all.22.recv_ref, f32[16,256]{1,0:T(8,128)S(1)} %copy-done.8, f32[256,16]{1,0:T(8,128)S(1)} %copy-done.4), custom_call_target="tpu_custom_call" | custom-call | tf_op jit(solution)/shard_map/pallas_call | solution.py:469
Async XLA Ops:
  2.8 10.4 %all-to-all-start = ((bf16[8,48,128]{2,1,0:T(8,128)(2,1)}), bf16[8,48,128]{2,1,0:T(8,128)(2,1)S(1)}, u32[]{:S(2)}, u32[]{:S(2)}) async-start(bf16[8,48,128]{2,1,0:T(8,128)(2,1)} %shard_map.140), calls=%async_computation | async-start | bytes 196608 | tf_op jit(solution)/shard_map/all_to_all | solution.py:510
  10.7 21.5 %copy-start.1 = (f32[2,64,192]{2,1,0:T(8,128)S(1)}, f32[2,64,192]{2,1,0:T(8,128)}, u32[]{:S(2)}) copy-start(f32[2,64,192]{2,1,0:T(8,128)} %coeffs_ref.1) | copy-start | bytes 294916
  10.7 21.5 %copy-start.7 = (s32[512]{0:T(512)S(1)}, s32[512]{0:T(512)}, u32[]{:S(2)}) copy-start(s32[512]{0:T(512)} %param.15) | copy-start | bytes 6148
  10.8 21.5 %copy-start.9 = (s32[64]{0:T(128)S(1)}, s32[64]{0:T(128)}, u32[]{:S(2)}) copy-start(s32[64]{0:T(128)} %param.16) | copy-start | bytes 772
  10.8 32.9 %copy-start = (bf16[512,16,192]{0,2,1:T(8,128)(2,1)S(1)}, bf16[512,16,192]{0,2,1:T(8,128)(2,1)}, u32[]{:S(2)}) copy-start(bf16[512,16,192]{0,2,1:T(8,128)(2,1)} %param.17) | copy-start | bytes 9437188
  10.8 32.9 %copy-start.5 = (bf16[256,256]{1,0:T(8,128)(2,1)S(1)}, bf16[256,256]{1,0:T(8,128)(2,1)}, u32[]{:S(2)}) copy-start(bf16[256,256]{1,0:T(8,128)(2,1)} %constant.20.clone.order_ref) | copy-start | bytes 393220
  13.2 19.1 %copy-start.2 = (bf16[192,512]{1,0:T(8,128)(2,1)S(1)}, bf16[192,512]{1,0:T(8,128)(2,1)}, u32[]{:S(2)}) copy-start(bf16[192,512]{1,0:T(8,128)(2,1)} %constant.19.clone.low_ref) | copy-start | bytes 589828
  13.2 19.1 %copy-start.3 = (bf16[192,512]{1,0:T(8,128)(2,1)S(1)}, bf16[192,512]{1,0:T(8,128)(2,1)}, u32[]{:S(2)}) copy-start(bf16[192,512]{1,0:T(8,128)(2,1)} %constant.18.clone.high_ref) | copy-start | bytes 589828
  13.2 30.5 %copy-start.6 = (bf16[192,192]{1,0:T(8,128)(2,1)S(1)}, bf16[192,192]{1,0:T(8,128)(2,1)}, u32[]{:S(2)}) copy-start(bf16[192,192]{1,0:T(8,128)(2,1)} %constant.21.clone.swap_ref) | copy-start | bytes 221188
  24.5 29.3 %copy-start.4 = (f32[256,16]{1,0:T(8,128)S(1)}, f32[256,16]{1,0:T(8,128)}, u32[]{:S(2)}) copy-start(f32[256,16]{1,0:T(8,128)} %constant.23.clone.fold_ref) | copy-start | bytes 49156
  24.5 29.3 %copy-start.8 = (f32[16,256]{1,0:T(8,128)S(1)}, f32[16,256]{1,0:T(8,128)}, u32[]{:S(2)}) copy-start(f32[16,256]{1,0:T(8,128)} %constant.22.clone.keep_ref) | copy-start | bytes 49156

commit v8 on v7

--- a/solution.py
+++ b/solution.py
@@ -333,7 +333,8 @@
         for t, start in enumerate(starts):
             slot = slot + (start - (t + 1) <= g).astype(jnp.int32)
         last.append(slot)
-    for p in range(planes):
+    copies[n_small].wait()
+    def fold_in(p):
         at = slice(p % 2 * 3 * LANES, (p % 2 + 1) * 3 * LANES)
         for g in range(blocks):
             real, imag = [], []
@@ -344,13 +345,18 @@
                 imag += [ic + rs, ic - rs]
             y_buf[p // 2, g * block : (g + 1) * block, at] = jnp.concatenate(pack(*real), 1).astype(BF16)
             y_buf[p // 2, half + g * block : half + (g + 1) * block, at] = jnp.concatenate(pack(*imag), 1).astype(BF16)
-    copies[n_small].wait()
-    for p in range(0, planes, 2):
+
+    def to_space(p):
         weight = [packed_potential(p + i) for i in range(2)]
         weight = jnp.concatenate(weight, 1)
         field = dot(table_x, y_buf[p // 2])
         p_buf[p // 2, :grid] = (field[:grid] * weight).astype(BF16)
         p_buf[p // 2, grid:] = (field[grid:] * weight).astype(BF16)
+
+    for p in range(0, planes, 2):
+        fold_in(p)
+        fold_in(p + 1)
+        to_space(p)
     for p in range(0, planes, 2):
         both = dot(table_xt, p_buf[p // 2])
         for i in range(2):

time: 55 us -> 54.7 us (level)
  no operation moved by 1% of the time
where the time goes in v8:
time: 54.7 us; the launch traced here: 54.3 us
  blocking collectives  27 us (49%)
  Pallas kernels  18.9 us (35%)
  starting transfers between devices  5.18 us (9%)
  waiting for transfers between devices  2.39 us (4%)
  between operations  0.74 us (1%)
    pallas_call x6, Pallas kernels, call(): pl.pallas_call(kernel, out_shape=out_shape, compiler_params=pltpu.Compile...  18.9 us
    all_to_all x1, blocking collectives, per_device(): received = lax.all_to_all(sent, 'band', 0, 0, tiled=True)  10.4 us
    all_to_all x1, blocking collectives, per_device(): received = lax.all_to_all(sent, ('band', 'fft'), 0, 0, tiled=True)  8.95 us
    all_to_all x1, blocking collectives, per_device(): received = lax.all_to_all(sent, 'fft', 0, 0, tiled=True)  7.71 us
    all_to_all x1, starting transfers between devices, per_device(): received = lax.all_to_all(sent, 'fft', 0, 0, tiled=True)  5.18 us
    all_to_all x1, waiting for transfers between devices, per_device(): received = lax.all_to_all(sent, 'fft', 0, 0, tiled=True)  2.39 us
  transfers between devices with their start and end apart: 1, of which 1 were waited for; matrix products, arithmetic and copies ran while one was open for 0% of the time, Pallas kernels for 5%

profile of v8, /device:TPU:0, one launch (start us, length us, event | category | flops | bytes accessed | tf_op | source)
XLA Modules:
  0.0 54.3 jit_solution(10677004775395840771)
XLA Ops:
  0.6 2.2 %shard_map.140 = bf16[8,48,128]{2,1,0:T(8,128)(2,1)} custom-call(s32[4,128]{1,0:T(4,128)} %bitcast.4, f32[2,64,192]{2,1,0:T(8,128)} %coeffs_ref.1, s32[1,64]{1,0:T(1,128)} %bitcast.7, bf16[768,192]{1,0:T(8,128)(2,1)} %constant.16.clone.table_hbm), custom_call_target="tpu_custom_call" | custom-call | tf_op jit(solution)/shard_map/pallas_call | solution.py:475
  2.8 5.2 %all-to-all-start = ((bf16[8,48,128]{2,1,0:T(8,128)(2,1)}), bf16[8,48,128]{2,1,0:T(8,128)(2,1)S(1)}, u32[]{:S(2)}, u32[]{:S(2)}) async-start(bf16[8,48,128]{2,1,0:T(8,128)(2,1)} %shard_map.140), calls=%async_computation | async-start | bytes 196608 | tf_op jit(solution)/shard_map/all_to_all | solution.py:516
  8.0 2.7 %shard_map.141.table_hbm = bf16[3008,256]{1,0:T(8,128)(2,1)} custom-call(s32[4,128]{1,0:T(4,128)} %bitcast.5, bf16[1024,256]{1,0:T(8,128)(2,1)} %constant.17.clone.const_hbm), custom_call_target="tpu_custom_call" | custom-call | tf_op jit(solution)/shard_map/pallas_call | solution.py:475
  10.7 0.0 copy-start.1
  10.7 0.0 copy-start.7
  10.8 0.0 copy-start.9
  10.8 0.0 copy-start
  10.8 0.0 copy-start.5
  10.8 2.4 %all-to-all-done.recv_hbm = bf16[8,48,128]{2,1,0:T(8,128)(2,1)S(1)} async-done(((bf16[8,48,128]{2,1,0:T(8,128)(2,1)}), bf16[8,48,128]{2,1,0:T(8,128)(2,1)S(1)}, u32[]{:S(2)}, u32[]{:S(2)}) %all-to-all-start) | async-done | bytes 98336 | tf_op jit(solution)/shard_map/all_to_all | solution.py:516
  13.2 0.0 copy-start.2
  13.2 0.0 copy-start.3
  13.2 0.0 copy-start.6
  13.2 11.0 %shard_map.142 = bf16[8,48,128]{2,1,0:T(8,128)(2,1)S(1)} custom-call(bf16[8,48,128]{2,1,0:T(8,128)(2,1)S(1)} %all-to-all-done.recv_hbm, bf16[3008,256]{1,0:T(8,128)(2,1)} %shard_map.141.table_hbm, f32[24,192,192]{2,1,0:T(8,128)} %pot_hbm.1), custom_call_target="tpu_custom_call" | custom-call | tf_op jit(solution)/shard_map/pallas_call | solution.py:475
  24.2 0.0 copy-start.4
  24.2 0.0 copy-start.8
  24.2 7.7 %all_to_all.20.recv_ref = bf16[8,48,128]{2,1,0:T(8,128)(2,1)S(1)} all-to-all(bf16[8,48,128]{2,1,0:T(8,128)(2,1)S(1)} %shard_map.142), channel_id=1, replica_groups=mesh['band'=4,'fft'=8] {'fft'}, dimensions={0} | all-to-all | bytes 196608 | tf_op jit(solution)/shard_map/all_to_all | solution.py:560
  32.0 0.0 copy-done.1
  32.0 0.0 copy-done.7
  32.0 0.0 copy-done.9
  32.0 0.0 copy-done.2
  32.0 0.0 copy-done.3
  32.0 1.1 %shard_map.143 = (bf16[2,64,192]{2,1,0:T(8,128)(2,1)}, bf16[4,3,16,128]{3,2,1,0:T(8,128)(2,1)S(1)}) custom-call(bf16[8,48,128]{2,1,0:T(8,128)(2,1)S(1)} %all_to_all.20.recv_ref, f32[2,64,192]{2,1,0:T(8,128)S(1)} %copy-done.1, s32[1,64]{1,0:T(1,128)S(1)} %bitcast.8, s32[4,128]{1,0:T(4,128)S(1)} %bitcast.6, bf16[192,512]{1,0:T(8,128)(2,1)S(1)} %copy-done.3, ...), custom_call_target="tpu_custom_call" | custom-call | tf_op jit(solution)/shard_map/pallas_call | solution.py:475
  33.1 10.4 %all_to_all.21.recv_ref = bf16[4,3,16,128]{3,2,1,0:T(8,128)(2,1)S(1)} all-to-all(bf16[4,3,16,128]{3,2,1,0:T(8,128)(2,1)S(1)} %get-tuple-element.5), channel_id=1, replica_groups=mesh['band'=4,'fft'=8] {'band'}, dimensions={0} | all-to-all | bytes 98304 | tf_op jit(solution)/shard_map/all_to_all | solution.py:571
  43.4 0.0 copy-done
  43.4 0.0 copy-done.5
  43.4 0.0 copy-done.6
  43.4 1.1 %shard_map.144 = f32[32,2,128]{2,1,0:T(2,128)S(1)} custom-call(bf16[4,3,16,128]{3,2,1,0:T(8,128)(2,1)S(1)} %all_to_all.21.recv_ref, bf16[16,192,512]{2,1,0:T(8,128)(2,1)S(1)} %bitcast.3, bf16[256,256]{1,0:T(8,128)(2,1)S(1)} %copy-done.5, bf16[192,192]{1,0:T(8,128)(2,1)S(1)} %copy-done.6), custom_call_target="tpu_custom_call" | custom-call | tf_op jit(solution)/shard_map/pallas_call | solution.py:475
  44.5 8.9 %all_to_all.22.recv_ref = f32[32,2,128]{2,1,0:T(2,128)S(1)} all-to-all(f32[32,2,128]{2,1,0:T(2,128)S(1)} %shard_map.144), channel_id=1, replica_groups=mesh['band'=4,'fft'=8] {'band','fft'}, dimensions={0} | all-to-all | bytes 65536 | tf_op jit(solution)/shard_map/all_to_all | solution.py:594
  53.5 0.0 copy-done.4
  53.5 0.0 copy-done.8
  53.5 0.8 %shard_map.145 = f32[16,16]{1,0:T(8,128)} custom-call(f32[32,2,128]{2,1,0:T(2,128)S(1)} %all_to_all.22.recv_ref, f32[16,256]{1,0:T(8,128)S(1)} %copy-done.8, f32[256,16]{1,0:T(8,128)S(1)} %copy-done.4), custom_call_target="tpu_custom_call" | custom-call | tf_op jit(solution)/shard_map/pallas_call | solution.py:475
Async XLA Ops:
  2.8 10.4 %all-to-all-start = ((bf16[8,48,128]{2,1,0:T(8,128)(2,1)}), bf16[8,48,128]{2,1,0:T(8,128)(2,1)S(1)}, u32[]{:S(2)}, u32[]{:S(2)}) async-start(bf16[8,48,128]{2,1,0:T(8,128)(2,1)} %shard_map.140), calls=%async_computation | async-start | bytes 196608 | tf_op jit(solution)/shard_map/all_to_all | solution.py:516
  10.7 21.2 %copy-start.1 = (f32[2,64,192]{2,1,0:T(8,128)S(1)}, f32[2,64,192]{2,1,0:T(8,128)}, u32[]{:S(2)}) copy-start(f32[2,64,192]{2,1,0:T(8,128)} %coeffs_ref.1) | copy-start | bytes 294916
  10.7 21.2 %copy-start.7 = (s32[512]{0:T(512)S(1)}, s32[512]{0:T(512)}, u32[]{:S(2)}) copy-start(s32[512]{0:T(512)} %param.15) | copy-start | bytes 6148
  10.8 21.2 %copy-start.9 = (s32[64]{0:T(128)S(1)}, s32[64]{0:T(128)}, u32[]{:S(2)}) copy-start(s32[64]{0:T(128)} %param.16) | copy-start | bytes 772
  10.8 32.7 %copy-start = (bf16[512,16,192]{0,2,1:T(8,128)(2,1)S(1)}, bf16[512,16,192]{0,2,1:T(8,128)(2,1)}, u32[]{:S(2)}) copy-start(bf16[512,16,192]{0,2,1:T(8,128)(2,1)} %param.17) | copy-start | bytes 9437188
  10.8 32.6 %copy-start.5 = (bf16[256,256]{1,0:T(8,128)(2,1)S(1)}, bf16[256,256]{1,0:T(8,128)(2,1)}, u32[]{:S(2)}) copy-start(bf16[256,256]{1,0:T(8,128)(2,1)} %constant.20.clone.order_ref) | copy-start | bytes 393220
  13.2 18.8 %copy-start.2 = (bf16[192,512]{1,0:T(8,128)(2,1)S(1)}, bf16[192,512]{1,0:T(8,128)(2,1)}, u32[]{:S(2)}) copy-start(bf16[192,512]{1,0:T(8,128)(2,1)} %constant.19.clone.low_ref) | copy-start | bytes 589828
  13.2 18.8 %copy-start.3 = (bf16[192,512]{1,0:T(8,128)(2,1)S(1)}, bf16[192,512]{1,0:T(8,128)(2,1)}, u32[]{:S(2)}) copy-start(bf16[192,512]{1,0:T(8,128)(2,1)} %constant.18.clone.high_ref) | copy-start | bytes 589828
  13.2 30.2 %copy-start.6 = (bf16[192,192]{1,0:T(8,128)(2,1)S(1)}, bf16[192,192]{1,0:T(8,128)(2,1)}, u32[]{:S(2)}) copy-start(bf16[192,192]{1,0:T(8,128)(2,1)} %constant.21.clone.swap_ref) | copy-start | bytes 221188
  24.2 29.3 %copy-start.4 = (f32[256,16]{1,0:T(8,128)S(1)}, f32[256,16]{1,0:T(8,128)}, u32[]{:S(2)}) copy-start(f32[256,16]{1,0:T(8,128)} %constant.23.clone.fold_ref) | copy-start | bytes 49156
  24.2 29.3 %copy-start.8 = (f32[16,256]{1,0:T(8,128)S(1)}, f32[16,256]{1,0:T(8,128)}, u32[]{:S(2)}) copy-start(f32[16,256]{1,0:T(8,128)} %constant.22.clone.keep_ref) | copy-start | bytes 49156

commit v9 on v8

--- a/solution.py
+++ b/solution.py
@@ -154,7 +154,9 @@
     nt = ((1,), (1,))
     copies[3].wait()
     high, low = table_ref[: 2 * grid], table_ref[2 * grid :]
-    sums = dot(high, c_high, nt) + dot(high, c_low, nt) + dot(low, c_high, nt)
+    rows = bands * sticks
+    sums = dot(high, jnp.concatenate([c_high, c_low], 0), nt)
+    sums = sums[:, :rows] + sums[:, rows:] + dot(low, c_high, nt)
     real, imag = sums[:grid], sums[grid:]
     real, imag = real * cosine + imag * sine, imag * cosine - real * sine
     first = lane_iota(real.shape) < sticks

time: 54.7 us -> 54.7 us (level)
  no operation moved by 1% of the time
where the time goes in v9:
time: 54.7 us; the launch traced here: 54.3 us
  blocking collectives  27 us (49%)
  Pallas kernels  18.9 us (35%)
  starting transfers between devices  5.18 us (9%)
  waiting for transfers between devices  2.39 us (4%)
  between operations  0.74 us (1%)
    pallas_call x6, Pallas kernels, call(): pl.pallas_call(kernel, out_shape=out_shape, compiler_params=pltpu.Compile...  18.9 us
    all_to_all x1, blocking collectives, per_device(): received = lax.all_to_all(sent, 'band', 0, 0, tiled=True)  10.4 us
    all_to_all x1, blocking collectives, per_device(): received = lax.all_to_all(sent, ('band', 'fft'), 0, 0, tiled=True)  8.95 us
    all_to_all x1, blocking collectives, per_device(): received = lax.all_to_all(sent, 'fft', 0, 0, tiled=True)  7.71 us
    all_to_all x1, starting transfers between devices, per_device(): received = lax.all_to_all(sent, 'fft', 0, 0, tiled=True)  5.18 us
    all_to_all x1, waiting for transfers between devices, per_device(): received = lax.all_to_all(sent, 'fft', 0, 0, tiled=True)  2.39 us
  transfers between devices with their start and end apart: 1, of which 1 were waited for; matrix products, arithmetic and copies ran while one was open for 0% of the time, Pallas kernels for 5%

profile of v9, /device:TPU:0, one launch (start us, length us, event | category | flops | bytes accessed | tf_op | source)
XLA Modules:
  0.0 54.3 jit_solution(11300807900854686442)
XLA Ops:
  0.6 2.1 %shard_map.140 = bf16[8,48,128]{2,1,0:T(8,128)(2,1)} custom-call(s32[4,128]{1,0:T(4,128)} %bitcast.4, f32[2,64,192]{2,1,0:T(8,128)} %coeffs_ref.1, s32[1,64]{1,0:T(1,128)} %bitcast.7, bf16[768,192]{1,0:T(8,128)(2,1)} %constant.16.clone.table_hbm), custom_call_target="tpu_custom_call" | custom-call | tf_op jit(solution)/shard_map/pallas_call | solution.py:477
  2.8 5.2 %all-to-all-start = ((bf16[8,48,128]{2,1,0:T(8,128)(2,1)}), bf16[8,48,128]{2,1,0:T(8,128)(2,1)S(1)}, u32[]{:S(2)}, u32[]{:S(2)}) async-start(bf16[8,48,128]{2,1,0:T(8,128)(2,1)} %shard_map.140), calls=%async_computation | async-start | bytes 196608 | tf_op jit(solution)/shard_map/all_to_all | solution.py:518
  8.0 2.7 %shard_map.141.table_hbm = bf16[3008,256]{1,0:T(8,128)(2,1)} custom-call(s32[4,128]{1,0:T(4,128)} %bitcast.5, bf16[1024,256]{1,0:T(8,128)(2,1)} %constant.17.clone.const_hbm), custom_call_target="tpu_custom_call" | custom-call | tf_op jit(solution)/shard_map/pallas_call | solution.py:477
  10.7 0.0 copy-start.1
  10.7 0.0 copy-start.7
  10.7 0.0 copy-start.9
  10.7 0.0 copy-start
  10.8 0.0 copy-start.5
  10.8 2.4 %all-to-all-done.recv_hbm = bf16[8,48,128]{2,1,0:T(8,128)(2,1)S(1)} async-done(((bf16[8,48,128]{2,1,0:T(8,128)(2,1)}), bf16[8,48,128]{2,1,0:T(8,128)(2,1)S(1)}, u32[]{:S(2)}, u32[]{:S(2)}) %all-to-all-start) | async-done | bytes 98336 | tf_op jit(solution)/shard_map/all_to_all | solution.py:518
  13.2 0.0 copy-start.2
  13.2 0.0 copy-start.3
  13.2 0.0 copy-start.6
  13.2 11.0 %shard_map.142 = bf16[8,48,128]{2,1,0:T(8,128)(2,1)S(1)} custom-call(bf16[8,48,128]{2,1,0:T(8,128)(2,1)S(1)} %all-to-all-done.recv_hbm, bf16[3008,256]{1,0:T(8,128)(2,1)} %shard_map.141.table_hbm, f32[24,192,192]{2,1,0:T(8,128)} %pot_hbm.1), custom_call_target="tpu_custom_call" | custom-call | tf_op jit(solution)/shard_map/pallas_call | solution.py:477
  24.2 0.0 copy-start.4
  24.2 0.0 copy-start.8
  24.2 7.7 %all_to_all.20.recv_ref = bf16[8,48,128]{2,1,0:T(8,128)(2,1)S(1)} all-to-all(bf16[8,48,128]{2,1,0:T(8,128)(2,1)S(1)} %shard_map.142), channel_id=1, replica_groups=mesh['band'=4,'fft'=8] {'fft'}, dimensions={0} | all-to-all | bytes 196608 | tf_op jit(solution)/shard_map/all_to_all | solution.py:562
  31.9 0.0 copy-done.1
  31.9 0.0 copy-done.7
  31.9 0.0 copy-done.9
  31.9 0.0 copy-done.2
  31.9 0.0 copy-done.3
  32.0 1.1 %shard_map.143 = (bf16[2,64,192]{2,1,0:T(8,128)(2,1)}, bf16[4,3,16,128]{3,2,1,0:T(8,128)(2,1)S(1)}) custom-call(bf16[8,48,128]{2,1,0:T(8,128)(2,1)S(1)} %all_to_all.20.recv_ref, f32[2,64,192]{2,1,0:T(8,128)S(1)} %copy-done.1, s32[1,64]{1,0:T(1,128)S(1)} %bitcast.8, s32[4,128]{1,0:T(4,128)S(1)} %bitcast.6, bf16[192,512]{1,0:T(8,128)(2,1)S(1)} %copy-done.3, ...), custom_call_target="tpu_custom_call" | custom-call | tf_op jit(solution)/shard_map/pallas_call | solution.py:477
  33.0 10.4 %all_to_all.21.recv_ref = bf16[4,3,16,128]{3,2,1,0:T(8,128)(2,1)S(1)} all-to-all(bf16[4,3,16,128]{3,2,1,0:T(8,128)(2,1)S(1)} %get-tuple-element.5), channel_id=1, replica_groups=mesh['band'=4,'fft'=8] {'band'}, dimensions={0} | all-to-all | bytes 98304 | tf_op jit(solution)/shard_map/all_to_all | solution.py:573
  43.4 0.0 copy-done
  43.4 0.0 copy-done.5
  43.4 0.0 copy-done.6
  43.4 1.1 %shard_map.144 = f32[32,2,128]{2,1,0:T(2,128)S(1)} custom-call(bf16[4,3,16,128]{3,2,1,0:T(8,128)(2,1)S(1)} %all_to_all.21.recv_ref, bf16[16,192,512]{2,1,0:T(8,128)(2,1)S(1)} %bitcast.3, bf16[256,256]{1,0:T(8,128)(2,1)S(1)} %copy-done.5, bf16[192,192]{1,0:T(8,128)(2,1)S(1)} %copy-done.6), custom_call_target="tpu_custom_call" | custom-call | tf_op jit(solution)/shard_map/pallas_call | solution.py:477
  44.5 8.9 %all_to_all.22.recv_ref = f32[32,2,128]{2,1,0:T(2,128)S(1)} all-to-all(f32[32,2,128]{2,1,0:T(2,128)S(1)} %shard_map.144), channel_id=1, replica_groups=mesh['band'=4,'fft'=8] {'band','fft'}, dimensions={0} | all-to-all | bytes 65536 | tf_op jit(solution)/shard_map/all_to_all | solution.py:596
  53.5 0.0 copy-done.4
  53.5 0.0 copy-done.8
  53.5 0.8 %shard_map.145 = f32[16,16]{1,0:T(8,128)} custom-call(f32[32,2,128]{2,1,0:T(2,128)S(1)} %all_to_all.22.recv_ref, f32[16,256]{1,0:T(8,128)S(1)} %copy-done.8, f32[256,16]{1,0:T(8,128)S(1)} %copy-done.4), custom_call_target="tpu_custom_call" | custom-call | tf_op jit(solution)/shard_map/pallas_call | solution.py:477
Async XLA Ops:
  2.8 10.4 %all-to-all-start = ((bf16[8,48,128]{2,1,0:T(8,128)(2,1)}), bf16[8,48,128]{2,1,0:T(8,128)(2,1)S(1)}, u32[]{:S(2)}, u32[]{:S(2)}) async-start(bf16[8,48,128]{2,1,0:T(8,128)(2,1)} %shard_map.140), calls=%async_computation | async-start | bytes 196608 | tf_op jit(solution)/shard_map/all_to_all | solution.py:518
  10.7 21.2 %copy-start.1 = (f32[2,64,192]{2,1,0:T(8,128)S(1)}, f32[2,64,192]{2,1,0:T(8,128)}, u32[]{:S(2)}) copy-start(f32[2,64,192]{2,1,0:T(8,128)} %coeffs_ref.1) | copy-start | bytes 294916
  10.7 21.2 %copy-start.7 = (s32[512]{0:T(512)S(1)}, s32[512]{0:T(512)}, u32[]{:S(2)}) copy-start(s32[512]{0:T(512)} %param.15) | copy-start | bytes 6148
  10.7 21.2 %copy-start.9 = (s32[64]{0:T(128)S(1)}, s32[64]{0:T(128)}, u32[]{:S(2)}) copy-start(s32[64]{0:T(128)} %param.16) | copy-start | bytes 772
  10.7 32.7 %copy-start = (bf16[512,16,192]{0,2,1:T(8,128)(2,1)S(1)}, bf16[512,16,192]{0,2,1:T(8,128)(2,1)}, u32[]{:S(2)}) copy-start(bf16[512,16,192]{0,2,1:T(8,128)(2,1)} %param.17) | copy-start | bytes 9437188
  10.8 32.7 %copy-start.5 = (bf16[256,256]{1,0:T(8,128)(2,1)S(1)}, bf16[256,256]{1,0:T(8,128)(2,1)}, u32[]{:S(2)}) copy-start(bf16[256,256]{1,0:T(8,128)(2,1)} %constant.20.clone.order_ref) | copy-start | bytes 393220
  13.2 18.8 %copy-start.2 = (bf16[192,512]{1,0:T(8,128)(2,1)S(1)}, bf16[192,512]{1,0:T(8,128)(2,1)}, u32[]{:S(2)}) copy-start(bf16[192,512]{1,0:T(8,128)(2,1)} %constant.19.clone.low_ref) | copy-start | bytes 589828
  13.2 18.8 %copy-start.3 = (bf16[192,512]{1,0:T(8,128)(2,1)S(1)}, bf16[192,512]{1,0:T(8,128)(2,1)}, u32[]{:S(2)}) copy-start(bf16[192,512]{1,0:T(8,128)(2,1)} %constant.18.clone.high_ref) | copy-start | bytes 589828
  13.2 30.3 %copy-start.6 = (bf16[192,192]{1,0:T(8,128)(2,1)S(1)}, bf16[192,192]{1,0:T(8,128)(2,1)}, u32[]{:S(2)}) copy-start(bf16[192,192]{1,0:T(8,128)(2,1)} %constant.21.clone.swap_ref) | copy-start | bytes 221188
  24.2 29.3 %copy-start.4 = (f32[256,16]{1,0:T(8,128)S(1)}, f32[256,16]{1,0:T(8,128)}, u32[]{:S(2)}) copy-start(f32[256,16]{1,0:T(8,128)} %constant.23.clone.fold_ref) | copy-start | bytes 49156
  24.2 29.3 %copy-start.8 = (f32[16,256]{1,0:T(8,128)S(1)}, f32[16,256]{1,0:T(8,128)}, u32[]{:S(2)}) copy-start(f32[16,256]{1,0:T(8,128)} %constant.22.clone.keep_ref) | copy-start | bytes 49156
